TPU v7x, 256 devices: a whole 4x4x8 slice. The times are simulated.
256 devices in a mesh: dp: 32 (over x, z_hi, core), space: 8 (over y, z_lo).
Axes of the slice: x: 4, y: 4, z: 8 (z_hi: 4, z_lo: 2; z = z_hi * 2 + z_lo), core: 2. Of those that a mesh axis runs over, the one named last changes fastest.
Arguments:
- block_input: bfloat16 [32, 56, 56, 768], P('dp', 'space'), may hold values from -8 to 8
- hidden_map: bfloat16 [32, 56, 56, 1536], P('dp', 'space'), may hold values from -6 to 6
- cotangent: bfloat16 [32, 56, 56, 768], P('dp', 'space'), may hold values from -16 to 16
- depth_weight: bfloat16 [9, 1536], replicated, may hold values from -2 to 2
- proj_weight: bfloat16 [1536, 768], replicated, may hold values from -0.15625 to 0.15625
- norm_gain: float32 [768], replicated, may hold values from 0.5 to 1.5
- qkv_weight: bfloat16 [768, 2304], replicated, may hold values from -10 to 10
- out_weight: bfloat16 [768, 768], replicated, may hold values from -0.21875 to 0.21875
Outputs:
- block_output: bfloat16 [32, 56, 56, 768], P('dp', 'space')
- input_grad: bfloat16 [32, 56, 56, 768], P('dp', 'space')
- hidden_grad: bfloat16 [32, 56, 56, 1536], P('dp', 'space')
- depth_grad: float32 [9, 1536], replicated
- gain_grad: float32 [768], replicated
- proj_grad: float32 [1536, 768], P('dp', 'space')
- qkv_grad: float32 [768, 2304], P('dp', 'space')
- out_grad: float32 [768, 768], P('dp', 'space')
All inputs are finite; a program needn't handle non-finite values.
Results may differ from a plain program's by a relative error of at most 0.025.
Values may be sent and summed in bfloat16 or wider, within the bound.
A program may use at most 128 MiB of HBM per device.

v0:
```python
import jax
import jax.numpy as jnp
from jax import lax
from jax.sharding import PartitionSpec as P

HEADS = 24
HD = 32
G = 7


EPS = 1e-05


def extended(shard, sides, width):
    for axis, dim in sides:
        peers, length = (lax.axis_size(axis), shard.shape[dim])
        up = [(i, (i + 1) % peers) for i in range(peers - 1)]
        down = [(j, i) for i, j in up]
        last = lax.slice_in_dim(shard, length - width, length, axis=dim)
        initial = lax.slice_in_dim(shard, 0, width, axis=dim)
        before = lax.ppermute(last, axis, up)
        after = lax.ppermute(initial, axis, down)
        shard = jnp.concatenate([before, shard, after], axis=dim)
    return shard


def conv_forward(padded, depth_weight, map_rows, map_cols):
    summed = None
    for tap_index in range(9):
        tap_row, tap_col = (tap_index // 3, tap_index % 3)
        shifted_piece = padded[
            ..., tap_row : tap_row + map_rows, tap_col : tap_col + map_cols, :
        ].astype(jnp.float32)
        term = shifted_piece * depth_weight[tap_index].astype(jnp.float32)
        summed = term if summed is None else summed + term
    return summed


def conv_backward(padded, depth_weight, map_rows, map_cols):
    summed = None
    for tap_index in range(9):
        tap_row, tap_col = (2 - tap_index // 3, 2 - tap_index % 3)
        shifted_piece = padded[
            ..., tap_row : tap_row + map_rows, tap_col : tap_col + map_cols, :
        ].astype(jnp.float32)
        term = shifted_piece * depth_weight[tap_index].astype(jnp.float32)
        summed = term if summed is None else summed + term
    return summed


def depth_sum(padded, grad_conv, map_rows, map_cols):
    grad_wide = grad_conv.astype(jnp.float32)
    lead_axes = tuple(range(grad_conv.ndim - 1))
    tap_sums = []
    for tap_index in range(9):
        tap_row, tap_col = (tap_index // 3, tap_index % 3)
        shifted_piece = padded[
            ..., tap_row : tap_row + map_rows, tap_col : tap_col + map_cols, :
        ].astype(jnp.float32)
        tap_sums.append(jnp.sum(shifted_piece * grad_wide, axis=lead_axes))
    return jnp.stack(tap_sums)


def norm_forward(mid_stream, norm_gain):
    token_mean = jnp.mean(mid_stream, axis=-1, keepdims=True)
    centred = mid_stream - token_mean
    variance = jnp.mean(centred * centred, axis=-1, keepdims=True)
    inv_std = lax.rsqrt(variance + EPS)
    normal_hat = centred * inv_std
    normed = (normal_hat * norm_gain).astype(jnp.bfloat16)
    return (normal_hat, inv_std, normed)


def to_windows(grid_part, row_step):
    images, all_rows, columns, local_step, features = grid_part.shape
    pieces = grid_part.reshape(images, G, row_step, G, local_step, features)
    pieces = pieces.transpose(0, 2, 4, 1, 3, 5)
    return pieces.reshape(images * row_step * local_step, G * G, features)


def from_windows(windowed, images, row_step, local_step):
    features = windowed.shape[-1]
    pieces = windowed.reshape(images, row_step, local_step, G, G, features)
    pieces = pieces.transpose(0, 3, 1, 4, 2, 5)
    return pieces.reshape(images, G * row_step, G, local_step, features)


def attend_forward(queries, key_rows, values):
    score_scale = HD ** (-0.5)
    scores = (
        jnp.einsum("nqhd,nkhd->nhqk", queries, key_rows, preferred_element_type=jnp.float32)
        * score_scale
    )
    shifted = scores - jnp.max(scores, axis=-1, keepdims=True)
    exponent = jnp.exp(shifted)
    weights = exponent / jnp.sum(exponent, axis=-1, keepdims=True)
    weights_low = weights.astype(jnp.bfloat16)
    attended = jnp.einsum(
        "nhqk,nkhd->nqhd", weights_low, values, preferred_element_type=jnp.float32
    )
    return (attended.astype(jnp.bfloat16), weights, weights_low)


def attend_backward(queries, key_rows, values, weights, weights_low, grad_att):
    score_scale = HD ** (-0.5)
    grad_weights = jnp.einsum(
        "nqhd,nkhd->nhqk", grad_att, values, preferred_element_type=jnp.float32
    )
    grad_values = jnp.einsum(
        "nhqk,nqhd->nkhd", weights_low, grad_att, preferred_element_type=jnp.float32
    )
    centred = grad_weights - jnp.sum(grad_weights * weights, axis=-1, keepdims=True)
    grad_low = (weights * centred * score_scale).astype(jnp.bfloat16)
    grad_queries = jnp.einsum(
        "nhqk,nkhd->nqhd", grad_low, key_rows, preferred_element_type=jnp.float32
    )
    grad_keys = jnp.einsum("nhqk,nqhd->nkhd", grad_low, queries, preferred_element_type=jnp.float32)
    return (
        grad_queries.astype(jnp.bfloat16),
        grad_keys.astype(jnp.bfloat16),
        grad_values.astype(jnp.bfloat16),
    )


def local(
    block_input, hidden_map, cotangent, depth_weight, proj_weight, norm_gain, qkv_weight, out_weight
):
    images, slab_rows, map_cols, hidden_units = hidden_map.shape
    channels = block_input.shape[-1]
    space_count = lax.axis_size("space")
    col_step = map_cols // G
    local_step = col_step // space_count
    row_step = slab_rows * space_count // G
    token_count = images * slab_rows * map_cols
    slab_shape = (images, slab_rows, G, col_step)
    hidden_rows = extended(hidden_map, (("space", 1),), 1)
    hidden_pad = jnp.pad(hidden_rows, ((0, 0), (0, 0), (1, 1), (0, 0)))
    conv_out = conv_forward(hidden_pad, depth_weight, slab_rows, map_cols)
    act_low = jax.nn.gelu(conv_out).astype(jnp.bfloat16).reshape(token_count, hidden_units)
    mid_stream = block_input.reshape(token_count, channels).astype(jnp.float32) + jnp.dot(
        act_low, proj_weight, preferred_element_type=jnp.float32
    )
    normal_hat, inv_std, normed = norm_forward(mid_stream, norm_gain)
    qkv_low = jnp.dot(normed, qkv_weight, preferred_element_type=jnp.float32).astype(jnp.bfloat16)
    qkv_grid = lax.all_to_all(
        qkv_low.reshape(slab_shape + (3 * channels,)),
        "space",
        split_axis=3,
        concat_axis=1,
        tiled=True,
    )
    qkv_win = to_windows(qkv_grid, row_step)
    window_count = qkv_win.shape[0]
    qkv_win = qkv_win.reshape(window_count, G * G, 3, HEADS, HD)
    queries, key_rows, values = (qkv_win[:, :, 0], qkv_win[:, :, 1], qkv_win[:, :, 2])
    attended, weights, weights_low = attend_forward(queries, key_rows, values)
    att_grid = from_windows(
        attended.reshape(window_count, G * G, channels), images, row_step, local_step
    )
    att_slab = lax.all_to_all(att_grid, "space", split_axis=1, concat_axis=3, tiled=True)
    att_tok = att_slab.reshape(token_count, channels)
    output_full = mid_stream + jnp.dot(att_tok, out_weight, preferred_element_type=jnp.float32)
    block_output = output_full.astype(jnp.bfloat16).reshape(images, slab_rows, map_cols, channels)
    cot_tok = cotangent.reshape(token_count, channels)
    out_local = jnp.einsum("tc,td->cd", att_tok, cot_tok, preferred_element_type=jnp.float32)
    grad_att = jnp.dot(cot_tok, out_weight.T, preferred_element_type=jnp.float32).astype(
        jnp.bfloat16
    )
    grad_att_grid = lax.all_to_all(
        grad_att.reshape(slab_shape + (channels,)), "space", split_axis=3, concat_axis=1, tiled=True
    )
    grad_win = to_windows(grad_att_grid, row_step).reshape(window_count, G * G, HEADS, HD)
    grad_queries, grad_keys, grad_values = attend_backward(
        queries, key_rows, values, weights, weights_low, grad_win
    )
    grad_stack = jnp.stack([grad_queries, grad_keys, grad_values], axis=2).reshape(
        window_count, G * G, 3 * channels
    )
    grad_qkv_grid = from_windows(grad_stack, images, row_step, local_step)
    grad_qkv = lax.all_to_all(
        grad_qkv_grid, "space", split_axis=1, concat_axis=3, tiled=True
    ).reshape(token_count, 3 * channels)
    qkv_local = jnp.einsum("tc,td->cd", normed, grad_qkv, preferred_element_type=jnp.float32)
    grad_normed = jnp.dot(grad_qkv, qkv_weight.T, preferred_element_type=jnp.float32).astype(
        jnp.bfloat16
    )
    grad_wide = grad_normed.astype(jnp.float32)
    grad_hat = grad_wide * norm_gain
    gain_local = jnp.sum(grad_wide * normal_hat, axis=0)
    grad_mid = cot_tok.astype(jnp.float32) + inv_std * (
        grad_hat
        - jnp.mean(grad_hat, axis=-1, keepdims=True)
        - normal_hat * jnp.mean(grad_hat * normal_hat, axis=-1, keepdims=True)
    )
    input_grad = grad_mid.astype(jnp.bfloat16)
    proj_local = jnp.einsum("te,tc->ec", act_low, input_grad, preferred_element_type=jnp.float32)
    grad_act = jnp.dot(input_grad, proj_weight.T, preferred_element_type=jnp.float32).reshape(
        images, slab_rows, map_cols, hidden_units
    )
    grad_conv = jax.vjp(jax.nn.gelu, conv_out)[1](grad_act)[0].astype(jnp.bfloat16)
    grad_rows = extended(grad_conv, (("space", 1),), 1)
    grad_pad = jnp.pad(grad_rows, ((0, 0), (0, 0), (1, 1), (0, 0)))
    hidden_grad = conv_backward(grad_pad, depth_weight, slab_rows, map_cols).astype(jnp.bfloat16)
    depth_local = depth_sum(hidden_pad, grad_conv, slab_rows, map_cols)
    depth_grad, gain_grad = lax.psum((depth_local, gain_local), ("dp", "space"))
    qkv_part, proj_part, out_part = (
        lax.psum_scatter(
            qkv_local.astype(jnp.bfloat16), "dp", scatter_dimension=0, tiled=True
        ).astype(jnp.float32),
        lax.psum_scatter(
            proj_local.astype(jnp.bfloat16), "dp", scatter_dimension=0, tiled=True
        ).astype(jnp.float32),
        lax.psum_scatter(
            out_local.astype(jnp.bfloat16), "dp", scatter_dimension=0, tiled=True
        ).astype(jnp.float32),
    )
    qkv_grad, proj_grad, out_grad = (
        lax.psum_scatter(
            qkv_part.astype(jnp.bfloat16), "space", scatter_dimension=1, tiled=True
        ).astype(jnp.float32),
        lax.psum_scatter(
            proj_part.astype(jnp.bfloat16), "space", scatter_dimension=1, tiled=True
        ).astype(jnp.float32),
        lax.psum_scatter(
            out_part.astype(jnp.bfloat16), "space", scatter_dimension=1, tiled=True
        ).astype(jnp.float32),
    )
    return (
        block_output,
        input_grad.reshape(images, slab_rows, map_cols, channels),
        hidden_grad,
        depth_grad,
        gain_grad,
        proj_grad,
        qkv_grad,
        out_grad,
    )


def solution(mesh):
    return jax.shard_map(
        local,
        mesh=mesh,
        in_specs=(
            P("dp", "space", None, None),
            P("dp", "space", None, None),
            P("dp", "space", None, None),
            P(),
            P(),
            P(),
            P(),
            P(),
        ),
        out_specs=(
            P("dp", "space", None, None),
            P("dp", "space", None, None),
            P("dp", "space", None, None),
            P(),
            P(),
            P("dp", "space"),
            P("dp", "space"),
            P("dp", "space"),
        ),
        check_vma=False,
    )
```

profile of v0, /device:TPU:2, one launch (start us, length us, event | category | flops | bytes accessed | tf_op | source)
XLA Modules:
  0.0 627.0 jit_solution(10147242951900035994)
XLA Ops:
  18.0 6.4 %all-to-all-start.2 = ((bf16[1,7,7,8,768]{4,1,2,0,3:T(8,128)(2,1)}), bf16[1,7,7,8,768]{4,1,2,0,3:T(8,128)(2,1)}, u32[]{:S(2)}, u32[]{:S(2)}) async-start(bf16[1,7,7,8,768]{4,1,2,0,3:T(8,128)(2,1)} %copy.51), calls=%async_computation.2 | async-start | bytes 1376256 | tf_op jit(solution)/shard_map/all_to_all | solution.py:169
  27.6 5.2 multiply_convert_fusion.1
  37.8 5.9 all-to-all-start
  58.8 10.5 %all-to-all-done = bf16[1,7,7,8,2304]{4,1,2,0,3:T(8,128)(2,1)} async-done(((bf16[1,7,7,8,2304]{4,1,2,0,3:T(8,128)(2,1)}), bf16[1,7,7,8,2304]{4,1,2,0,3:T(8,128)(2,1)}, u32[]{:S(2)}, u32[]{:S(2)}) %all-to-all-start) | async-done | bytes 1806368 | tf_op jit(solution)/shard_map/all_to_all | solution.py:145
  79.0 9.1 %reshape_reshape.12 = bf16[8,49,3,24,32]{4,3,2,0,1:T(8,128)(2,1)} reshape(bf16[1,8,1,7,7,2304]{5,1,4,3,2,0:T(8,128)(2,1)} %copy.41) | data formatting | bytes 3612672 | tf_op jit(solution)/shard_map/reshape;reshape | solution.py:154
  88.1 6.6 %fusion.96 = (bf16[8,49,1,24,32]{4,3,2,0,1:T(8,128)(2,1)}, bf16[8,49,1,24,32]{4,3,2,0,1:T(8,128)(2,1)}, bf16[8,49,1,24,32]{4,3,2,0,1:T(8,128)(2,1)}) fusion(bf16[8,49,3,24,32]{4,3,2,0,1:T(8,128)(2,1)} %reshape_reshape.12), kind=kLoop, calls=%fused_computation.142 | loop fusion | bytes 3612672 | tf_op jit(solution)/shard_map/slice | solution.py:155
  118.2 5.9 fusion.60
  124.1 11.2 %fusion.71 = bf16[8,49,1,24,32]{1,4,3,0,2:T(8,128)(2,1)} fusion(f32[8,24,49,49]{2,3,1,0:T(8,128)} %fusion.60, bf16[8,49,1,24,32]{1,4,3,0,2:T(8,128)(2,1)} %copy.78, f32[8,24,49,49]{2,3,1,0:T(8,128)} %get-tuple-element.47, f32[8,24,49]{2,1,0:T(8,128)} %get-tuple-element.46), kind=kOutput, calls=%fused_computation.99 | convolution fusion | flops 33040944 | bytes 4929792 | tf_op jit(solution)/shard_map/nhqk,nkhd->nqhd/dot_general | solution.py:114
  135.2 10.9 %fusion.66 = bf16[8,49,1,24,32]{1,4,3,0,2:T(8,128)(2,1)} fusion(f32[8,24,49,49]{2,3,1,0:T(8,128)} %fusion.60, bf16[8,49,1,24,32]{1,4,3,0,2:T(8,128)(2,1)} %copy.77, f32[8,24,49,49]{2,3,1,0:T(8,128)} %get-tuple-element.47, f32[8,24,49]{2,1,0:T(8,128)} %get-tuple-element.46), kind=kOutput, calls=%fused_computation.98 | convolution fusion | flops 33040944 | bytes 4929792 | tf_op jit(solution)/shard_map/nhqk,nqhd->nkhd/dot_general | solution.py:117
  146.2 5.8 fusion.79
  156.8 5.9 copy.46
  173.5 5.7 pad_maximum_fusion
  179.2 9.3 %copy.59 = bf16[8,49,3,24,32]{4,3,2,0,1:T(8,128)(2,1)} copy(bf16[8,49,3,24,32]{1,4,3,0,2:T(8,128)(2,1)} %pad_maximum_fusion) | data formatting | bytes 3612672 | tf_op jit(solution)/shard_map/stack | solution.py:176
  188.4 9.2 %reshape_reshape.15 = bf16[1,8,1,7,7,2304]{5,1,4,3,2,0:T(8,128)(2,1)} reshape(bf16[8,49,3,24,32]{4,3,2,0,1:T(8,128)(2,1)} %copy.59) | data formatting | bytes 3612672 | tf_op jit(solution)/shard_map/reshape;reshape | solution.py:83
  201.0 5.7 all-to-all-start.3
  210.8 90.1 %reduce-scatter.17.cloned.1.call-done = bf16[24,768]{1,0:T(8,128)(2,1)} async-done(((bf16[768,768]{1,0:T(8,128)(2,1)}), bf16[24,768]{1,0:T(8,128)(2,1)}) %reduce-scatter.17.cloned.1.call-update) | async-done | bytes 36880 | tf_op jit(solution)/shard_map/reduce_scatter | solution.py:213
  312.6 5.9 convolution_convert_fusion
  322.1 6.1 fusion.47
  336.0 5.9 reduce-scatter.23.cloned.1.call-done
  359.0 75.4 %all-reduce.2 = (f32[9,1536]{1,0:T(8,128)}, f32[768]{0:T(1024)}) all-reduce(f32[9,1536]{1,0:T(8,128)} %stack.55, f32[768]{0:T(1024)} %get-tuple-element.17), channel_id=1, replica_groups=mesh['dp'=32,'space'=8] {'dp','space'}, use_global_device_ids=true, to_apply=%region_16.17 | all-reduce | flops 14592 | bytes 116736 | tf_op jit(solution)/shard_map/psum | solution.py:205
  441.3 93.0 %reduce-scatter.15.cloned.1.call-done = bf16[24,2304]{1,0:T(8,128)(2,1)} async-done(((bf16[768,2304]{1,0:T(8,128)(2,1)}), bf16[24,2304]{1,0:T(8,128)(2,1)}) %reduce-scatter.15.cloned.1.call-update) | async-done | bytes 110608 | tf_op jit(solution)/shard_map/reduce_scatter | solution.py:207
  536.2 7.0 %fusion.38 = bf16[1,7,56,1536]{3,2,1,0:T(8,128)(2,1)} fusion(bf16[1,7,56,1536]{3,2,1,0:T(8,128)(2,1)} %copy-done.5, bf16[1,9,58,1536]{3,2,1,0:T(8,128)(2,1)} %select_maximum_fusion, bf16[1,1,56,1536]{3,2,1,0:T(8,128)(2,1)} %collective-permute-done.2, bf16[1,1,56,1536]{3,2,1,0:T(8,128)(2,1)} %collective-permute-done.3, f32[1536]{0:T(1024)} %copy-done.26, ...), kind=kLoop, calls=%fused_computation.62 | loop fusion | flops 17461248 | bytes 10033152 | tf_op jit(solution)/shard_map/convert_element_type | solution.py:203
  543.2 31.9 %reduce-scatter.19.cloned.1.call-done = bf16[96,48]{1,0:T(8,128)(2,1)} async-done(((bf16[768,48]{1,0:T(8,128)(2,1)}), bf16[96,48]{1,0:T(8,128)(2,1)}) %reduce-scatter.19.cloned.1.call-update) | async-done | bytes 9232
  576.5 40.5 %reduce-scatter.21.cloned.1.call-done = bf16[288,24]{1,0:T(8,128)(2,1)} async-done(((bf16[2304,24]{1,0:T(8,128)(2,1)}), bf16[288,24]{1,0:T(8,128)(2,1)}) %reduce-scatter.21.cloned.1.call-update) | async-done | bytes 13840
  (159 shorter events, 143.0 us)
Async XLA Ops:
  7.2 27.3 %copy-start = (bf16[768,2304]{1,0:T(8,128)(2,1)S(1)}, bf16[768,2304]{1,0:T(8,128)(2,1)}, u32[]{:S(2)}) copy-start(bf16[768,2304]{1,0:T(8,128)(2,1)} %param.14) | copy-start | bytes 10616836
  9.1 16.5 %collective-permute-start = (bf16[1,1,56,1536]{3,2,1,0:T(8,128)(2,1)}, bf16[1,1,56,1536]{3,2,1,0:T(8,128)(2,1)}, u32[]{:S(2)}, u32[]{:S(2)}) collective-permute-start(bf16[1,1,56,1536]{3,2,1,0:T(8,128)(2,1)} %get-tuple-element.42), channel_id=1, source_target_pairs={{0,1},{1,2},{2,3},{3,4},{4,5},{5,6},{6,7},{8,9},{9,10},{10,11},{11... | collective-permute-start | bytes 516104 | tf_op jit(solution)/shard_map/ppermute | solution.py:21
  13.6 12.1 %collective-permute-start.1 = (bf16[1,1,56,1536]{3,2,1,0:T(8,128)(2,1)}, bf16[1,1,56,1536]{3,2,1,0:T(8,128)(2,1)}, u32[]{:S(2)}, u32[]{:S(2)}) collective-permute-start(bf16[1,1,56,1536]{3,2,1,0:T(8,128)(2,1)} %get-tuple-element.43), channel_id=1, source_target_pairs={{1,0},{2,1},{3,2},{4,3},{5,4},{6,5},{7,6},{9,8},{10,9},{11,10},{12... | collective-permute-start | bytes 516104 | tf_op jit(solution)/shard_map/ppermute | solution.py:22
  18.0 19.8 %all-to-all-start.2 = ((bf16[1,7,7,8,768]{4,1,2,0,3:T(8,128)(2,1)}), bf16[1,7,7,8,768]{4,1,2,0,3:T(8,128)(2,1)}, u32[]{:S(2)}, u32[]{:S(2)}) async-start(bf16[1,7,7,8,768]{4,1,2,0,3:T(8,128)(2,1)} %copy.51), calls=%async_computation.2 | async-start | bytes 1376256 | tf_op jit(solution)/shard_map/all_to_all | solution.py:169
  25.5 7.2 %copy-start.21 = (f32[1536]{0:T(1024)}, f32[1536]{0:T(1024)S(1)}, u32[]{:S(2)}) copy-start(f32[1536]{0:T(1024)S(1)} %get-tuple-element.25) | copy-start | bytes 18436
  25.6 7.2 %copy-start.22 = (f32[1536]{0:T(1024)}, f32[1536]{0:T(1024)S(1)}, u32[]{:S(2)}) copy-start(f32[1536]{0:T(1024)S(1)} %get-tuple-element.26) | copy-start | bytes 18436
  25.6 7.2 %copy-start.23 = (f32[1536]{0:T(1024)}, f32[1536]{0:T(1024)S(1)}, u32[]{:S(2)}) copy-start(f32[1536]{0:T(1024)S(1)} %get-tuple-element.27) | copy-start | bytes 18436
  25.6 7.2 %copy-start.24 = (f32[1536]{0:T(1024)}, f32[1536]{0:T(1024)S(1)}, u32[]{:S(2)}) copy-start(f32[1536]{0:T(1024)S(1)} %get-tuple-element.28) | copy-start | bytes 18436
  25.6 7.2 %copy-start.25 = (f32[1536]{0:T(1024)}, f32[1536]{0:T(1024)S(1)}, u32[]{:S(2)}) copy-start(f32[1536]{0:T(1024)S(1)} %get-tuple-element.29) | copy-start | bytes 18436
  25.6 7.2 %copy-start.26 = (f32[1536]{0:T(1024)}, f32[1536]{0:T(1024)S(1)}, u32[]{:S(2)}) copy-start(f32[1536]{0:T(1024)S(1)} %get-tuple-element.30) | copy-start | bytes 18436
  37.8 31.5 %all-to-all-start = ((bf16[1,7,7,8,2304]{4,1,2,0,3:T(8,128)(2,1)}), bf16[1,7,7,8,2304]{4,1,2,0,3:T(8,128)(2,1)}, u32[]{:S(2)}, u32[]{:S(2)}) async-start(bf16[1,7,7,8,2304]{4,1,2,0,3:T(8,128)(2,1)} %copy.39), calls=%async_computation | async-start | bytes 4128768 | tf_op jit(solution)/shard_map/all_to_all | solution.py:145
  168.8 32.1 %all-to-all-start.1 = ((bf16[1,56,7,1,768]{4,2,3,0,1:T(8,128)(2,1)}), bf16[1,56,7,1,768]{4,2,3,0,1:T(8,128)(2,1)}, u32[]{:S(2)}, u32[]{:S(2)}) async-start(bf16[1,56,7,1,768]{4,2,3,0,1:T(8,128)(2,1)} %copy.48), calls=%async_computation.1 | async-start | bytes 1376256 | tf_op jit(solution)/shard_map/all_to_all | solution.py:160
  201.0 101.7 %all-to-all-start.3 = ((bf16[1,56,7,1,2304]{4,2,3,0,1:T(8,128)(2,1)}), bf16[1,56,7,1,2304]{4,2,3,0,1:T(8,128)(2,1)}, u32[]{:S(2)}, u32[]{:S(2)}) async-start(bf16[1,56,7,1,2304]{4,2,3,0,1:T(8,128)(2,1)} %copy.61), calls=%async_computation.3 | async-start | bytes 4128768 | tf_op jit(solution)/shard_map/all_to_all | solution.py:180
  206.6 94.4 %reduce-scatter.17.cloned.1.call-start = ((), (), s32[]{:S(2)}) async-start(), calls=%async_computation.12 | async-start | bytes 1216512 | tf_op jit(solution)/shard_map/reduce_scatter | solution.py:213
  210.8 131.1 %reduce-scatter.23.cloned.1.call-start = ((), (), s32[]{:S(2)}) async-start(), calls=%async_computation.15 | async-start | bytes 221184
  302.6 133.8 %reduce-scatter.13.cloned.1.call-start = ((), (), s32[]{:S(2)}) async-start(), calls=%async_computation.10 | async-start | bytes 2433024 | tf_op jit(solution)/shard_map/reduce_scatter | solution.py:210
  312.6 221.7 %reduce-scatter.15.cloned.1.call-start = ((), (), s32[]{:S(2)}) async-start(), calls=%async_computation.11 | async-start | bytes 3649536 | tf_op jit(solution)/shard_map/reduce_scatter | solution.py:207
  318.5 256.6 %reduce-scatter.19.cloned.1.call-start = ((), (), s32[]{:S(2)}) async-start(), calls=%async_computation.13 | async-start | bytes 221184
  322.1 12.4 %copy-start.8 = (f32[392,768]{1,0:T(8,128)S(1)}, f32[392,768]{1,0:T(8,128)}, u32[]{:S(2)}) copy-start(f32[392,768]{1,0:T(8,128)} %copy-done.6) | copy-start | bytes 3612676
  322.1 12.4 %copy-start.12 = (bf16[1,7,7,8,1,768]{5,3,2,1,4,0:T(8,128)(2,1)S(1)}, bf16[1,7,7,8,1,768]{5,3,2,1,4,0:T(8,128)(2,1)}, u32[]{:S(2)}) copy-start(bf16[1,7,7,8,1,768]{5,3,2,1,4,0:T(8,128)(2,1)} %copy-done.11) | copy-start | bytes 1806340
  322.1 12.4 %copy-start.16 = (bf16[768,768]{1,0:T(8,128)(2,1)S(1)}, bf16[768,768]{1,0:T(8,128)(2,1)}, u32[]{:S(2)}) copy-start(bf16[768,768]{1,0:T(8,128)(2,1)} %param.15) | copy-start | bytes 3538948
  330.0 108.2 %collective-permute-start.2 = (bf16[1,1,56,1536]{3,2,1,0:T(8,128)(2,1)}, bf16[1,1,56,1536]{3,2,1,0:T(8,128)(2,1)}, u32[]{:S(2)}, u32[]{:S(2)}) collective-permute-start(bf16[1,1,56,1536]{3,2,1,0:T(8,128)(2,1)} %get-tuple-element.40), channel_id=1, source_target_pairs={{0,1},{1,2},{2,3},{3,4},{4,5},{5,6},{6,7},{8,9},{9,10},{10,11},{11... | collective-permute-start | bytes 516104 | tf_op jit(solution)/shard_map/ppermute | solution.py:21
  333.2 105.0 %collective-permute-start.3 = (bf16[1,1,56,1536]{3,2,1,0:T(8,128)(2,1)}, bf16[1,1,56,1536]{3,2,1,0:T(8,128)(2,1)}, u32[]{:S(2)}, u32[]{:S(2)}) collective-permute-start(bf16[1,1,56,1536]{3,2,1,0:T(8,128)(2,1)} %get-tuple-element.41), channel_id=1, source_target_pairs={{1,0},{2,1},{3,2},{4,3},{5,4},{6,5},{7,6},{9,8},{10,9},{11,10},{12... | collective-permute-start | bytes 516104 | tf_op jit(solution)/shard_map/ppermute | solution.py:22
  438.1 178.9 %reduce-scatter.21.cloned.1.call-start = ((), (), s32[]{:S(2)}) async-start(), calls=%async_computation.14 | async-start | bytes 663552
  (26 other events, 73.5 us)
Sparse Core Ops, SparseCore 0:
  211.3 89.6 reduce-scatter.16
  303.5 38.3 reduce-scatter.22
  346.2 90.1 reduce-scatter.12
  440.3 93.9 reduce-scatter.14
  536.6 38.4 reduce-scatter.18
  577.6 39.3 reduce-scatter.20
where the time goes:
time: 635 us; the launch traced here: 627 us
  waiting for transfers between devices  274 us (43%)
  local copies, waits for them, and re-layouts  126 us (20%)
  blocking collectives  75.4 us (12%)
  matrix products  64.7 us (10%)
  other arithmetic  38.9 us (6%)
  starting transfers between devices  33.1 us (5%)
  between operations  14.9 us (2%)
    reduce_scatter x1, waiting for transfers between devices, local(): lax.psum_scatter(qkv_local.astype(jnp.bfloat16), 'dp', scatter_dimension=...  93 us
    reduce_scatter x1, waiting for transfers between devices, local(): lax.psum_scatter(out_local.astype(jnp.bfloat16), 'dp', scatter_dimension=...  90.1 us
    unnamed x9, waiting for transfers between devices  78.4 us
    psum x1, blocking collectives, local(): depth_grad, gain_grad = lax.psum((depth_local, gain_local), ('dp', 'space'))  75.4 us
    unnamed x81, local copies, waits for them, and re-layouts  28.3 us
    another operation x10, local copies, waits for them, and re-layouts, depth_sum(): return jnp.stack(tap_sums)  14.5 us
    another operation x2, local copies, waits for them, and re-layouts, from_windows(): pieces = windowed.reshape(images, row_step, local_step, G, G, features)  13.3 us
  transfers between devices with their start and end apart: 14, of which 7 were waited for; matrix products, arithmetic and copies ran while one was open for 19% of the time, Pallas kernels for 0%

commit v1 on v0

--- a/solution.py
+++ b/solution.py
@@ -1,6 +1,8 @@
 import jax
 import jax.numpy as jnp
 from jax import lax
+from jax.experimental import pallas as pl
+from jax.experimental.pallas import tpu as pltpu
 from jax.sharding import PartitionSpec as P
 
 HEADS = 24
@@ -120,6 +122,184 @@
         grad_keys.astype(jnp.bfloat16),
         grad_values.astype(jnp.bfloat16),
     )
+
+
+MESH = pl.DeviceIdType.MESH
+F32, BF16 = jnp.float32, jnp.bfloat16
+
+
+def place():
+    dp, sp = lax.axis_index("dp"), lax.axis_index("space")
+    return lax.div(dp, 8), lax.rem(lax.div(dp, 2), 4), lax.rem(dp, 2), sp
+
+
+def dp_of(x, zh, core):
+    return (x * 4 + zh) * 2 + core
+
+
+def sum_partners(x, zh, core, sp):
+    dp = dp_of(x, zh, core)
+    ids = [(dp_of(x, zh, 1 - core), sp)]
+    ids += [(dp_of(lax.rem(x + j, 4), zh, core), sp) for j in (1, 2, 3)]
+    ids += [(dp_of(x, lax.rem(zh + j, 4), core), sp) for j in (1, 2, 3)]
+    ids += [(dp, lax.rem(sp + j, 8)) for j in range(1, 8)]
+    return ids
+
+
+def greet(ids):
+    barrier = pltpu.get_barrier_semaphore()
+    for one in ids:
+        pl.semaphore_signal(barrier, inc=1, device_id=one, device_id_type=MESH)
+    pl.semaphore_wait(barrier, len(ids))
+
+
+def remote(src, dst, send, recv, to):
+    return pltpu.make_async_remote_copy(
+        src_ref=src, dst_ref=dst, send_sem=send, recv_sem=recv, device_id=to, device_id_type=MESH
+    )
+
+
+def sum_kernel(
+    grads, small, proj_o, qkv_o, out_o, small_o,
+    r0, s0, r1, s1, r2, tiles, r3, sacc, sr,
+    s0s, s0r, s1s, s1r, s2s, s2r, s3s, s3r, sms, smr,
+):
+    x, zh, core, sp = place()
+    ids = sum_partners(x, zh, core, sp)
+    greet(ids)
+    pair, xs, zs, sps = ids[0], ids[1:4], ids[4:7], ids[7:14]
+    order = (1, 3, 2, 0)
+    first = []
+    for j in order:
+        xx = lax.rem(x + j, 4)
+        cp = remote(grads.at[xx, :, 1 - core], r0.at[xx], s0s.at[j], s0r.at[j], pair)
+        cp.start()
+        first.append(cp)
+
+    def small_stage(src, dst, base, peers):
+        cps = []
+        for n, peer in enumerate(peers):
+            cp = remote(src, sr.at[base + n], sms.at[base + n], smr.at[base + n], peer)
+            cp.start()
+            cps.append(cp)
+        return cps
+
+    def small_sum(cps, src, dst, base):
+        for cp in cps:
+            cp.wait()
+        total = src[...]
+        for n in range(len(cps)):
+            total = total + sr[base + n]
+        dst[...] = total
+
+    c0 = small_stage(small, sacc.at[0], 0, [pair])
+    second = []
+    for n, j in enumerate(order):
+        xx = lax.rem(x + j, 4)
+        first[n].wait_recv()
+
+        def body(i, carry, xx=xx):
+            s0[xx, i] = (grads[xx, i, core].astype(F32) + r0[xx, i].astype(F32)).astype(BF16)
+            return carry
+
+        lax.fori_loop(0, 4, body, 0)
+        if j:
+            cp = remote(s0.at[xx], r1.at[j - 1], s1s.at[j - 1], s1r.at[j - 1], xs[j - 1])
+            cp.start()
+            second.append(cp)
+    small_sum(c0, small, sacc.at[0], 0)
+    c1 = small_stage(sacc.at[0], None, 1, xs)
+    for cp in second:
+        cp.wait_recv()
+    third = []
+    for j in order:
+        zz = lax.rem(zh + j, 4)
+        total = s0[x, zz].astype(F32)
+        for n in range(3):
+            total = total + r1[n, zz].astype(F32)
+        s1[zz] = total.astype(BF16)
+        if j:
+            cp = remote(s1.at[zz], r2.at[j - 1], s2s.at[j - 1], s2r.at[j - 1], zs[j - 1])
+            cp.start()
+            third.append(cp)
+    small_sum(c1, sacc.at[0], sacc.at[1], 1)
+    c2 = small_stage(sacc.at[1], None, 4, zs)
+    for cp in third:
+        cp.wait_recv()
+    total = s1[zh].astype(F32)
+    for n in range(3):
+        total = total + r2[n].astype(F32)
+    for j in range(8):
+        half, col = j // 4, j % 4
+        qkv = total[24 * half : 24 * half + 24, 768 + 288 * col : 768 + 288 * col + 288]
+        out = total[24 * half : 24 * half + 24, 1920 + 96 * col : 1920 + 96 * col + 96]
+        tiles[j, :, 0:96] = total[:, 96 * j : 96 * j + 96].astype(BF16)
+        tiles[j, :, 128:272] = jnp.concatenate([qkv[:, :144], qkv[:, 144:]], axis=0).astype(BF16)
+        tiles[j, :, 272:320] = jnp.concatenate([out[:, :48], out[:, 48:]], axis=0).astype(BF16)
+    fourth = []
+    for j in range(1, 8):
+        to = lax.rem(sp + j, 8)
+        cp = remote(tiles.at[to], r3.at[j - 1], s3s.at[j - 1], s3r.at[j - 1], sps[j - 1])
+        cp.start()
+        fourth.append(cp)
+    small_sum(c2, sacc.at[1], sacc.at[2], 4)
+    c3 = small_stage(sacc.at[2], None, 7, sps)
+    for cp in fourth:
+        cp.wait_recv()
+    total = tiles[sp].astype(F32)
+    for n in range(7):
+        total = total + r3[n].astype(F32)
+    proj_o[...] = total[:, 0:96]
+    qkv_o[:, 0:144] = total[0:24, 128:272]
+    qkv_o[:, 144:288] = total[24:48, 128:272]
+    out_o[:, 0:48] = total[0:24, 272:320]
+    out_o[:, 48:96] = total[24:48, 272:320]
+    small_sum(c3, sacc.at[2], small_o, 7)
+    for cp in first + second + third + fourth:
+        cp.wait_send()
+
+
+def sum_grads(proj_local, qkv_local, out_local, depth_local, gain_local):
+    proj = proj_local.astype(BF16).reshape(32, 48, 768)
+    qkv = qkv_local.astype(BF16).reshape(32, 24, 2, 1152).transpose(0, 2, 1, 3).reshape(32, 48, 1152)
+    out = out_local.astype(BF16).reshape(32, 24, 2, 384).transpose(0, 2, 1, 3).reshape(32, 48, 384)
+    grads = jnp.concatenate([proj, qkv, out], axis=2).reshape(4, 4, 2, 48, 2304)
+    tail = jnp.concatenate([depth_local[8], gain_local, jnp.zeros((768,), F32)]).reshape(8, 384)
+    small = jnp.concatenate([depth_local[:8], tail], axis=1)
+    vm = pl.BlockSpec(memory_space=pltpu.VMEM)
+    dma = pltpu.SemaphoreType.DMA
+    proj_o, qkv_o, out_o, small_o = pl.pallas_call(
+        sum_kernel,
+        out_shape=(
+            jax.ShapeDtypeStruct((48, 96), F32),
+            jax.ShapeDtypeStruct((24, 288), F32),
+            jax.ShapeDtypeStruct((24, 96), F32),
+            jax.ShapeDtypeStruct((8, 1920), F32),
+        ),
+        in_specs=[vm, vm],
+        out_specs=(vm, vm, vm, vm),
+        scratch_shapes=[
+            pltpu.VMEM((4, 4, 48, 2304), BF16),
+            pltpu.VMEM((4, 4, 48, 2304), BF16),
+            pltpu.VMEM((3, 4, 48, 2304), BF16),
+            pltpu.VMEM((4, 48, 2304), BF16),
+            pltpu.VMEM((3, 48, 2304), BF16),
+            pltpu.VMEM((8, 48, 384), BF16),
+            pltpu.VMEM((7, 48, 384), BF16),
+            pltpu.VMEM((3, 8, 1920), F32),
+            pltpu.VMEM((14, 8, 1920), F32),
+            dma((4,)), dma((4,)), dma((3,)), dma((3,)), dma((3,)), dma((3,)),
+            dma((7,)), dma((7,)), dma((14,)), dma((14,)),
+        ],
+        compiler_params=pltpu.CompilerParams(
+            collective_id=0, has_side_effects=True, vmem_limit_bytes=48 * 1024 * 1024
+        ),
+        cost_estimate=pl.CostEstimate(flops=10**7, bytes_accessed=10**7, transcendentals=0),
+        name="sum_grads",
+    )(grads, small)
+    tail = small_o[:, 1536:].reshape(-1)
+    depth = jnp.concatenate([small_o[:, :1536], tail[None, :1536]], axis=0)
+    return depth, tail[1536:2304], proj_o, qkv_o, out_o
 
 
 def local(
@@ -202,28 +382,8 @@
     grad_pad = jnp.pad(grad_rows, ((0, 0), (0, 0), (1, 1), (0, 0)))
     hidden_grad = conv_backward(grad_pad, depth_weight, slab_rows, map_cols).astype(jnp.bfloat16)
     depth_local = depth_sum(hidden_pad, grad_conv, slab_rows, map_cols)
-    depth_grad, gain_grad = lax.psum((depth_local, gain_local), ("dp", "space"))
-    qkv_part, proj_part, out_part = (
-        lax.psum_scatter(
-            qkv_local.astype(jnp.bfloat16), "dp", scatter_dimension=0, tiled=True
-        ).astype(jnp.float32),
-        lax.psum_scatter(
-            proj_local.astype(jnp.bfloat16), "dp", scatter_dimension=0, tiled=True
-        ).astype(jnp.float32),
-        lax.psum_scatter(
-            out_local.astype(jnp.bfloat16), "dp", scatter_dimension=0, tiled=True
-        ).astype(jnp.float32),
-    )
-    qkv_grad, proj_grad, out_grad = (
-        lax.psum_scatter(
-            qkv_part.astype(jnp.bfloat16), "space", scatter_dimension=1, tiled=True
-        ).astype(jnp.float32),
-        lax.psum_scatter(
-            proj_part.astype(jnp.bfloat16), "space", scatter_dimension=1, tiled=True
-        ).astype(jnp.float32),
-        lax.psum_scatter(
-            out_part.astype(jnp.bfloat16), "space", scatter_dimension=1, tiled=True
-        ).astype(jnp.float32),
+    depth_grad, gain_grad, proj_grad, qkv_grad, out_grad = sum_grads(
+        proj_local, qkv_local, out_local, depth_local, gain_local
     )
     return (
         block_output,

time: 635 us -> 391 us (0.62)
  waiting for transfers between devices: 274 us -> 28.4 us
  Pallas kernels: 0 us -> 88.2 us
  blocking collectives: 75.4 us -> 0 us
  between operations: 14.9 us -> 1.59 us
    reduce_scatter x3 -> x0, waiting for transfers between devices: 185 us -> none  [the longest x1 93 us: local(): lax.psum_scatter(qkv_local.astype(jnp.bfloat16), 'dp', scatter_dimension=...]
    pallas_call x0 -> x1, Pallas kernels: none -> 88.2 us  [sum_grads(): pl.pallas_call(sum_kernel, out_shape=(jax.ShapeDtypeStruct((48, 96), F32)...]
    unnamed x9 -> x0, waiting for transfers between devices: 78.4 us -> none
    psum x1 -> x0, blocking collectives: 75.4 us -> none  [local(): depth_grad, gain_grad = lax.psum((depth_local, gain_local), ('dp', 'space'))]
    reshape x0 -> x5, local copies, waits for them, and re-layouts: none -> 19.1 us  [the longest x2 12.3 us: sum_grads(): qkv_local.astype(BF16).reshape(32, 24, 2, 1152).transpose(0, 2, 1, 3)]
    all_to_all x1, waiting for transfers between devices: 0.01 us -> 11.8 us  [local(): lax.all_to_all(grad_qkv_grid, 'space', split_axis=1, concat_axis=3, tiled...]
    concatenate x0 -> x4, other arithmetic: none -> 8.51 us  [the longest x1 6.23 us: sum_grads(): grads = jnp.concatenate([proj, qkv, out], axis=2).reshape(4, 4, 2, 48, 2304)]
    another operation x10 -> x9, local copies, waits for them, and re-layouts: 14.5 us -> 6.26 us  [depth_sum(): return jnp.stack(tap_sums)]
  transfers between devices with their start and end apart: 14 -> 8, of which waited for: 7 -> 4; matrix products, arithmetic and copies ran while one was open for 19% -> 19% of each run, Pallas kernels for 0% -> 0%
where the time goes in v1:
time: 391 us; the launch traced here: 383 us
  local copies, waits for them, and re-layouts  131 us (34%)
  Pallas kernels  88.2 us (23%)
  matrix products  61.6 us (16%)
  other arithmetic  38.9 us (10%)
  starting transfers between devices  33 us (8%)
  waiting for transfers between devices  28.4 us (7%)
    pallas_call x1, Pallas kernels, sum_grads(): pl.pallas_call(sum_kernel, out_shape=(jax.ShapeDtypeStruct((48, 96), F32)...  88.2 us
    unnamed x100, local copies, waits for them, and re-layouts  21.1 us
    another operation x2, local copies, waits for them, and re-layouts, from_windows(): pieces = windowed.reshape(images, row_step, local_step, G, G, features)  13.3 us
    reshape x2, local copies, waits for them, and re-layouts, sum_grads(): qkv_local.astype(BF16).reshape(32, 24, 2, 1152).transpose(0, 2, 1, 3)  12.3 us
    all_to_all x1, waiting for transfers between devices, local(): lax.all_to_all(grad_qkv_grid, 'space', split_axis=1, concat_axis=3, tiled...  11.8 us
    dot_general x1, matrix products, attend_backward(): jnp.einsum('nhqk,nkhd->nqhd', grad_low, key_rows, preferred_element_type=...  11.2 us
    dot_general x1, matrix products, attend_backward(): jnp.einsum('nhqk,nqhd->nkhd', grad_low, queries, preferred_element_type=j...  10.9 us
    all_to_all x1, waiting for transfers between devices, local(): lax.all_to_all(qkv_low.reshape(slab_shape + (3 * channels,)), 'space', sp...  10.5 us
  transfers between devices with their start and end apart: 8, of which 4 were waited for; matrix products, arithmetic and copies ran while one was open for 19% of the time, Pallas kernels for 0%

profile of v1, /device:TPU:2, one launch (start us, length us, event | category | flops | bytes accessed | tf_op | source)
XLA Modules:
  0.0 383.1 jit_solution(2865011837688357852)
XLA Ops:
  11.4 6.4 %all-to-all-start.2 = ((bf16[1,7,7,8,768]{4,1,2,0,3:T(8,128)(2,1)}), bf16[1,7,7,8,768]{4,1,2,0,3:T(8,128)(2,1)}, u32[]{:S(2)}, u32[]{:S(2)}) async-start(bf16[1,7,7,8,768]{4,1,2,0,3:T(8,128)(2,1)} %copy.55), calls=%async_computation.2 | async-start | bytes 1376256 | tf_op jit(solution)/shard_map/all_to_all | solution.py:349
  21.1 5.2 %multiply_convert_fusion.1 = (bf16[1,7,56,1536]{3,2,1,0:T(8,128)(2,1)S(1)}, f32[1,7,56,1536]{3,2,1,0:T(8,128)}) fusion(f32[1536]{0:T(1024)S(1)} %get-tuple-element.41, bf16[1,9,58,1536]{3,2,1,0:T(8,128)(2,1)S(1)} %select_maximum_fusion.2, f32[1536]{0:T(1024)S(1)} %get-tuple-element.42, bf16[1,1,56,1536]{3,2,1,0:T(8,128)(2,1)} %collective-permute-done.1, ...), kind=kLoop, calls=%fused_computation.73 | loop fusion | flops 22278144 | bytes 12441600 | tf_op jit(solution)/shard_map/convert_element_type | solution.py:319
  31.4 6.3 %all-to-all-start = ((bf16[1,7,7,8,2304]{4,1,2,0,3:T(8,128)(2,1)}), bf16[1,7,7,8,2304]{4,1,2,0,3:T(8,128)(2,1)}, u32[]{:S(2)}, u32[]{:S(2)}) async-start(bf16[1,7,7,8,2304]{4,1,2,0,3:T(8,128)(2,1)} %copy.43), calls=%async_computation | async-start | bytes 4128768 | tf_op jit(solution)/shard_map/all_to_all | solution.py:325
  52.7 10.5 %all-to-all-done = bf16[1,7,7,8,2304]{4,1,2,0,3:T(8,128)(2,1)} async-done(((bf16[1,7,7,8,2304]{4,1,2,0,3:T(8,128)(2,1)}), bf16[1,7,7,8,2304]{4,1,2,0,3:T(8,128)(2,1)}, u32[]{:S(2)}, u32[]{:S(2)}) %all-to-all-start) | async-done | bytes 1806368 | tf_op jit(solution)/shard_map/all_to_all | solution.py:325
  72.9 9.1 %reshape_reshape.12 = bf16[8,49,3,24,32]{4,3,2,0,1:T(8,128)(2,1)} reshape(bf16[1,8,1,7,7,2304]{5,1,4,3,2,0:T(8,128)(2,1)} %copy.45) | data formatting | bytes 3612672 | tf_op jit(solution)/shard_map/reshape;reshape | solution.py:334
  82.0 6.6 %fusion.96 = (bf16[8,49,1,24,32]{4,3,2,0,1:T(8,128)(2,1)}, bf16[8,49,1,24,32]{4,3,2,0,1:T(8,128)(2,1)}, bf16[8,49,1,24,32]{4,3,2,0,1:T(8,128)(2,1)}) fusion(bf16[8,49,3,24,32]{4,3,2,0,1:T(8,128)(2,1)} %reshape_reshape.12), kind=kLoop, calls=%fused_computation.147 | loop fusion | bytes 3612672 | tf_op jit(solution)/shard_map/slice | solution.py:335
  88.6 5.0 %copy.77 = bf16[8,49,1,24,32]{1,4,3,0,2:T(8,128)(2,1)} copy(bf16[8,49,1,24,32]{4,3,2,0,1:T(8,128)(2,1)} %get-tuple-element.46) | data formatting | bytes 1204224
  93.7 5.0 %copy.78 = bf16[8,49,1,24,32]{1,4,3,0,2:T(8,128)(2,1)} copy(bf16[8,49,1,24,32]{4,3,2,0,1:T(8,128)(2,1)} %get-tuple-element.48) | data formatting | bytes 1204224
  106.9 5.2 %copy.76 = bf16[8,49,1,24,32]{1,4,3,0,2:T(8,128)(2,1)} copy(bf16[8,49,1,24,32]{4,3,2,0,1:T(8,128)(2,1)} %get-tuple-element.47) | data formatting | bytes 1204224
  112.1 5.9 %fusion.60 = f32[8,24,49,49]{2,3,1,0:T(8,128)} fusion(bf16[8,49,24,32]{1,3,2,0:T(8,128)(2,1)} %copy.58, bf16[8,49,1,24,32]{1,4,3,0,2:T(8,128)(2,1)} %copy.76), kind=kOutput, calls=%fused_computation.90 | convolution fusion | flops 29503488 | bytes 3048192 | tf_op jit(solution)/shard_map/nqhd,nkhd->nhqk/dot_general | solution.py:108
  118.0 11.2 %fusion.71 = bf16[8,49,1,24,32]{1,4,3,0,2:T(8,128)(2,1)} fusion(f32[8,24,49,49]{2,3,1,0:T(8,128)} %fusion.60, bf16[8,49,1,24,32]{1,4,3,0,2:T(8,128)(2,1)} %copy.78, f32[8,24,49,49]{2,3,1,0:T(8,128)} %get-tuple-element.56, f32[8,24,49]{2,1,0:T(8,128)} %get-tuple-element.55), kind=kOutput, calls=%fused_computation.100 | convolution fusion | flops 33040944 | bytes 4929792 | tf_op jit(solution)/shard_map/nhqk,nkhd->nqhd/dot_general | solution.py:116
  129.2 10.9 %fusion.66 = bf16[8,49,1,24,32]{1,4,3,0,2:T(8,128)(2,1)} fusion(f32[8,24,49,49]{2,3,1,0:T(8,128)} %fusion.60, bf16[8,49,1,24,32]{1,4,3,0,2:T(8,128)(2,1)} %copy.77, f32[8,24,49,49]{2,3,1,0:T(8,128)} %get-tuple-element.56, f32[8,24,49]{2,1,0:T(8,128)} %get-tuple-element.55), kind=kOutput, calls=%fused_computation.99 | convolution fusion | flops 33040944 | bytes 4929792 | tf_op jit(solution)/shard_map/nhqk,nqhd->nkhd/dot_general | solution.py:119
  140.1 5.9 %fusion.79 = bf16[8,49,1,24,32]{1,4,3,0,2:T(8,128)(2,1)} fusion(bf16[8,49,24,32]{1,3,2,0:T(8,128)(2,1)} %copy.58, f32[8,24,49,49]{2,3,1,0:T(8,128)} %get-tuple-element.56, f32[8,24,49]{2,1,0:T(8,128)} %get-tuple-element.55), kind=kOutput, calls=%fused_computation.102 | convolution fusion | flops 30726528 | bytes 3085824 | tf_op jit(solution)/shard_map/nhqk,nqhd->nkhd/dot_general | solution.py:111
  150.7 5.9 %copy.50 = bf16[8,49,24,32]{3,2,0,1:T(8,128)(2,1)} copy(bf16[8,49,24,32]{1,3,2,0:T(8,128)(2,1)} %fusion.76) | data formatting | bytes 1204224 | tf_op jit(solution)/shard_map/convert_element_type | solution.py:103
  167.0 5.7 %pad_maximum_fusion.1 = bf16[8,49,3,24,32]{1,4,3,0,2:T(8,128)(2,1)} fusion(bf16[8,49,1,24,32]{1,4,3,0,2:T(8,128)(2,1)} %fusion.79, bf16[8,49,1,24,32]{1,4,3,0,2:T(8,128)(2,1)} %fusion.66, bf16[8,49,1,24,32]{1,4,3,0,2:T(8,128)(2,1)} %fusion.71), kind=kLoop, calls=%fused_computation.22 | loop fusion | flops 1806336 | bytes 3612672 | tf_op jit(solution)/shard_map/stack | solution.py:356
  172.7 9.3 %copy.63 = bf16[8,49,3,24,32]{4,3,2,0,1:T(8,128)(2,1)} copy(bf16[8,49,3,24,32]{1,4,3,0,2:T(8,128)(2,1)} %pad_maximum_fusion.1) | data formatting | bytes 3612672 | tf_op jit(solution)/shard_map/stack | solution.py:356
  182.0 9.2 %reshape_reshape.15 = bf16[1,8,1,7,7,2304]{5,1,4,3,2,0:T(8,128)(2,1)} reshape(bf16[8,49,3,24,32]{4,3,2,0,1:T(8,128)(2,1)} %copy.63) | data formatting | bytes 3612672 | tf_op jit(solution)/shard_map/reshape;reshape | solution.py:85
  194.5 5.9 %all-to-all-start.3 = ((bf16[1,56,7,1,2304]{4,2,3,0,1:T(8,128)(2,1)}), bf16[1,56,7,1,2304]{4,2,3,0,1:T(8,128)(2,1)}, u32[]{:S(2)}, u32[]{:S(2)}) async-start(bf16[1,56,7,1,2304]{4,2,3,0,1:T(8,128)(2,1)} %copy.65), calls=%async_computation.3 | async-start | bytes 4128768 | tf_op jit(solution)/shard_map/all_to_all | solution.py:360
  213.4 11.8 %all-to-all-done.3 = bf16[1,56,7,1,2304]{4,2,3,0,1:T(8,128)(2,1)} async-done(((bf16[1,56,7,1,2304]{4,2,3,0,1:T(8,128)(2,1)}), bf16[1,56,7,1,2304]{4,2,3,0,1:T(8,128)(2,1)}, u32[]{:S(2)}, u32[]{:S(2)}) %all-to-all-start.3) | async-done | bytes 1806368 | tf_op jit(solution)/shard_map/all_to_all | solution.py:360
  240.4 5.9 %fusion.46 = (f32[1536]{0:T(1024)S(1)}, f32[1536]{0:T(1024)S(1)}, f32[1536]{0:T(1024)S(1)}, f32[1536]{0:T(1024)S(1)}, f32[1536]{0:T(1024)S(1)}, /*index=5*/f32[1...) fusion(bf16[1,1,56,1536]{3,2,1,0:T(8,128)(2,1)} %collective-permute-done., ...), kind=kLoop, calls=%fused_computation.71 | loop fusion | flops 30091776 | bytes 14850048 | tf_op jit(solution)/shard_map/reduce_sum | solution.py:62
  251.7 8.1 %reshape.203 = bf16[32,24,2,1152]{3,2,1,0:T(2,128)(2,1)} reshape(bf16[768,2304]{1,0:T(8,128)(2,1)} %convolution_convert_fusion) | data formatting | bytes 7077888 | tf_op jit(solution)/shard_map/reshape | solution.py:264
  266.3 6.2 %pad_maximum_fusion.grads = bf16[4,4,2,48,2304]{4,3,2,1,0:T(8,128)(2,1)} fusion(bf16[4,4,2,48,384]{4,3,2,1,0:T(8,128)(2,1)} %bitcast.125, bf16[4,4,2,48,1152]{4,3,2,1,0:T(8,128)(2,1)} %bitcast.122, bf16[4,4,2,48,768]{4,3,2,1,0:T(8,128)(2,1)} %bitcast.131), kind=kLoop, calls=%fused_computation.12 | loop fusion | flops 21233664 | bytes 14155776 | tf_op jit(solution)/shard_map/concatenate | solution.py:266
  272.5 88.2 %sum_grads.1 = (f32[48,96]{1,0:T(8,128)S(1)}, f32[24,288]{1,0:T(8,128)S(1)}, f32[24,96]{1,0:T(8,128)S(1)}, f32[8,1920]{1,0:T(8,128)S(1)}) custom-call(bf16[4,4,2,48,2304]{4,3,2,1,0:T(8,128)(2,1)} %pad_maximum_fusion.grads, f32[8,1920]{1,0:T(8,128)S(1)} %pad_maximum_fusion.7.small), custom_call_target="tpu_custom_call" | custom-call | flops 10000000 | bytes 10000000 | tf_op jit(solution)/shard_map/sum_grads/pallas_call | solution.py:271
  370.3 5.6 %collective-permute-done.3 = bf16[1,1,56,1536]{3,2,1,0:T(8,128)(2,1)S(1)} collective-permute-done((bf16[1,1,56,1536]{3,2,1,0:T(8,128)(2,1)S(1)}, bf16[1,1,56,1536]{3,2,1,0:T(8,128)(2,1)S(1)}, u32[]{:S(2)}, u32[]{:S(2)}) %collective-permute-start.3) | collective-permute-done | bytes 172064 | tf_op jit(solution)/shard_map/ppermute | solution.py:24
  (169 shorter events, 126.6 us)
Async XLA Ops:
  0.6 27.4 %copy-start = (bf16[768,2304]{1,0:T(8,128)(2,1)S(1)}, bf16[768,2304]{1,0:T(8,128)(2,1)}, u32[]{:S(2)}) copy-start(bf16[768,2304]{1,0:T(8,128)(2,1)} %param.14) | copy-start | bytes 10616836
  2.6 16.6 %collective-permute-start = (bf16[1,1,56,1536]{3,2,1,0:T(8,128)(2,1)}, bf16[1,1,56,1536]{3,2,1,0:T(8,128)(2,1)}, u32[]{:S(2)}, u32[]{:S(2)}) collective-permute-start(bf16[1,1,56,1536]{3,2,1,0:T(8,128)(2,1)} %get-tuple-element.51), channel_id=1, source_target_pairs={{0,1},{1,2},{2,3},{3,4},{4,5},{5,6},{6,7},{8,9},{9,10},{10,11},{11... | collective-permute-start | bytes 516104 | tf_op jit(solution)/shard_map/ppermute | solution.py:23
  7.0 12.2 %collective-permute-start.1 = (bf16[1,1,56,1536]{3,2,1,0:T(8,128)(2,1)}, bf16[1,1,56,1536]{3,2,1,0:T(8,128)(2,1)}, u32[]{:S(2)}, u32[]{:S(2)}) collective-permute-start(bf16[1,1,56,1536]{3,2,1,0:T(8,128)(2,1)} %get-tuple-element.52), channel_id=1, source_target_pairs={{1,0},{2,1},{3,2},{4,3},{5,4},{6,5},{7,6},{9,8},{10,9},{11,10},{12... | collective-permute-start | bytes 516104 | tf_op jit(solution)/shard_map/ppermute | solution.py:24
  11.4 19.9 %all-to-all-start.2 = ((bf16[1,7,7,8,768]{4,1,2,0,3:T(8,128)(2,1)}), bf16[1,7,7,8,768]{4,1,2,0,3:T(8,128)(2,1)}, u32[]{:S(2)}, u32[]{:S(2)}) async-start(bf16[1,7,7,8,768]{4,1,2,0,3:T(8,128)(2,1)} %copy.55), calls=%async_computation.2 | async-start | bytes 1376256 | tf_op jit(solution)/shard_map/all_to_all | solution.py:349
  19.1 7.2 %copy-start.23 = (f32[1536]{0:T(1024)}, f32[1536]{0:T(1024)S(1)}, u32[]{:S(2)}) copy-start(f32[1536]{0:T(1024)S(1)} %get-tuple-element.34) | copy-start | bytes 18436
  19.1 7.2 %copy-start.25 = (f32[1536]{0:T(1024)}, f32[1536]{0:T(1024)S(1)}, u32[]{:S(2)}) copy-start(f32[1536]{0:T(1024)S(1)} %get-tuple-element.35) | copy-start | bytes 18436
  19.1 7.2 %copy-start.27 = (f32[1536]{0:T(1024)}, f32[1536]{0:T(1024)S(1)}, u32[]{:S(2)}) copy-start(f32[1536]{0:T(1024)S(1)} %get-tuple-element.36) | copy-start | bytes 18436
  19.1 7.2 %copy-start.29 = (f32[1536]{0:T(1024)}, f32[1536]{0:T(1024)S(1)}, u32[]{:S(2)}) copy-start(f32[1536]{0:T(1024)S(1)} %get-tuple-element.37) | copy-start | bytes 18436
  19.1 7.2 %copy-start.31 = (f32[1536]{0:T(1024)}, f32[1536]{0:T(1024)S(1)}, u32[]{:S(2)}) copy-start(f32[1536]{0:T(1024)S(1)} %get-tuple-element.38) | copy-start | bytes 18436
  31.4 31.8 %all-to-all-start = ((bf16[1,7,7,8,2304]{4,1,2,0,3:T(8,128)(2,1)}), bf16[1,7,7,8,2304]{4,1,2,0,3:T(8,128)(2,1)}, u32[]{:S(2)}, u32[]{:S(2)}) async-start(bf16[1,7,7,8,2304]{4,1,2,0,3:T(8,128)(2,1)} %copy.43), calls=%async_computation | async-start | bytes 4128768 | tf_op jit(solution)/shard_map/all_to_all | solution.py:325
  162.7 31.8 %all-to-all-start.1 = ((bf16[1,56,7,1,768]{4,2,3,0,1:T(8,128)(2,1)}), bf16[1,56,7,1,768]{4,2,3,0,1:T(8,128)(2,1)}, u32[]{:S(2)}, u32[]{:S(2)}) async-start(bf16[1,56,7,1,768]{4,2,3,0,1:T(8,128)(2,1)} %copy.52), calls=%async_computation.1 | async-start | bytes 1376256 | tf_op jit(solution)/shard_map/all_to_all | solution.py:340
  194.5 30.7 %all-to-all-start.3 = ((bf16[1,56,7,1,2304]{4,2,3,0,1:T(8,128)(2,1)}), bf16[1,56,7,1,2304]{4,2,3,0,1:T(8,128)(2,1)}, u32[]{:S(2)}, u32[]{:S(2)}) async-start(bf16[1,56,7,1,2304]{4,2,3,0,1:T(8,128)(2,1)} %copy.65), calls=%async_computation.3 | async-start | bytes 4128768 | tf_op jit(solution)/shard_map/all_to_all | solution.py:360
  362.6 15.1 %copy-start.9 = (bf16[1,7,56,1536]{3,2,1,0:T(8,128)(2,1)S(1)}, bf16[1,7,56,1536]{3,2,1,0:T(8,128)(2,1)}, u32[]{:S(2)}) copy-start(bf16[1,7,56,1536]{3,2,1,0:T(8,128)(2,1)} %get-tuple-element.43) | copy-start | bytes 3612676
  362.6 15.1 %copy-start.24 = (f32[1536]{0:T(1024)S(1)}, f32[1536]{0:T(1024)}, u32[]{:S(2)}) copy-start(f32[1536]{0:T(1024)} %copy-done.23) | copy-start | bytes 18436
  362.6 15.1 %copy-start.26 = (f32[1536]{0:T(1024)S(1)}, f32[1536]{0:T(1024)}, u32[]{:S(2)}) copy-start(f32[1536]{0:T(1024)} %copy-done.25) | copy-start | bytes 18436
  362.6 15.1 %copy-start.28 = (f32[1536]{0:T(1024)S(1)}, f32[1536]{0:T(1024)}, u32[]{:S(2)}) copy-start(f32[1536]{0:T(1024)} %copy-done.27) | copy-start | bytes 18436
  362.6 15.1 %copy-start.30 = (f32[1536]{0:T(1024)S(1)}, f32[1536]{0:T(1024)}, u32[]{:S(2)}) copy-start(f32[1536]{0:T(1024)} %copy-done.29) | copy-start | bytes 18436
  362.6 15.1 %copy-start.32 = (f32[1536]{0:T(1024)S(1)}, f32[1536]{0:T(1024)}, u32[]{:S(2)}) copy-start(f32[1536]{0:T(1024)} %copy-done.31) | copy-start | bytes 18436
  362.6 15.1 %copy-start.34 = (f32[1536]{0:T(1024)S(1)}, f32[1536]{0:T(1024)}, u32[]{:S(2)}) copy-start(f32[1536]{0:T(1024)} %copy-done.33) | copy-start | bytes 18436
  362.6 15.1 %copy-start.36 = (f32[1536]{0:T(1024)S(1)}, f32[1536]{0:T(1024)}, u32[]{:S(2)}) copy-start(f32[1536]{0:T(1024)} %copy-done.35) | copy-start | bytes 18436
  362.7 15.1 %copy-start.38 = (f32[1536]{0:T(1024)S(1)}, f32[1536]{0:T(1024)}, u32[]{:S(2)}) copy-start(f32[1536]{0:T(1024)} %copy-done.37) | copy-start | bytes 18436
  362.7 15.1 %copy-start.40 = (f32[1536]{0:T(1024)S(1)}, f32[1536]{0:T(1024)}, u32[]{:S(2)}) copy-start(f32[1536]{0:T(1024)} %copy-done.39) | copy-start | bytes 18436
  363.8 6.5 %collective-permute-start.2 = (bf16[1,1,56,1536]{3,2,1,0:T(8,128)(2,1)S(1)}, bf16[1,1,56,1536]{3,2,1,0:T(8,128)(2,1)S(1)}, u32[]{:S(2)}, u32[]{:S(2)}) collective-permute-start(bf16[1,1,56,1536]{3,2,1,0:T(8,128)(2,1)S(1)} %get-tuple-element.49), channel_id=1, source_target_pairs={{0,1},{1,2},{2,3},{3,4},{4,5},{5,6},{6,7},{8,9},{9,10},{10,11},{11... | collective-permute-start | bytes 516104 | tf_op jit(solution)/shard_map/ppermute | solution.py:23
  367.0 8.9 %collective-permute-start.3 = (bf16[1,1,56,1536]{3,2,1,0:T(8,128)(2,1)S(1)}, bf16[1,1,56,1536]{3,2,1,0:T(8,128)(2,1)S(1)}, u32[]{:S(2)}, u32[]{:S(2)}) collective-permute-start(bf16[1,1,56,1536]{3,2,1,0:T(8,128)(2,1)S(1)} %get-tuple-element.50), channel_id=1, source_target_pairs={{1,0},{2,1},{3,2},{4,3},{5,4},{6,5},{7,6},{9,8},{10,9},{11,10},{12... | collective-permute-start | bytes 516104 | tf_op jit(solution)/shard_map/ppermute | solution.py:24
  (30 other events, 106.2 us)

commit v2 on v0

v2 whole, which is shorter than its diff:
```python
import jax
import jax.numpy as jnp
from jax import lax
from jax.experimental import pallas as pl
from jax.experimental.pallas import tpu as pltpu
from jax.sharding import PartitionSpec as P

MESH = pl.DeviceIdType.MESH
F32, BF16 = jnp.float32, jnp.bfloat16
EPS = 1e-05
C, E, HEADS, HD = 768, 1536, 24, 32
ROWS, COLS, PLANE = 7, 56, 64
TOK = ROWS * PLANE
WIN = 512
SCALE = HD ** (-0.5)
ORDER = (1, 3, 2, 0)
NT = (((1,), (1,)), ((), ()))
TN = (((0,), (0,)), ((), ()))


def place():
    dp, sp = lax.axis_index("dp"), lax.axis_index("space")
    return dp, sp, lax.div(dp, 8), lax.rem(lax.div(dp, 2), 4), lax.rem(dp, 2)


def dp_of(x, zh, core):
    return (x * 4 + zh) * 2 + core


def greet(ids):
    barrier = pltpu.get_barrier_semaphore()
    for one in ids:
        pl.semaphore_signal(barrier, inc=1, device_id=one, device_id_type=MESH)
    pl.semaphore_wait(barrier, len(ids))


def remote(src, dst, send, recv, to):
    return pltpu.make_async_remote_copy(
        src_ref=src, dst_ref=dst, send_sem=send, recv_sem=recv, device_id=to, device_id_type=MESH
    )


def planes(ref, n):
    return ref.at[pl.ds(pl.multiple_of(n * PLANE, PLANE), PLANE)]


class Rows:
    def __init__(self, src, dst, ssem, rsem, dp, sp, out):
        self.src, self.dst, self.ssem, self.rsem = src, dst, ssem, rsem
        self.dp, self.sp, self.out = dp, sp, out

    def target(self, n):
        if self.out:
            row = self.sp * 7 + n
            return lax.rem(row, 8), lax.div(row, 8)
        row = n * 8 + self.sp
        return lax.div(row, 7), lax.rem(row, 7)

    def copies(self, n):
        to, slot = self.target(n)
        src, dst = planes(self.src, n), planes(self.dst, slot)
        far = remote(src, dst, self.ssem.at[n], self.rsem.at[slot], (self.dp, to))
        near = pltpu.make_async_copy(src, dst, self.rsem.at[slot])
        return to, far, near

    def start(self, n):
        to, far, near = self.copies(n)

        @pl.when(to != self.sp)
        def _():
            far.start()

        @pl.when(to == self.sp)
        def _():
            near.start()

    def wait_recv(self, n):
        one = planes(self.dst, n)
        pltpu.make_async_copy(one, one, self.rsem.at[n]).wait()

    def wait_send(self, n):
        to, far, _ = self.copies(n)

        @pl.when(to != self.sp)
        def _():
            far.wait_send()


class Halo:
    def __init__(self, top, bottom, halo, ssem, rsem, dp, sp):
        self.sp = sp
        self.up = remote(top, halo.at[1], ssem.at[0], rsem.at[1], (dp, jnp.maximum(sp - 1, 0)))
        self.down = remote(bottom, halo.at[0], ssem.at[1], rsem.at[0], (dp, jnp.minimum(sp + 1, 7)))
        self.halo = halo

    def start(self):
        @pl.when(self.sp > 0)
        def _():
            self.up.start()

        @pl.when(self.sp < 7)
        def _():
            self.down.start()

        zero = jnp.zeros(self.halo.shape[1:], self.halo.dtype)

        @pl.when(self.sp == 0)
        def _():
            self.halo[0] = zero

        @pl.when(self.sp == 7)
        def _():
            self.halo[1] = zero

    def wait_recv(self):
        @pl.when(self.sp > 0)
        def _():
            self.down.wait_recv()

        @pl.when(self.sp < 7)
        def _():
            self.up.wait_recv()

    def wait_send(self):
        @pl.when(self.sp > 0)
        def _():
            self.up.wait_send()

        @pl.when(self.sp < 7)
        def _():
            self.down.wait_send()


def col_masks(lanes):
    index = lax.broadcasted_iota(jnp.int32, (COLS, lanes), 0)
    return index == 0, index == COLS - 1


def later(value, first):
    return jnp.where(first, 0.0, pltpu.roll(value, 1, 0))


def earlier(value, last):
    return jnp.where(last, 0.0, pltpu.roll(value, COLS - 1, 0))


def padded(value):
    return jnp.concatenate([value, jnp.zeros((PLANE - COLS, value.shape[1]), F32)], axis=0)


def gelu_and_slope(value):
    k0, k1 = 0.7978845608028654, 0.044715
    square = value * value
    tanh = jnp.tanh(k0 * value * (1.0 + k1 * square))
    half = 0.5 * (1.0 + tanh)
    slope = half + 0.5 * value * (1.0 - tanh * tanh) * (k0 * (1.0 + 3.0 * k1 * square))
    return value * half, slope


def conv_forward(hidden, halo, taps, act, slope):
    def chunk(n, carry):
        lanes = pl.ds(pl.multiple_of(n * 128, 128), 128)
        first, last = col_masks(128)
        rows = [halo[0, :, lanes].astype(F32)]
        rows += [hidden[r, :, lanes].astype(F32) for r in range(ROWS)]
        rows += [halo[1, :, lanes].astype(F32)]
        tap = [taps[t : t + 1, lanes] for t in range(9)]
        for r in range(ROWS):
            part = [sum(tap[3 * a + b] * rows[r + a] for a in range(3)) for b in range(3)]
            conv = later(part[0], first) + part[1] + earlier(part[2], last)
            low, grad = gelu_and_slope(conv)
            act[PLANE * r : PLANE * (r + 1), lanes] = padded(low).astype(BF16)
            slope[PLANE * r : PLANE * (r + 1), lanes] = padded(grad)
        return carry

    lax.fori_loop(0, E // 128, chunk, 0)


def normal(mid):
    mean = jnp.mean(mid, axis=1, keepdims=True)
    centred = mid - mean
    inv = lax.rsqrt(jnp.mean(centred * centred, axis=1, keepdims=True) + EPS)
    return centred * inv, inv


def front_kernel(
    block, hidden, cot, depth_w, proj_w, gain,
    win_n, win_c, mid, act, slope,
    halo, taps, own_n, own_c, hs, hr, ns, nr, cs, cr,
):
    dp, sp, x, zh, core = place()
    greet([(dp, lax.rem(sp + j, 8)) for j in range(1, 8)])
    edge = Halo(hidden.at[0], hidden.at[ROWS - 1], halo, hs, hr, dp, sp)
    edge.start()
    cots = Rows(own_c, win_c, cs, cr, dp, sp, True)
    norms = Rows(own_n, win_n, ns, nr, dp, sp, True)
    for r in range(ROWS):
        own_c[PLANE * r : PLANE * (r + 1)] = padded(cot[r].astype(F32)).astype(BF16)
        cots.start(r)
    taps[0:9] = depth_w[...].astype(F32)
    edge.wait_recv()
    conv_forward(hidden, halo, taps, act, slope)

    def proj(n, carry):
        lanes = pl.ds(pl.multiple_of(n * 256, 256), 256)
        mid[:, lanes] = jnp.dot(act[...], proj_w[:, lanes], preferred_element_type=F32)
        return carry

    lax.fori_loop(0, C // 256, proj, 0)

    def norm(r, carry):
        here = pl.ds(pl.multiple_of(r * PLANE, PLANE), PLANE)
        total = mid[here, :] + padded(block[r].astype(F32))
        mid[here, :] = total
        own_n[here, :] = (normal(total)[0] * gain[...]).astype(BF16)
        norms.start(r)
        return carry

    lax.fori_loop(0, ROWS, norm, 0)
    for r in range(ROWS):
        cots.wait_recv(r)
        norms.wait_recv(r)
    for r in range(ROWS):
        cots.wait_send(r)
        norms.wait_send(r)
    edge.wait_send()


def window_place(index):
    win, n = index >> 6, index & 63
    g = (n * 37) >> 8
    return jnp.where(n < 49, g * PLANE + (n - 7 * g) * 8 + win, -1)


def attention(qkv, gatt, att, gqkv):
    lane = lax.broadcasted_iota(jnp.int32, (64, 128), 1) >> 5
    big = lax.broadcasted_iota(jnp.int32, (256, 128), 0) >> 6
    own = (big == (lax.broadcasted_iota(jnp.int32, (256, 128), 1) >> 5)).astype(F32).astype(BF16)
    valid = lax.broadcasted_iota(jnp.int32, (64, 256), 0) < 49

    def spread(value):
        return jnp.concatenate([value] * 4, axis=0) * own

    def gather(value):
        return jnp.where(
            lane < 2,
            jnp.where(lane == 0, value[0:64], value[64:128]),
            jnp.where(lane == 2, value[128:192], value[192:256]),
        )

    def window(w, carry):
        rows = pl.ds(pl.multiple_of(w * 64, 64), 64)
        for g in range(6):
            at = [slice(part * C + 128 * g, part * C + 128 * (g + 1)) for part in range(3)]
            query, key, value = (qkv[rows, at[part]] for part in range(3))
            query = spread(query)
            grad = spread(gatt[rows, at[0]])
            score = lax.dot_general(key, query, NT, preferred_element_type=F32) * SCALE
            score = jnp.where(valid, score, -1e30)
            power = jnp.exp(score - jnp.max(score, axis=0, keepdims=True))
            prob = power * (1.0 / jnp.sum(power, axis=0, keepdims=True))
            low = prob.astype(BF16)
            grad_prob = lax.dot_general(value, grad, NT, preferred_element_type=F32)
            inner = jnp.sum(grad_prob * prob, axis=0, keepdims=True)
            grad_low = (prob * (grad_prob - inner) * SCALE).astype(BF16)
            att[rows, at[0]] = gather(
                lax.dot_general(low, value, TN, preferred_element_type=F32)
            ).astype(BF16)
            gqkv[rows, at[0]] = gather(
                lax.dot_general(grad_low, key, TN, preferred_element_type=F32)
            ).astype(BF16)
            gqkv[rows, at[1]] = jnp.dot(grad_low, query, preferred_element_type=F32).astype(BF16)
            gqkv[rows, at[2]] = jnp.dot(low, grad, preferred_element_type=F32).astype(BF16)
        return carry

    lax.fori_loop(0, 8, window, 0)


def half_rows(value):
    left, right = (value[:, 128 * h : 128 * (h + 1)].reshape(32, 24, 128) for h in range(2))
    return jnp.concatenate([left, right], axis=1).reshape(4, 4, 2, 48, 128).astype(BF16)


def middle_kernel(
    win_n, win_c, qkv_w, out_w,
    att_t, gn_t, grads,
    norm_p, cot_p, qkv, gatt, att, gqkv, turned, gn_p,
):
    index = window_place(lax.broadcasted_iota(jnp.int32, (WIN, 1), 0))
    tokens = lax.broadcasted_iota(jnp.int32, (WIN, TOK), 1)
    perm = (index == tokens).astype(F32).astype(BF16)
    norm_p[...] = jnp.dot(perm, win_n[...], preferred_element_type=F32).astype(BF16)
    cot_p[...] = jnp.dot(perm, win_c[...], preferred_element_type=F32).astype(BF16)

    def tile(n):
        return pl.ds(pl.multiple_of(n * 256, 256), 256)

    def qkv_step(n, carry):
        qkv[:, tile(n)] = jnp.dot(
            norm_p[...], qkv_w[:, tile(n)], preferred_element_type=F32
        ).astype(BF16)
        return carry

    lax.fori_loop(0, 9, qkv_step, 0)

    def gatt_step(n, carry):
        gatt[:, tile(n)] = lax.dot_general(
            cot_p[...], out_w[tile(n), :], NT, preferred_element_type=F32
        ).astype(BF16)
        return carry

    lax.fori_loop(0, 3, gatt_step, 0)
    attention(qkv, gatt, att, gqkv)
    index = window_place(lax.broadcasted_iota(jnp.int32, (1, WIN), 1))
    tokens = lax.broadcasted_iota(jnp.int32, (TOK, WIN), 0)
    back = (index == tokens).astype(F32).astype(BF16)
    att_t[...] = jnp.dot(back, att[...], preferred_element_type=F32).astype(BF16)

    def gn_step(n, carry):
        gn_p[:, tile(n)] = lax.dot_general(
            gqkv[...], qkv_w[tile(n), :], NT, preferred_element_type=F32
        ).astype(BF16)
        return carry

    lax.fori_loop(0, 3, gn_step, 0)
    gn_t[...] = jnp.dot(back, gn_p[...], preferred_element_type=F32).astype(BF16)
    turned[...] = att[...].T

    def lanes(n):
        return pl.ds(pl.multiple_of(n * 128, 128), 128)

    def out_step(n, carry):
        right = jnp.concatenate([cot_p[:, lanes(n)], cot_p[:, lanes(n + 3)]], axis=1)
        grads[:, :, :, :, lanes(n + 9)] = half_rows(
            jnp.dot(turned[...], right, preferred_element_type=F32)
        )
        return carry

    lax.fori_loop(0, 3, out_step, 0)
    turned[...] = norm_p[...].T

    def grad_step(n, carry):
        right = jnp.concatenate([gqkv[:, lanes(n)], gqkv[:, lanes(n + 9)]], axis=1)
        grads[:, :, :, :, lanes(n)] = half_rows(
            jnp.dot(turned[...], right, preferred_element_type=F32)
        )
        return carry

    lax.fori_loop(0, 9, grad_step, 0)


class Sum:
    def __init__(self, grads, bufs, sems, spot, pair, xs, zs):
        self.g = grads
        self.r0, self.s0, self.r1, self.s1, self.r2 = bufs
        self.s0s, self.s0r, self.s1s, self.s1r, self.s2s, self.s2r = sems
        self.x, self.zh, self.core = spot
        self.pair, self.xs, self.zs = pair, xs, zs
        self.sent = []
        self.first, self.second, self.third = {}, [], []

    def start0(self, j):
        xx = lax.rem(self.x + j, 4)
        cp = remote(
            self.g.at[xx, :, 1 - self.core], self.r0.at[xx], self.s0s.at[j], self.s0r.at[j], self.pair
        )
        cp.start()
        self.first[j] = cp
        self.sent.append(cp)

    def step1(self, j):
        xx = lax.rem(self.x + j, 4)
        self.first[j].wait_recv()

        def body(i, carry):
            mine = self.g[xx, i, self.core].astype(F32)
            self.s0[xx, i] = (mine + self.r0[xx, i].astype(F32)).astype(BF16)
            return carry

        lax.fori_loop(0, 4, body, 0)
        if j:
            cp = remote(
                self.s0.at[xx], self.r1.at[j - 1], self.s1s.at[j - 1], self.s1r.at[j - 1], self.xs[j - 1]
            )
            cp.start()
            self.second.append(cp)
            self.sent.append(cp)

    def step2(self):
        for cp in self.second:
            cp.wait_recv()
        for j in ORDER:
            zz = lax.rem(self.zh + j, 4)
            total = self.s0[self.x, zz].astype(F32)
            for n in range(3):
                total = total + self.r1[n, zz].astype(F32)
            self.s1[zz] = total.astype(BF16)
            if j:
                cp = remote(
                    self.s1.at[zz], self.r2.at[j - 1], self.s2s.at[j - 1], self.s2r.at[j - 1], self.zs[j - 1]
                )
                cp.start()
                self.third.append(cp)
                self.sent.append(cp)

    def step3(self):
        for cp in self.third:
            cp.wait_recv()
        total = self.s1[self.zh].astype(F32)
        for n in range(3):
            total = total + self.r2[n].astype(F32)
        return total


class Last:
    def __init__(self, tiles, recv, ssem, rsem, sp, sps):
        self.tiles, self.recv, self.sp = tiles, recv, sp
        self.cps = [
            remote(tiles.at[lax.rem(sp + j, 8)], recv.at[j - 1], ssem.at[j - 1], rsem.at[j - 1], sps[j - 1])
            for j in range(1, 8)
        ]

    def start(self):
        for cp in self.cps:
            cp.start()

    def total(self):
        for cp in self.cps:
            cp.wait_recv()
        total = self.tiles[self.sp].astype(F32)
        for n in range(7):
            total = total + self.recv[n].astype(F32)
        return total

    def wait_send(self):
        for cp in self.cps:
            cp.wait_send()


class Small:
    def __init__(self, acc, recv, ssem, rsem, stages):
        self.acc, self.recv, self.ssem, self.rsem, self.stages = acc, recv, ssem, rsem, stages
        self.cps, base = [], 0
        for n, peers in enumerate(stages):
            self.cps.append([
                remote(acc.at[n], recv.at[base + i], ssem.at[base + i], rsem.at[base + i], peer)
                for i, peer in enumerate(peers)
            ])
            base += len(peers)

    def start(self, n):
        for cp in self.cps[n]:
            cp.start()

    def total(self, n):
        base = sum(len(peers) for peers in self.stages[:n])
        total = self.acc[n]
        for i, cp in enumerate(self.cps[n]):
            cp.wait_recv()
            total = total + self.recv[base + i]
        return total

    def step(self, n):
        self.acc[n + 1] = self.total(n)
        self.start(n + 1)

    def wait_send(self):
        for stage in self.cps:
            for cp in stage:
                cp.wait_send()


def conv_backward(grad, halo, hidden, taps, hidden_grad, depth):
    def chunk(n, carry):
        lanes = pl.ds(pl.multiple_of(n * 128, 128), 128)
        first, last = col_masks(128)
        rows = [halo[0, 0:COLS, lanes].astype(F32)]
        rows += [grad[PLANE * r : PLANE * r + COLS, lanes].astype(F32) for r in range(ROWS)]
        rows += [halo[1, 0:COLS, lanes].astype(F32)]
        tap = [taps[t : t + 1, lanes] for t in range(9)]
        sums = [jnp.zeros((8, 128), F32) for _ in range(9)]
        for r in range(ROWS):
            near = [rows[r + 2 - a] for a in range(3)]
            part = [sum(tap[3 * a + b] * near[a] for a in range(3)) for b in range(3)]
            total = earlier(part[0], last) + part[1] + later(part[2], first)
            hidden_grad[r, :, lanes] = total.astype(BF16)
            own = hidden[r, :, lanes].astype(F32)
            moved = [later(own, first), own, earlier(own, last)]
            for a in range(3):
                for b in range(3):
                    product = moved[b] * near[a]
                    for i in range(7):
                        sums[3 * a + b] = sums[3 * a + b] + product[8 * i : 8 * i + 8]
        for t in range(9):
            depth[t : t + 1, lanes] = jnp.sum(sums[t], axis=0, keepdims=True)
        return carry

    lax.fori_loop(0, E // 128, chunk, 0)


def back_kernel(
    att_w, gn_w, mid, act, slope, hidden, cot, depth_w, proj_w, gain, out_w, grads,
    block_o, input_o, hidden_o, depth_o, gain_o, proj_o, qkv_o, out_o,
    att, gn, ig, gc, halo, taps, depth, pgrads,
    ar0, as0, ar1, as1, ar2, pr0, ps0, pr1, ps1, pr2,
    atile, arecv, ptile, precv, sacc, srecv,
    ts, tr, us, ur, hs, hr,
    a0s, a0r, a1s, a1r, a2s, a2r, p0s, p0r, p1s, p1r, p2s, p2r,
    las, lar, lps, lpr, sms, smr,
):
    dp, sp, x, zh, core = place()
    pair = (dp_of(x, zh, 1 - core), sp)
    xs = [(dp_of(lax.rem(x + j, 4), zh, core), sp) for j in (1, 2, 3)]
    zs = [(dp_of(x, lax.rem(zh + j, 4), core), sp) for j in (1, 2, 3)]
    sps = [(dp, lax.rem(sp + j, 8)) for j in range(1, 8)]
    greet([pair] + xs + zs + sps)
    spot = (x, zh, core)
    asum = Sum(grads, (ar0, as0, ar1, as1, ar2), (a0s, a0r, a1s, a1r, a2s, a2r), spot, pair, xs, zs)
    psum = Sum(pgrads, (pr0, ps0, pr1, ps1, pr2), (p0s, p0r, p1s, p1r, p2s, p2r), spot, pair, xs, zs)
    alast = Last(atile, arecv, las, lar, sp, sps)
    plast = Last(ptile, precv, lps, lpr, sp, sps)
    small = Small(sacc, srecv, sms, smr, ([pair], xs, zs, sps))
    gns = Rows(gn_w, gn, us, ur, dp, sp, False)
    atts = Rows(att_w, att, ts, tr, dp, sp, False)
    for g in range(ROWS):
        gns.start(g)
    for g in range(ROWS):
        atts.start(g)
    for j in ORDER:
        asum.start0(j)
    taps[0:9] = depth_w[...].astype(F32)

    for r in range(ROWS):
        gns.wait_recv(r)

    def norm_step(r, carry):
        here = pl.ds(pl.multiple_of(r * PLANE, PLANE), PLANE)
        hat, inv = normal(mid[here, :])
        wide = gn[here, :].astype(F32)
        grad_hat = wide * gain[...]
        carry = carry + (wide * hat).reshape(8, 8, C).sum(axis=0)
        inner = jnp.mean(grad_hat * hat, axis=1, keepdims=True)
        mean = jnp.mean(grad_hat, axis=1, keepdims=True)
        cots = padded(cot[r].astype(F32))
        low = (cots + inv * (grad_hat - mean - hat * inner)).astype(BF16)
        ig[here, :] = low
        input_o[r] = low[0:COLS]
        return carry

    gain_part = lax.fori_loop(0, ROWS, norm_step, jnp.zeros((8, C), F32))
    gain_part = jnp.sum(gain_part, axis=0, keepdims=True)
    for j in ORDER:
        asum.step1(j)
    for j in ORDER:
        xx = lax.rem(x + j, 4)
        left = act[:, pl.ds(pl.multiple_of(xx * 384, 128), 384)].T
        for n in range(3):
            tile = slice(256 * n, 256 * (n + 1))
            part = jnp.dot(left, ig[:, tile], preferred_element_type=F32)
            pgrads[xx, :, :, :, tile] = part.reshape(4, 2, 48, 256).astype(BF16)
        psum.start0(j)

    def act_step(n, carry):
        here = pl.ds(pl.multiple_of(n * 256, 256), 256)
        part = lax.dot_general(ig[...], proj_w[here, :], NT, preferred_element_type=F32)
        gc[:, here] = (part * slope[:, here]).astype(BF16)
        return carry

    lax.fori_loop(0, E // 256, act_step, 0)
    edge = Halo(gc.at[0:PLANE], gc.at[TOK - PLANE : TOK], halo, hs, hr, dp, sp)
    edge.start()
    for j in ORDER:
        psum.step1(j)
    for r in range(ROWS):
        atts.wait_recv(r)

    def out_step(n, carry):
        here = pl.ds(pl.multiple_of(n * 256, 256), 256)
        part = jnp.dot(att[...], out_w[:, here], preferred_element_type=F32)
        part = (part + mid[:, here]).astype(BF16)
        for r in range(ROWS):
            block_o[r, :, here] = part[PLANE * r : PLANE * r + COLS]
        return carry

    lax.fori_loop(0, C // 256, out_step, 0)
    asum.step2()
    edge.wait_recv()
    conv_backward(gc, halo, hidden, taps, hidden_o, depth)
    sacc[0, 0:8, 0:E] = depth[0:8]
    for i in range(4):
        sacc[0, i : i + 1, E : E + 384] = depth[8:9, 384 * i : 384 * (i + 1)]
    for i in range(2):
        sacc[0, 4 + i : 5 + i, E : E + 384] = gain_part[:, 384 * i : 384 * (i + 1)]
    sacc[0, 6:8, E : E + 384] = jnp.zeros((2, 384), F32)
    small.start(0)
    psum.step2()
    total = asum.step3()
    for j in range(8):
        half, col = j // 4, j % 4
        qkv = total[24 * half : 24 * half + 24, 288 * col : 288 * col + 288]
        out = total[24 * half : 24 * half + 24, 1152 + 96 * col : 1152 + 96 * col + 96]
        atile[j, :, 0:144] = jnp.concatenate([qkv[:, :144], qkv[:, 144:]], axis=0).astype(BF16)
        atile[j, :, 144:192] = jnp.concatenate([out[:, :48], out[:, 48:]], axis=0).astype(BF16)
    alast.start()
    small.step(0)
    total = psum.step3()
    for j in range(8):
        ptile[j, :, 0:96] = total[:, 96 * j : 96 * j + 96].astype(BF16)
    plast.start()
    small.step(1)
    total = alast.total()
    qkv_o[:, 0:144] = total[0:24, 0:144]
    qkv_o[:, 144:288] = total[24:48, 0:144]
    out_o[:, 0:48] = total[0:24, 144:192]
    out_o[:, 48:96] = total[24:48, 144:192]
    small.step(2)
    proj_o[...] = plast.total()[:, 0:96]
    total = small.total(3)
    depth_o[0:8] = total[:, 0:E]
    for i in range(4):
        depth_o[8:9, 384 * i : 384 * (i + 1)] = total[i : i + 1, E : E + 384]
    for i in range(2):
        gain_o[:, 384 * i : 384 * (i + 1)] = total[4 + i : 5 + i, E : E + 384]
    for g in range(ROWS):
        gns.wait_send(g)
        atts.wait_send(g)
    edge.wait_send()
    for cp in asum.sent + psum.sent:
        cp.wait_send()
    alast.wait_send()
    plast.wait_send()
    small.wait_send()


VM = pl.BlockSpec(memory_space=pltpu.VMEM)
DMA = pltpu.SemaphoreType.DMA
MIB = 1024 * 1024


def shape(dims, dtype=BF16):
    return jax.ShapeDtypeStruct(dims, dtype)


def sum_bufs(width):
    return [
        pltpu.VMEM((4, 4, 48, width), BF16),
        pltpu.VMEM((4, 4, 48, width), BF16),
        pltpu.VMEM((3, 4, 48, width), BF16),
        pltpu.VMEM((4, 48, width), BF16),
        pltpu.VMEM((3, 48, width), BF16),
    ]


def sum_sems():
    return [DMA((4,)), DMA((4,)), DMA((3,)), DMA((3,)), DMA((3,)), DMA((3,))]


def local(block, hidden, cot, depth_w, proj_w, gain, qkv_w, out_w):
    gain = gain.reshape(1, C)
    block, hidden, cot = block[0], hidden[0], cot[0]
    win_n, win_c, mid, act, slope = pl.pallas_call(
        front_kernel,
        out_shape=(shape((TOK, C)), shape((TOK, C)), shape((TOK, C), F32), shape((TOK, E)), shape((TOK, E), F32)),
        in_specs=[VM] * 6,
        out_specs=(VM,) * 5,
        scratch_shapes=[
            pltpu.VMEM((2, COLS, E), BF16),
            pltpu.VMEM((16, E), F32),
            pltpu.VMEM((TOK, C), BF16),
            pltpu.VMEM((TOK, C), BF16),
            DMA((2,)), DMA((2,)), DMA((7,)), DMA((7,)), DMA((7,)), DMA((7,)),
        ],
        compiler_params=pltpu.CompilerParams(
            collective_id=1, has_side_effects=True, vmem_limit_bytes=48 * MIB
        ),
        name="front",
    )(block, hidden, cot, depth_w, proj_w, gain)
    att_w, gn_w, grads = pl.pallas_call(
        middle_kernel,
        out_shape=(shape((TOK, C)), shape((TOK, C)), shape((4, 4, 2, 48, E))),
        in_specs=[VM] * 4,
        out_specs=(VM,) * 3,
        scratch_shapes=[
            pltpu.VMEM((WIN, C), BF16),
            pltpu.VMEM((WIN, C), BF16),
            pltpu.VMEM((WIN, 3 * C), BF16),
            pltpu.VMEM((WIN, C), BF16),
            pltpu.VMEM((WIN, C), BF16),
            pltpu.VMEM((WIN, 3 * C), BF16),
            pltpu.VMEM((C, WIN), BF16),
            pltpu.VMEM((WIN, C), BF16),
        ],
        compiler_params=pltpu.CompilerParams(vmem_limit_bytes=48 * MIB),
        name="middle",
    )(win_n, win_c, qkv_w, out_w)
    block_o, input_o, hidden_o, depth_o, gain_o, proj_o, qkv_o, out_o = pl.pallas_call(
        back_kernel,
        out_shape=(
            shape((ROWS, COLS, C)), shape((ROWS, COLS, C)), shape((ROWS, COLS, E)),
            shape((9, E), F32), shape((1, C), F32),
            shape((48, 96), F32), shape((24, 288), F32), shape((24, 96), F32),
        ),
        in_specs=[VM] * 12,
        out_specs=(VM,) * 8,
        scratch_shapes=[
            pltpu.VMEM((TOK, C), BF16),
            pltpu.VMEM((TOK, C), BF16),
            pltpu.VMEM((TOK, C), BF16),
            pltpu.VMEM((TOK, E), BF16),
            pltpu.VMEM((2, PLANE, E), BF16),
            pltpu.VMEM((16, E), F32),
            pltpu.VMEM((16, E), F32),
            pltpu.VMEM((4, 4, 2, 48, C), BF16),
        ]
        + sum_bufs(E)
        + sum_bufs(C)
        + [
            pltpu.VMEM((8, 48, 256), BF16),
            pltpu.VMEM((7, 48, 256), BF16),
            pltpu.VMEM((8, 48, 128), BF16),
            pltpu.VMEM((7, 48, 128), BF16),
            pltpu.VMEM((4, 8, 1920), F32),
            pltpu.VMEM((14, 8, 1920), F32),
        ]
        + [DMA((7,)), DMA((7,)), DMA((7,)), DMA((7,)), DMA((2,)), DMA((2,))]
        + sum_sems()
        + sum_sems()
        + [DMA((7,)), DMA((7,)), DMA((7,)), DMA((7,)), DMA((14,)), DMA((14,))],
        compiler_params=pltpu.CompilerParams(
            collective_id=2, has_side_effects=True, vmem_limit_bytes=58 * MIB
        ),
        name="back",
    )(att_w, gn_w, mid, act, slope, hidden, cot, depth_w, proj_w, gain, out_w, grads)
    return (
        block_o[None], input_o[None], hidden_o[None], depth_o, gain_o.reshape(C), proj_o, qkv_o, out_o,
    )


def solution(mesh):
    slab = P("dp", "space", None, None)
    part = P("dp", "space")
    return jax.shard_map(
        local,
        mesh=mesh,
        in_specs=(slab, slab, slab, P(), P(), P(), P(), P()),
        out_specs=(slab, slab, slab, P(), P(), part, part, part),
        check_vma=False,
    )
```

time: 635 us -> 179 us (0.28); the launches traced: 627 us -> 178 us
  waiting for transfers between devices: 274 us -> 0 us
  Pallas kernels: 0 us -> 161 us
  local copies, waits for them, and re-layouts: 126 us -> 15.1 us
  blocking collectives: 75.4 us -> 0 us
  matrix products: 64.7 us -> 0 us
  other arithmetic: 38.9 us -> 1.36 us
  starting transfers between devices: 33.1 us -> 0 us
  between operations: 14.9 us -> 0.7 us
    reduce_scatter x3 -> x0, waiting for transfers between devices: 185 us -> none  [the longest x1 93 us: local(): lax.psum_scatter(qkv_local.astype(jnp.bfloat16), 'dp', scatter_dimension=...]
    pallas_call x0 -> x3, Pallas kernels: none -> 161 us  [the longest x1 94.1 us: local(): pl.pallas_call(back_kernel, out_shape=(shape((ROWS, COLS, C)), shape((ROW...]
    unnamed x9 -> x0, waiting for transfers between devices: 78.4 us -> none
    psum x1 -> x0, blocking collectives: 75.4 us -> none  [local(): depth_grad, gain_grad = lax.psum((depth_local, gain_local), ('dp', 'space'))]
    dot_general x15 -> x0, matrix products: 64.7 us -> none  [the longest x1 11.2 us: attend_backward(): jnp.einsum('nhqk,nkhd->nqhd', grad_low, key_rows, preferred_element_type=...]
    another operation x16 -> x0, local copies, waits for them, and re-layouts: 55.2 us -> none  [the longest x10 14.5 us: depth_sum(): return jnp.stack(tap_sums)]
    all_to_all x4 -> x0, starting transfers between devices: 22.6 us -> none  [the longest x1 6.37 us: local(): lax.all_to_all(grad_att.reshape(slab_shape + (channels,)), 'space', split...]
    convert_element_type x7 -> x0, other arithmetic: 17.2 us -> none  [the longest x1 6.98 us: local(): conv_backward(grad_pad, depth_weight, slab_rows, map_cols)]
  transfers between devices with their start and end apart: 14 -> 0, of which waited for: 7 -> 0; matrix products, arithmetic and copies ran while one was open for 19% -> 0% of each run, Pallas kernels for 0% -> 0%
where the time goes in v2:
time: 179 us; the launch traced here: 178 us
  Pallas kernels  161 us (90%)
  local copies, waits for them, and re-layouts  15.1 us (8%)
    pallas_call x1, Pallas kernels, local(): pl.pallas_call(back_kernel, out_shape=(shape((ROWS, COLS, C)), shape((ROW...  94.1 us
    pallas_call x1, Pallas kernels, local(): pl.pallas_call(middle_kernel, out_shape=(shape((TOK, C)), shape((TOK, C))...  33.8 us
    pallas_call x1, Pallas kernels, local(): pl.pallas_call(front_kernel, out_shape=(shape((TOK, C)), shape((TOK, C)),...  33.2 us
    unnamed x35, local copies, waits for them, and re-layouts  14.4 us

profile of v2, /device:TPU:2, one launch (start us, length us, event | category | flops | bytes accessed | tf_op | source)
XLA Modules:
  0.0 178.2 jit_solution(1356160877940282972)
XLA Ops:
  0.6 0.7 reshape.22.gain
  1.3 1.3 copy-done
  2.6 1.1 copy-done.2
  3.7 1.1 copy-done.6
  4.7 0.8 copy-done.7
  5.5 33.2 %front.1 = (bf16[448,768]{1,0:T(8,128)(2,1)S(1)}, bf16[448,768]{1,0:T(8,128)(2,1)S(1)}, f32[448,768]{1,0:T(8,128)S(1)}, bf16[448,1536]{1,0:T(8,128)(2,1)}, f32[448,1536]{1,0:T(8,128)}) custom-call(bf16[7,56,768]{2,1,0:T(8,128)(2,1)S(1)} %bitcast.10, bf16[7,56,1536]{2,1,0:T(8,128)(2,1)S(1)} %bitcast.7, bf16[7,56,768]{2,1,0:T(8,128)(2,1)S(1)} %bitcast.9, ...), custom_call_target="tpu_custom_call" | custom-call | tf_op jit(solution)/shard_map/front/pallas_call | solution.py:661
  38.7 0.0 copy-done.8
  38.7 0.0 copy-start.3
  38.8 1.1 copy-done.3
  39.8 0.0 copy-done.1
  39.8 33.8 %middle.1 = (bf16[448,768]{1,0:T(8,128)(2,1)S(1)}, bf16[448,768]{1,0:T(8,128)(2,1)S(1)}, bf16[4,4,2,48,1536]{4,3,2,1,0:T(8,128)(2,1)}) custom-call(bf16[448,768]{1,0:T(8,128)(2,1)S(1)} %get-tuple-element.24.win_n, bf16[448,768]{1,0:T(8,128)(2,1)S(1)} %get-tuple-element.25.win_c, bf16[768,2304]{1,0:T(8,128)(2,1)} %qkv_w.1, bf16[768,768]{1,0:T(8,128)(2,1)S(1)} %copy-done.1), custom_call_target="tpu_custom_call" | custom-call | tf_op jit(solution)/shard_map/middle/pallas_call | solution.py:678
  73.6 0.8 copy-done.4
  74.5 0.9 copy-done.5
  75.3 94.1 %back.1 = (bf16[7,56,768]{2,1,0:T(8,128)(2,1)}, bf16[7,56,768]{2,1,0:T(8,128)(2,1)}, bf16[7,56,1536]{2,1,0:T(8,128)(2,1)}, f32[9,1536]{1,0:T(8,128)}, f32[1,768]...) custom-call(bf16[448,768]{1,0:T(8,128)(2,1)} %copy-done.4, bf16[448,768]{1,0:T(8,128)(2,1)} %copy-done.5, ...), custom_call_target="tpu_custom_call" | custom-call | tf_op jit(solution)/shard_map/back/pallas_call | solution.py:696
  169.4 1.4 reduce
  170.8 1.9 %copy.23 = bf16[1,7,56,768]{3,2,1,0:T(8,128)(2,1)} copy(bf16[1,7,56,768]{3,2,1,0:T(8,128)(2,1)} %bitcast.13) | data formatting | bytes 1204224
  172.7 1.9 %copy.24 = bf16[1,7,56,768]{3,2,1,0:T(8,128)(2,1)} copy(bf16[1,7,56,768]{3,2,1,0:T(8,128)(2,1)} %bitcast.12) | data formatting | bytes 1204224
  174.6 0.0 copy-start.13
  174.7 1.0 copy.25
  175.7 0.6 copy.26
  176.3 0.6 copy.27
  176.9 0.6 copy.28
  177.5 0.0 copy-done.13
  177.6 0.6 copy.29
  (16 shorter events, 0.0 us)
Async XLA Ops:
  1.3 1.3 copy-start
  2.6 1.1 copy-start.2
  3.7 1.1 copy-start.6
  4.7 0.8 copy-start.7
  5.5 33.2 %copy-start.8 = (f32[1,768]{1,0:T(1,128)}, f32[1,768]{1,0:T(1,128)S(1)}, u32[]{:S(2)}) copy-start(f32[1,768]{1,0:T(1,128)S(1)} %reshape.22.gain) | copy-start | bytes 9220
  5.5 34.3 %copy-start.1 = (bf16[768,768]{1,0:T(8,128)(2,1)S(1)}, bf16[768,768]{1,0:T(8,128)(2,1)}, u32[]{:S(2)}) copy-start(bf16[768,768]{1,0:T(8,128)(2,1)} %out_w.3) | copy-start | bytes 3538948
  38.7 1.1 copy-start.3
  73.6 0.8 copy-start.4
  74.5 0.9 copy-start.5
  169.4 5.2 %copy-start.9 = (bf16[7,56,1536]{2,1,0:T(8,128)(2,1)S(1)}, bf16[7,56,1536]{2,1,0:T(8,128)(2,1)}, u32[]{:S(2)}) copy-start(bf16[7,56,1536]{2,1,0:T(8,128)(2,1)} %get-tuple-element.34) | copy-start | bytes 3612676
  174.6 1.0 copy-start.10
  174.6 1.7 copy-start.12
  174.6 2.3 %copy-start.11 = (f32[24,288]{1,0:T(8,128)S(1)}, f32[24,288]{1,0:T(8,128)}, u32[]{:S(2)}) copy-start(f32[24,288]{1,0:T(8,128)} %get-tuple-element.54) | copy-start | bytes 82948
  174.6 2.9 %copy-start.13 = (f32[24,96]{1,0:T(8,128)S(1)}, f32[24,96]{1,0:T(8,128)}, u32[]{:S(2)}) copy-start(f32[24,96]{1,0:T(8,128)} %get-tuple-element.55) | copy-start | bytes 27652

commit v3 on v2

v3 whole, which is shorter than its diff:
```python
import jax
import jax.numpy as jnp
from jax import lax
from jax.experimental import pallas as pl
from jax.experimental.pallas import tpu as pltpu
from jax.sharding import PartitionSpec as P

MESH = pl.DeviceIdType.MESH
F32, BF16 = jnp.float32, jnp.bfloat16
EPS = 1e-05
C, E, HEADS, HD = 768, 1536, 24, 32
ROWS, COLS, PLANE = 7, 56, 64
TOK = ROWS * PLANE
WIN = 512
SCALE = HD ** (-0.5)
XORS = (2, 1, 3, 0)
NT = (((1,), (1,)), ((), ()))
TN = (((0,), (0,)), ((), ()))


def place():
    dp, sp = lax.axis_index("dp"), lax.axis_index("space")
    return dp, sp, lax.div(dp, 8), lax.rem(lax.div(dp, 2), 4), lax.rem(dp, 2)


def dp_of(x, zh, core):
    return (x * 4 + zh) * 2 + core


def greet(ids):
    barrier = pltpu.get_barrier_semaphore()
    for one in ids:
        pl.semaphore_signal(barrier, inc=1, device_id=one, device_id_type=MESH)
    pl.semaphore_wait(barrier, len(ids))


def remote(src, dst, send, recv, to):
    return pltpu.make_async_remote_copy(
        src_ref=src, dst_ref=dst, send_sem=send, recv_sem=recv, device_id=to, device_id_type=MESH
    )


def planes(ref, n):
    return ref.at[pl.ds(pl.multiple_of(n * PLANE, PLANE), PLANE)]


class Rows:
    def __init__(self, src, dst, ssem, rsem, dp, sp, out):
        self.src, self.dst, self.ssem, self.rsem = src, dst, ssem, rsem
        self.dp, self.sp, self.out = dp, sp, out

    def target(self, n):
        if self.out:
            row = self.sp * 7 + n
            return lax.rem(row, 8), lax.div(row, 8)
        row = n * 8 + self.sp
        return lax.div(row, 7), lax.rem(row, 7)

    def copies(self, n):
        to, slot = self.target(n)
        src, dst = planes(self.src, n), planes(self.dst, slot)
        far = remote(src, dst, self.ssem.at[n], self.rsem.at[slot], (self.dp, to))
        near = pltpu.make_async_copy(src, dst, self.rsem.at[slot])
        return to, far, near

    def start(self, n):
        to, far, near = self.copies(n)

        @pl.when(to != self.sp)
        def _():
            far.start()

        @pl.when(to == self.sp)
        def _():
            near.start()

    def wait_recv(self, n):
        one = planes(self.dst, n)
        pltpu.make_async_copy(one, one, self.rsem.at[n]).wait()

    def wait_send(self, n):
        to, far, _ = self.copies(n)

        @pl.when(to != self.sp)
        def _():
            far.wait_send()


class Halo:
    def __init__(self, top, bottom, halo, ssem, rsem, dp, sp):
        self.sp = sp
        self.up = remote(top, halo.at[1], ssem.at[0], rsem.at[1], (dp, jnp.maximum(sp - 1, 0)))
        self.down = remote(bottom, halo.at[0], ssem.at[1], rsem.at[0], (dp, jnp.minimum(sp + 1, 7)))
        self.halo = halo

    def start(self):
        @pl.when(self.sp > 0)
        def _():
            self.up.start()

        @pl.when(self.sp < 7)
        def _():
            self.down.start()

        zero = jnp.zeros(self.halo.shape[1:], self.halo.dtype)

        @pl.when(self.sp == 0)
        def _():
            self.halo[0] = zero

        @pl.when(self.sp == 7)
        def _():
            self.halo[1] = zero

    def wait_recv(self):
        @pl.when(self.sp > 0)
        def _():
            self.down.wait_recv()

        @pl.when(self.sp < 7)
        def _():
            self.up.wait_recv()

    def wait_send(self):
        @pl.when(self.sp > 0)
        def _():
            self.up.wait_send()

        @pl.when(self.sp < 7)
        def _():
            self.down.wait_send()


def col_masks(lanes):
    index = lax.broadcasted_iota(jnp.int32, (COLS, lanes), 0)
    return index == 0, index == COLS - 1


def later(value, first):
    return jnp.where(first, 0.0, pltpu.roll(value, 1, 0))


def earlier(value, last):
    return jnp.where(last, 0.0, pltpu.roll(value, COLS - 1, 0))


def padded(value):
    return jnp.concatenate([value, jnp.zeros((PLANE - COLS, value.shape[1]), F32)], axis=0)


def gelu_and_slope(value):
    k0, k1 = 0.7978845608028654, 0.044715
    square = value * value
    tanh = jnp.tanh(k0 * value * (1.0 + k1 * square))
    half = 0.5 * (1.0 + tanh)
    slope = half + 0.5 * value * (1.0 - tanh * tanh) * (k0 * (1.0 + 3.0 * k1 * square))
    return value * half, slope


def conv_forward(hidden, halo, taps, act, slope, begin, end):
    def chunk(n, carry):
        lanes = pl.ds(pl.multiple_of(n * 128, 128), 128)
        first, last = col_masks(128)
        rows = {}
        for r in range(begin - 1, end + 1):
            if r < 0:
                rows[r] = halo[0, :, lanes].astype(F32)
            elif r == ROWS:
                rows[r] = halo[1, :, lanes].astype(F32)
            else:
                rows[r] = hidden[r, :, lanes].astype(F32)
        tap = [taps[t : t + 1, lanes] for t in range(9)]
        for r in range(begin, end):
            part = [sum(tap[3 * a + b] * rows[r + a - 1] for a in range(3)) for b in range(3)]
            conv = later(part[0], first) + part[1] + earlier(part[2], last)
            low, grad = gelu_and_slope(conv)
            act[PLANE * r : PLANE * (r + 1), lanes] = padded(low).astype(BF16)
            slope[PLANE * r : PLANE * (r + 1), lanes] = padded(grad)
        return carry

    lax.fori_loop(0, E // 128, chunk, 0)


def normal(mid):
    mean = jnp.mean(mid, axis=1, keepdims=True)
    centred = mid - mean
    inv = lax.rsqrt(jnp.mean(centred * centred, axis=1, keepdims=True) + EPS)
    return centred * inv, inv


def window_place(index):
    win, n = index >> 6, index & 63
    g = (n * 37) >> 8
    return jnp.where(n < 49, g * PLANE + (n - 7 * g) * 8 + win, -1)


def attention(qkv, gatt, att, gqkv):
    lane = lax.broadcasted_iota(jnp.int32, (64, 128), 1) >> 5
    big = lax.broadcasted_iota(jnp.int32, (256, 128), 0) >> 6
    own = (big == (lax.broadcasted_iota(jnp.int32, (256, 128), 1) >> 5)).astype(F32).astype(BF16)
    valid = lax.broadcasted_iota(jnp.int32, (64, 256), 0) < 49

    def spread(value):
        return jnp.concatenate([value] * 4, axis=0) * own

    def gather(value):
        return jnp.where(
            lane < 2,
            jnp.where(lane == 0, value[0:64], value[64:128]),
            jnp.where(lane == 2, value[128:192], value[192:256]),
        )

    def window(w, carry):
        rows = pl.ds(pl.multiple_of(w * 64, 64), 64)
        for g in range(6):
            at = [slice(part * C + 128 * g, part * C + 128 * (g + 1)) for part in range(3)]
            query, key, value = (qkv[rows, at[part]] for part in range(3))
            query = spread(query)
            grad = spread(gatt[rows, at[0]])
            score = lax.dot_general(key, query, NT, preferred_element_type=F32) * SCALE
            score = jnp.where(valid, score, -1e30)
            power = jnp.exp(score - jnp.max(score, axis=0, keepdims=True))
            prob = power * (1.0 / jnp.sum(power, axis=0, keepdims=True))
            low = prob.astype(BF16)
            grad_prob = lax.dot_general(value, grad, NT, preferred_element_type=F32)
            inner = jnp.sum(grad_prob * prob, axis=0, keepdims=True)
            grad_low = (prob * (grad_prob - inner) * SCALE).astype(BF16)
            att[rows, at[0]] = gather(
                lax.dot_general(low, value, TN, preferred_element_type=F32)
            ).astype(BF16)
            gqkv[rows, at[0]] = gather(
                lax.dot_general(grad_low, key, TN, preferred_element_type=F32)
            ).astype(BF16)
            gqkv[rows, at[1]] = jnp.dot(grad_low, query, preferred_element_type=F32).astype(BF16)
            gqkv[rows, at[2]] = jnp.dot(low, grad, preferred_element_type=F32).astype(BF16)
        return carry

    lax.fori_loop(0, 8, window, 0)


def flip(q, mask):
    if mask == 0:
        return q
    if mask == 1:
        return q + 1 - 2 * lax.rem(q, 2)
    if mask == 3:
        return 3 - q
    return lax.rem(q + 2, 4)


class Pair:
    def __init__(self, grads, recv, total, ssem, rsem, core, peer, depth):
        self.grads, self.recv, self.dst, self.core, self.depth = grads, recv, total, core, depth
        self.ssem, self.rsem, self.peer = ssem, rsem, peer

    def copy(self, q):
        index = (q,) + (slice(None),) * self.depth + (1 - self.core,)
        return remote(
            self.grads.at[index], self.recv.at[q], self.ssem.at[q], self.rsem.at[q], self.peer
        )

    def start(self, q):
        self.copy(q).start()

    def add(self, q):
        self.copy(q).wait_recv()

        def body(i, carry):
            index = (q, lax.div(i, 4), lax.rem(i, 4)) if self.depth == 2 else (q, i)
            mine = self.grads[index + (self.core,)].astype(F32)
            self.dst[index] = (mine + self.recv[index].astype(F32)).astype(BF16)
            return carry

        lax.fori_loop(0, 4**self.depth, body, 0)

    def wait_send(self):
        for q in range(4):
            self.copy(q).wait_send()


class Halve:
    def __init__(self, src, recv, ssem, rsem, q, peers, view, piece, count):
        self.src, self.recv, self.q, self.view, self.piece, self.count = src, recv, q, view, piece, count
        self.cps = {}
        for h in range(2):
            near, far = (1, 3) if h == 0 else (3, 1)
            for slot, (block, to) in enumerate(((near, near), (2, near), (far, far))):
                n = 3 * h + slot
                self.cps[h, slot] = remote(
                    src.at[view(flip(q, block), h)], recv.at[view(slot, h)], ssem.at[n], rsem.at[n], peers[to]
                )

    def start(self):
        for slot in (1, 0):
            for h in range(2):
                self.cps[h, slot].start()

    def forward(self):
        for h in range(2):
            self.cps[h, 1].wait_recv()
            block = flip(self.q, 3 if h == 0 else 1)

            def body(i, carry, h=h, block=block):
                mine = self.src[self.piece(block, h, i)].astype(F32)
                mine = mine + self.recv[self.piece(1, h, i)].astype(F32)
                self.src[self.piece(block, h, i)] = mine.astype(BF16)
                return carry

            lax.fori_loop(0, self.count, body, 0)
            self.cps[h, 2].start()

    def finish(self, put):
        for h in range(2):
            self.cps[h, 0].wait_recv()
            self.cps[h, 2].wait_recv()

            def body(i, carry, h=h):
                mine = self.src[self.piece(self.q, h, i)].astype(F32)
                mine = mine + self.recv[self.piece(0, h, i)].astype(F32)
                put(h, i, mine + self.recv[self.piece(2, h, i)].astype(F32))
                return carry

            lax.fori_loop(0, self.count, body, 0)

    def wait_send(self):
        for cp in self.cps.values():
            cp.wait_send()


class Fan:
    def __init__(self, pieces, recvs, ssem, rsem, peers):
        self.cps = [
            remote(pieces(n), recvs(n), ssem.at[n], rsem.at[n], peer) for n, peer in enumerate(peers)
        ]

    def start(self):
        for cp in self.cps:
            cp.start()

    def wait_recv(self):
        for cp in self.cps:
            cp.wait_recv()

    def wait_send(self):
        for cp in self.cps:
            cp.wait_send()


def conv_backward(grad, halo, hidden, taps, hidden_grad, depth, begin, end):
    def chunk(n, carry):
        lanes = pl.ds(pl.multiple_of(n * 128, 128), 128)
        first, last = col_masks(128)
        rows = [halo[0, 0:COLS, lanes].astype(F32)]
        rows += [grad[PLANE * r : PLANE * r + COLS, lanes].astype(F32) for r in range(ROWS)]
        rows += [halo[1, 0:COLS, lanes].astype(F32)]
        tap = [taps[t : t + 1, lanes] for t in range(9)]
        sums = [jnp.zeros((8, 128), F32) for _ in range(9)]
        for r in range(ROWS):
            near = [rows[r + 2 - a] for a in range(3)]
            part = [sum(tap[3 * a + b] * near[a] for a in range(3)) for b in range(3)]
            total = earlier(part[0], last) + part[1] + later(part[2], first)
            hidden_grad[r, :, lanes] = total.astype(BF16)
            own = hidden[r, :, lanes].astype(F32)
            moved = [later(own, first), own, earlier(own, last)]
            for a in range(3):
                for b in range(3):
                    product = moved[b] * near[a]
                    for i in range(7):
                        sums[3 * a + b] = sums[3 * a + b] + product[8 * i : 8 * i + 8]
        for t in range(9):
            depth[t : t + 1, lanes] = jnp.sum(sums[t], axis=0, keepdims=True)
        return carry

    lax.fori_loop(begin, end, chunk, 0)


def tile(n, width=256):
    return pl.ds(pl.multiple_of(n * width, width), width)


def section_kernel(
    block_h, hidden_h, cot_h, proj_h, qkv_h, out_h, depth_w, gain,
    block_o, input_o, hidden_o, depth_o, gain_o, proj_o, qkv_o, out_o,
    block, hidden, cot, proj_w, qkv_w, out_w, loads,
    halo, taps, own_n, own_c, win_n, win_c, mid, act, slope,
    norm_p, cot_p, qkv, gatt, att_p, gqkv, turned, gn_p, wide,
    att_w, gn_w, att, gn, ig, gc, edges, depth,
    agrads, ar0, as0, ary, as1, arx, as2, arz, alast, alrecv,
    pgrads, pr0, ps0, prx, ps1, prz, ptile, precv,
    small, srecv, ssum, sall, sfinal,
    hs, hr, ns, nr, cs, cr, ts, tr, us, ur, es, er,
    a0s, a0r, ays, ayr, axs, axr, azs, azr, als, alr,
    p0s, p0r, pxs, pxr, pzs, pzr, pls, plr,
    d0s, d0r, d1s, d1r, d2s, d2r,
):
    dp, sp, x, zh, core = place()
    y, zl = lax.div(sp, 2), lax.rem(sp, 2)
    pulls = {}
    pairs = ((hidden_h, hidden), (cot_h, cot), (proj_h, proj_w), (block_h, block), (out_h, out_w), (qkv_h, qkv_w))
    for n, (src, dst) in enumerate(pairs):
        pulls[n] = pltpu.make_async_copy(src, dst, loads.at[n])
        pulls[n].start()
    pair = (dp_of(x, zh, 1 - core), sp)
    plane16 = [(dp_of(lax.rem(x + i, 4), lax.rem(zh + j, 4), core), sp) for i in range(4) for j in range(4)][1:]
    sps = [(dp, lax.rem(sp + j, 8)) for j in range(1, 8)]
    others = sps + [(dp_of(x, zh, 1 - core), lax.rem(sp + j, 8)) for j in range(8)]
    greet(plane16 + others)
    xp = {m: (dp_of(flip(x, m), zh, core), sp) for m in (1, 3)}
    zp = {m: (dp_of(x, flip(zh, m), core), sp) for m in (1, 3)}
    yp = {m: (dp, flip(y, m) * 2 + zl) for m in (1, 3)}

    edge = Halo(hidden_h.at[0], hidden_h.at[ROWS - 1], halo, hs, hr, dp, sp)
    edge.start()
    cots = Rows(own_c, win_c, cs, cr, dp, sp, True)
    norms = Rows(own_n, win_n, ns, nr, dp, sp, True)
    pulls[1].wait()
    for r in range(ROWS):
        own_c[PLANE * r : PLANE * (r + 1)] = padded(cot[r].astype(F32)).astype(BF16)
        cots.start(r)
    taps[0:9] = depth_w[...].astype(F32)
    scale = gain[...].reshape(1, C)
    pulls[0].wait()
    edge.wait_recv()
    for begin, end in ((0, 4), (4, 7)):
        conv_forward(hidden, halo, taps, act, slope, begin, end)
        if begin == 0:
            pulls[2].wait()
            pulls[3].wait()
        span = slice(PLANE * begin, PLANE * end)

        def proj(n, carry, span=span):
            mid[span, tile(n)] = jnp.dot(act[span, :], proj_w[:, tile(n)], preferred_element_type=F32)
            return carry

        lax.fori_loop(0, C // 256, proj, 0)

        def norm(r, carry):
            here = tile(r, PLANE)
            total = mid[here, :] + padded(block[r].astype(F32))
            mid[here, :] = total
            own_n[here, :] = (normal(total)[0] * scale).astype(BF16)
            norms.start(r)
            return carry

        lax.fori_loop(begin, end, norm, 0)

    index = window_place(lax.broadcasted_iota(jnp.int32, (WIN, 1), 0))
    tokens = lax.broadcasted_iota(jnp.int32, (WIN, TOK), 1)
    perm = (index == tokens).astype(F32).astype(BF16)
    for r in range(ROWS):
        cots.wait_recv(r)
    cot_p[...] = jnp.dot(perm, win_c[...], preferred_element_type=F32).astype(BF16)
    pulls[4].wait()

    def gatt_step(n, carry):
        gatt[:, tile(n)] = lax.dot_general(
            cot_p[...], out_w[tile(n), :], NT, preferred_element_type=F32
        ).astype(BF16)
        return carry

    lax.fori_loop(0, 3, gatt_step, 0)
    for r in range(ROWS):
        norms.wait_recv(r)
    norm_p[...] = jnp.dot(perm, win_n[...], preferred_element_type=F32).astype(BF16)
    pulls[5].wait()

    def qkv_step(n, carry):
        qkv[:, tile(n)] = jnp.dot(
            norm_p[...], qkv_w[:, tile(n)], preferred_element_type=F32
        ).astype(BF16)
        return carry

    lax.fori_loop(0, 9, qkv_step, 0)
    attention(qkv, gatt, att_p, gqkv)
    index = window_place(lax.broadcasted_iota(jnp.int32, (1, WIN), 1))
    tokens = lax.broadcasted_iota(jnp.int32, (TOK, WIN), 0)
    back = (index == tokens).astype(F32).astype(BF16)

    def gn_step(n, carry):
        gn_p[:, tile(n)] = lax.dot_general(
            gqkv[...], qkv_w[tile(n), :], NT, preferred_element_type=F32
        ).astype(BF16)
        return carry

    lax.fori_loop(0, 3, gn_step, 0)
    gns = Rows(gn_w, gn, us, ur, dp, sp, False)
    atts = Rows(att_w, att, ts, tr, dp, sp, False)
    gn_w[...] = jnp.dot(back, gn_p[...], preferred_element_type=F32).astype(BF16)
    for g in range(ROWS):
        gns.start(g)
    att_w[...] = jnp.dot(back, att_p[...], preferred_element_type=F32).astype(BF16)
    for g in range(ROWS):
        atts.start(g)

    apair = Pair(agrads, ar0, as0, a0s, a0r, core, pair, 2)
    ahalf = [
        Halve(as0, ary, ays, ayr, y, yp, lambda q, h: (q, slice(None), pl.ds(2 * h, 2)),
              lambda q, h, i: (q, i, pl.ds(2 * h, 2)), 4),
        Halve(as1, arx, axs, axr, x, xp, lambda q, h: (q, pl.ds(2 * h, 2)),
              lambda q, h, i: (q, 2 * h + i), 2),
        Halve(as2, arz, azs, azr, zh, zp, lambda q, h: (q, slice(None), slice(256 * h, 256 + 128 * h)),
              lambda q, h, i: (q, slice(None), slice(256 * h, 256 + 128 * h)), 1),
    ]
    for half in range(2):
        turned[...] = norm_p[...].T

        def grad_step(n, carry, half=half):
            right = gqkv[:, pl.ds(pl.multiple_of(1152 * half + 384 * n, 128), 384)]
            wide[:, tile(n, 384)] = jnp.dot(turned[...], right, preferred_element_type=F32)
            return carry

        lax.fori_loop(0, 3, grad_step, 0)
        turned[...] = att_p[...].T

        def out_grad_step(n, carry, half=half):
            right = cot_p[:, pl.ds(pl.multiple_of(384 * half + 128 * n, 128), 128)]
            wide[:, pl.ds(pl.multiple_of(1152 + 128 * n, 128), 128)] = jnp.dot(
                turned[...], right, preferred_element_type=F32
            )
            return carry

        lax.fori_loop(0, 3, out_grad_step, 0)

        def pack(xx, carry, half=half):
            rows = pl.ds(pl.multiple_of(192 * xx, 8), 192)
            for yy in range(2):
                both = []
                for low in range(2):
                    i = 2 * yy + low
                    left = wide[rows, 288 * i : 288 * (i + 1)]
                    right = wide[rows, 1152 + 96 * i : 1152 + 96 * (i + 1)]
                    both.append(jnp.concatenate([left, right], axis=1).reshape(8, 24, 384))
                value = jnp.concatenate(both, axis=1).astype(BF16)
                agrads[2 * half + yy, xx] = value.reshape(4, 2, 48, 384)
            return carry

        lax.fori_loop(0, 4, pack, 0)
        apair.start(2 * half)
        apair.start(2 * half + 1)

    for r in range(ROWS):
        gns.wait_recv(r)

    def norm_step(r, carry):
        here = tile(r, PLANE)
        hat, inv = normal(mid[here, :])
        grad = gn[here, :].astype(F32)
        grad_hat = grad * scale
        carry = carry + (grad * hat).reshape(8, 8, C).sum(axis=0)
        inner = jnp.mean(grad_hat * hat, axis=1, keepdims=True)
        mean = jnp.mean(grad_hat, axis=1, keepdims=True)
        cotangent = padded(cot[r].astype(F32))
        low = (cotangent + inv * (grad_hat - mean - hat * inner)).astype(BF16)
        ig[here, :] = low
        input_o[r] = low[0:COLS]
        return carry

    gain_part = lax.fori_loop(0, ROWS, norm_step, jnp.zeros((8, C), F32))
    gain_part = jnp.sum(gain_part, axis=0, keepdims=True)
    for m in XORS:
        apair.add(flip(y, m))
    ahalf[0].start()

    ppair = Pair(pgrads, pr0, ps0, p0s, p0r, core, pair, 1)
    phalf = [
        Halve(ps0, prx, pxs, pxr, x, xp, lambda q, h: (q, pl.ds(2 * h, 2)),
              lambda q, h, i: (q, 2 * h + i), 2),
        Halve(ps1, prz, pzs, pzr, zh, zp, lambda q, h: (q, slice(None), slice(384 * h, 384 * (h + 1))),
              lambda q, h, i: (q, slice(None), slice(384 * h, 384 * (h + 1))), 1),
    ]
    for m in XORS:
        xx = flip(x, m)
        turned[0:384, 0:TOK] = act[:, pl.ds(pl.multiple_of(xx * 384, 128), 384)].T

        def proj_step(n, carry, xx=xx):
            part = jnp.dot(turned[0:384, 0:TOK], ig[:, tile(n)], preferred_element_type=F32)
            pgrads[xx, :, :, :, tile(n)] = part.reshape(4, 2, 48, 256).astype(BF16)
            return carry

        lax.fori_loop(0, 3, proj_step, 0)
        ppair.start(xx)

    def act_step(n, carry):
        part = lax.dot_general(ig[...], proj_w[tile(n), :], NT, preferred_element_type=F32)
        gc[:, tile(n)] = (part * slope[:, tile(n)]).astype(BF16)
        return carry

    lax.fori_loop(0, E // 256, act_step, 0)
    edge2 = Halo(gc.at[0:PLANE], gc.at[TOK - PLANE : TOK], edges, es, er, dp, sp)
    edge2.start()
    for m in XORS:
        ppair.add(flip(x, m))
    phalf[0].start()
    ahalf[0].forward()
    for r in range(ROWS):
        atts.wait_recv(r)

    def out_step(n, carry):
        part = jnp.dot(att[...], out_w[:, tile(n)], preferred_element_type=F32)
        part = (part + mid[:, tile(n)]).astype(BF16)
        for r in range(ROWS):
            block_o[r, :, tile(n)] = part[PLANE * r : PLANE * r + COLS]
        return carry

    lax.fori_loop(0, C // 256, out_step, 0)
    edge2.wait_recv()
    conv_backward(gc, edges, hidden, taps, hidden_o, depth, 0, 6)
    phalf[0].forward()

    def put_as1(h, i, value):
        as1[i, pl.ds(2 * h, 2)] = value.astype(BF16)

    ahalf[0].finish(put_as1)
    ahalf[1].start()
    conv_backward(gc, edges, hidden, taps, hidden_o, depth, 6, 12)

    for n in range(12):
        small[n] = depth[0:8, 128 * n : 128 * (n + 1)]
        small[12 + n // 8, n % 8 : n % 8 + 1, :] = depth[8:9, 128 * n : 128 * (n + 1)]
    for n in range(6):
        small[13 + (4 + n) // 8, (4 + n) % 8 : (4 + n) % 8 + 1, :] = gain_part[:, 128 * n : 128 * (n + 1)]
    small[14, 2:8, :] = jnp.zeros((6, 128), F32)
    small[15] = jnp.zeros((8, 128), F32)
    shifts = [(i, j) for i in range(4) for j in range(4)][1:]

    def spot(i, j):
        return lax.rem(x + i, 4) * 4 + lax.rem(zh + j, 4)

    mine = x * 4 + zh
    scatter = Fan(lambda n: small.at[spot(*shifts[n])], lambda n: srecv.at[n], d0s, d0r, plane16)
    spread = Fan(lambda n: ssum, lambda n: sall.at[n], d1s, d1r, others)
    collect = Fan(lambda n: sfinal.at[mine], lambda n: sfinal.at[mine], d2s, d2r, plane16)
    scatter.start()

    def put_ps1(h, i, value):
        ps1[2 * h + i] = value.astype(BF16)

    phalf[0].finish(put_ps1)
    phalf[1].start()
    ahalf[1].forward()
    scatter.wait_recv()
    total = small[mine]
    for n in range(15):
        total = total + srecv[n]
    ssum[...] = total
    spread.start()
    phalf[1].forward()

    def put_as2(h, i, value):
        as2[2 * h + i] = value.astype(BF16)

    ahalf[1].finish(put_as2)
    ahalf[2].start()
    spread.wait_recv()
    total = ssum[...]
    for n in range(15):
        total = total + sall[n]
    sfinal[mine] = total
    collect.start()

    def put_tiles(h, i, value):
        for j in range(4):
            ptile[4 * h + j, :, 0:96] = value[:, 96 * j : 96 * (j + 1)].astype(BF16)

    phalf[1].finish(put_tiles)
    plast = Fan(lambda n: ptile.at[lax.rem(sp + n + 1, 8)], lambda n: precv.at[n], pls, plr, sps)
    plast.start()
    ahalf[2].forward()

    def put_last(h, i, value):
        for low in range(2):
            alast[low, :, 256 * h : 256 + 128 * h] = value[24 * low : 24 * (low + 1)]

    ahalf[2].finish(put_last)
    final = Fan(lambda n: alast.at[1 - zl], lambda n: alrecv, als, alr, [(dp, 2 * y + 1 - zl)])
    final.start()
    plast.wait_recv()
    total = ptile[sp].astype(F32)
    for n in range(7):
        total = total + precv[n].astype(F32)
    proj_o[...] = total[:, 0:96]
    final.wait_recv()
    total = alast[zl] + alrecv[...]
    qkv_o[...] = total[:, 0:288]
    out_o[...] = total[:, 288:384]
    collect.wait_recv()
    for n in range(12):
        depth_o[0:8, 128 * n : 128 * (n + 1)] = sfinal[n]
        depth_o[8:9, 128 * n : 128 * (n + 1)] = sfinal[12 + n // 8, n % 8 : n % 8 + 1, :]
    gains = [sfinal[13 + (4 + n) // 8, (4 + n) % 8 : (4 + n) % 8 + 1, :] for n in range(6)]
    gain_o[...] = jnp.concatenate(gains, axis=1).reshape(C)
    for g in range(ROWS):
        for rows in (cots, norms, gns, atts):
            rows.wait_send(g)
    for one in [edge, edge2, apair, ppair, scatter, spread, collect, plast, final] + ahalf + phalf:
        one.wait_send()


VM = pl.BlockSpec(memory_space=pltpu.VMEM)
ANY = pl.BlockSpec(memory_space=pl.ANY)
DMA = pltpu.SemaphoreType.DMA
MIB = 1024 * 1024


def shape(dims, dtype=BF16):
    return jax.ShapeDtypeStruct(dims, dtype)


def low(*dims):
    return pltpu.VMEM(dims, BF16)


def full(*dims):
    return pltpu.VMEM(dims, F32)


def local(block, hidden, cot, depth_w, proj_w, gain, qkv_w, out_w):
    scratch = [low(ROWS, COLS, C), low(ROWS, COLS, E), low(ROWS, COLS, C), low(E, C), low(C, 3 * C), low(C, C), DMA((6,))]
    scratch += [low(2, COLS, E), full(16, E)] + [low(TOK, C)] * 4 + [full(TOK, C), low(TOK, E), full(TOK, E)]
    scratch += [low(WIN, C), low(WIN, C), low(WIN, 3 * C), low(WIN, C), low(WIN, C), low(WIN, 3 * C), low(C, WIN), low(WIN, C)]
    scratch += [full(C, E)]
    scratch += [low(TOK, C)] * 5 + [low(TOK, E), low(2, PLANE, E), full(16, E)]
    scratch += [
        low(4, 4, 4, 2, 48, 384), low(4, 4, 4, 48, 384), low(4, 4, 4, 48, 384), low(3, 4, 4, 48, 384),
        low(4, 4, 48, 384), low(3, 4, 48, 384), low(4, 48, 384), low(3, 48, 384), full(2, 24, 384), full(24, 384),
    ]
    scratch += [
        low(4, 4, 2, 48, C), low(4, 4, 48, C), low(4, 4, 48, C), low(3, 4, 48, C),
        low(4, 48, C), low(3, 48, C), low(8, 48, 128), low(7, 48, 128),
    ]
    scratch += [full(16, 8, 128), full(15, 8, 128), full(8, 128), full(15, 8, 128), full(16, 8, 128)]
    counts = [2, 2, 7, 7, 7, 7, 7, 7, 7, 7, 2, 2]
    counts += [4, 4, 6, 6, 6, 6, 6, 6, 1, 1]
    counts += [4, 4, 6, 6, 6, 6, 7, 7]
    counts += [15] * 6
    scratch += [DMA((n,)) for n in counts]
    block_o, input_o, hidden_o, depth_o, gain_o, proj_o, qkv_o, out_o = pl.pallas_call(
        section_kernel,
        out_shape=(
            shape((ROWS, COLS, C)), shape((ROWS, COLS, C)), shape((ROWS, COLS, E)),
            shape((9, E), F32), shape((C,), F32),
            shape((48, 96), F32), shape((24, 288), F32), shape((24, 96), F32),
        ),
        in_specs=[ANY] * 6 + [VM] * 2,
        out_specs=(VM,) * 8,
        scratch_shapes=scratch,
        compiler_params=pltpu.CompilerParams(
            collective_id=1, has_side_effects=True, vmem_limit_bytes=63 * MIB
        ),
        name="section",
    )(block[0], hidden[0], cot[0], proj_w, qkv_w, out_w, depth_w, gain)
    return (block_o[None], input_o[None], hidden_o[None], depth_o, gain_o, proj_o, qkv_o, out_o)


def solution(mesh):
    slab = P("dp", "space", None, None)
    part = P("dp", "space")
    return jax.shard_map(
        local,
        mesh=mesh,
        in_specs=(slab, slab, slab, P(), P(), P(), P(), P()),
        out_specs=(slab, slab, slab, P(), P(), part, part, part),
        check_vma=False,
    )
```

time: 179 us -> 134 us (0.75)
  Pallas kernels: 161 us -> 124 us
  local copies, waits for them, and re-layouts: 15.1 us -> 6.98 us
    pallas_call x3 -> x1, Pallas kernels: 161 us -> 124 us  [local(): pl.pallas_call(section_kernel, out_shape=(shape((ROWS, COLS, C)), shape((...]
    unnamed x35 -> x22, local copies, waits for them, and re-layouts: 14.4 us -> 6.98 us
where the time goes in v3:
time: 134 us; the launch traced here: 132 us
  Pallas kernels  124 us (93%)
  local copies, waits for them, and re-layouts  6.98 us (5%)
    pallas_call x1, Pallas kernels, local(): pl.pallas_call(section_kernel, out_shape=(shape((ROWS, COLS, C)), shape((...  124 us
    unnamed x22, local copies, waits for them, and re-layouts  6.98 us

profile of v3, /device:TPU:2, one launch (start us, length us, event | category | flops | bytes accessed | tf_op | source)
XLA Modules:
  0.0 132.1 jit_solution(16021364568019491470)
XLA Ops:
  0.6 124.4 %section.1 = (bf16[7,56,768]{2,1,0:T(8,128)(2,1)}, bf16[7,56,768]{2,1,0:T(8,128)(2,1)}, bf16[7,56,1536]{2,1,0:T(8,128)(2,1)}, f32[9,1536]{1,0:T(8,128)}, f32[768...) custom-call(bf16[7,56,768]{2,1,0:T(8,128)(2,1)} %bitcast.10, bf16[7,56,1536]{2,1,0:T(8,128)(2,1)} %bitcast.7, ...), custom_call_target="tpu_custom_call" | custom-call | tf_op jit(solution)/shard_map/section/pallas_call | solution.py:737
  125.0 0.0 copy-start.1
  125.0 0.0 copy-start
  125.1 2.1 %copy.24 = bf16[1,7,56,768]{3,2,1,0:T(8,128)(2,1)} copy(bf16[1,7,56,768]{3,2,1,0:T(8,128)(2,1)} %bitcast.9) | data formatting | bytes 1204224
  127.1 0.0 copy-done.1
  127.1 0.8 copy.25
  127.9 0.0 copy-done
  127.9 0.0 copy-start.2
  127.9 0.0 copy-start.6
  127.9 0.0 copy-start.4
  127.9 0.0 copy-start.3
  128.0 0.0 copy-start.5
  128.0 1.0 copy.26
  129.0 0.0 copy-done.2
  129.0 0.6 copy.27
  129.6 0.0 copy-done.6
  129.6 0.6 copy.28
  130.2 0.0 copy-done.4
  130.2 0.6 copy.29
  130.8 0.0 copy-done.3
  130.8 0.6 copy.30
  131.5 0.0 copy-done.5
  131.5 0.6 copy.31
Async XLA Ops:
  125.0 2.1 %copy-start.1 = (bf16[7,56,768]{2,1,0:T(8,128)(2,1)S(1)}, bf16[7,56,768]{2,1,0:T(8,128)(2,1)}, u32[]{:S(2)}) copy-start(bf16[7,56,768]{2,1,0:T(8,128)(2,1)} %get-tuple-element.17) | copy-start | bytes 1806340
  125.0 2.9 %copy-start = (bf16[7,56,1536]{2,1,0:T(8,128)(2,1)S(1)}, bf16[7,56,1536]{2,1,0:T(8,128)(2,1)}, u32[]{:S(2)}) copy-start(bf16[7,56,1536]{2,1,0:T(8,128)(2,1)} %get-tuple-element.18) | copy-start | bytes 3612676
  127.9 1.1 copy-start.2
  127.9 1.7 %copy-start.6 = (f32[768]{0:T(1024)S(1)}, f32[768]{0:T(1024)}, u32[]{:S(2)}) copy-start(f32[768]{0:T(1024)} %get-tuple-element.36) | copy-start | bytes 9220
  127.9 2.3 %copy-start.4 = (f32[48,96]{1,0:T(8,128)S(1)}, f32[48,96]{1,0:T(8,128)}, u32[]{:S(2)}) copy-start(f32[48,96]{1,0:T(8,128)} %get-tuple-element.37) | copy-start | bytes 55300
  127.9 2.9 %copy-start.3 = (f32[24,288]{1,0:T(8,128)S(1)}, f32[24,288]{1,0:T(8,128)}, u32[]{:S(2)}) copy-start(f32[24,288]{1,0:T(8,128)} %get-tuple-element.38) | copy-start | bytes 82948
  128.0 3.5 %copy-start.5 = (f32[24,96]{1,0:T(8,128)S(1)}, f32[24,96]{1,0:T(8,128)}, u32[]{:S(2)}) copy-start(f32[24,96]{1,0:T(8,128)} %get-tuple-element.39) | copy-start | bytes 27652

commit v4 on v3

--- a/solution.py
+++ b/solution.py
@@ -194,11 +194,10 @@
     return jnp.where(n < 49, g * PLANE + (n - 7 * g) * 8 + win, -1)
 
 
-def attention(qkv, gatt, att, gqkv):
+def head_tools():
     lane = lax.broadcasted_iota(jnp.int32, (64, 128), 1) >> 5
     big = lax.broadcasted_iota(jnp.int32, (256, 128), 0) >> 6
     own = (big == (lax.broadcasted_iota(jnp.int32, (256, 128), 1) >> 5)).astype(F32).astype(BF16)
-    valid = lax.broadcasted_iota(jnp.int32, (64, 256), 0) < 49
 
     def spread(value):
         return jnp.concatenate([value] * 4, axis=0) * own
@@ -210,32 +209,64 @@
             jnp.where(lane == 2, value[128:192], value[192:256]),
         )
 
+    return spread, gather
+
+
+def heads(part, g):
+    return slice(part * C + 128 * g, part * C + 128 * (g + 1))
+
+
+def attend(qkv, probs, att):
+    spread, gather = head_tools()
+    valid = lax.broadcasted_iota(jnp.int32, (64, 256), 0) < 49
+
     def window(w, carry):
         rows = pl.ds(pl.multiple_of(w * 64, 64), 64)
         for g in range(6):
-            at = [slice(part * C + 128 * g, part * C + 128 * (g + 1)) for part in range(3)]
-            query, key, value = (qkv[rows, at[part]] for part in range(3))
-            query = spread(query)
-            grad = spread(gatt[rows, at[0]])
-            score = lax.dot_general(key, query, NT, preferred_element_type=F32) * SCALE
+            query, key, value = (qkv[rows, heads(part, g)] for part in range(3))
+            score = lax.dot_general(key, spread(query), NT, preferred_element_type=F32) * SCALE
             score = jnp.where(valid, score, -1e30)
             power = jnp.exp(score - jnp.max(score, axis=0, keepdims=True))
             prob = power * (1.0 / jnp.sum(power, axis=0, keepdims=True))
-            low = prob.astype(BF16)
-            grad_prob = lax.dot_general(value, grad, NT, preferred_element_type=F32)
-            inner = jnp.sum(grad_prob * prob, axis=0, keepdims=True)
-            grad_low = (prob * (grad_prob - inner) * SCALE).astype(BF16)
-            att[rows, at[0]] = gather(
-                lax.dot_general(low, value, TN, preferred_element_type=F32)
+            probs[g, rows] = prob
+            att[rows, heads(0, g)] = gather(
+                lax.dot_general(prob.astype(BF16), value, TN, preferred_element_type=F32)
             ).astype(BF16)
-            gqkv[rows, at[0]] = gather(
-                lax.dot_general(grad_low, key, TN, preferred_element_type=F32)
-            ).astype(BF16)
-            gqkv[rows, at[1]] = jnp.dot(grad_low, query, preferred_element_type=F32).astype(BF16)
-            gqkv[rows, at[2]] = jnp.dot(low, grad, preferred_element_type=F32).astype(BF16)
         return carry
 
     lax.fori_loop(0, 8, window, 0)
+
+
+def attend_back(qkv, gatt, probs, gqkv, groups):
+    spread, gather = head_tools()
+
+    def window(pair, carry):
+        for w in range(2):
+            rows = pl.ds(pl.multiple_of(pair * 128 + 64 * w, 64), 64)
+            for g in groups:
+                query, key, value = (qkv[rows, heads(part, g)] for part in range(3))
+                query = spread(query)
+                grad = spread(gatt[rows, heads(0, g)])
+                prob = probs[g, rows]
+                low = prob.astype(BF16)
+                grad_prob = lax.dot_general(value, grad, NT, preferred_element_type=F32)
+                inner = jnp.sum(grad_prob * prob, axis=0, keepdims=True)
+                grad_low = (prob * (grad_prob - inner) * SCALE).astype(BF16)
+                gqkv[rows, heads(0, g)] = gather(
+                    lax.dot_general(grad_low, key, TN, preferred_element_type=F32)
+                ).astype(BF16)
+                gqkv[rows, heads(1, g)] = jnp.dot(
+                    grad_low, query, preferred_element_type=F32
+                ).astype(BF16)
+                gqkv[rows, heads(2, g)] = jnp.dot(low, grad, preferred_element_type=F32).astype(BF16)
+        return carry
+
+    lax.fori_loop(0, 4, window, 0)
+
+
+def half_rows(value):
+    left, right = (value[:, 128 * h : 128 * (h + 1)].reshape(32, 24, 128) for h in range(2))
+    return jnp.concatenate([left, right], axis=1).reshape(4, 4, 2, 48, 128).astype(BF16)
 
 
 def flip(q, mask):
@@ -249,33 +280,51 @@
 
 
 class Pair:
-    def __init__(self, grads, recv, total, ssem, rsem, core, peer, depth):
-        self.grads, self.recv, self.dst, self.core, self.depth = grads, recv, total, core, depth
+    def __init__(self, grads, recv, ssem, rsem, core, peer):
+        self.grads, self.recv, self.core = grads, recv, core
         self.ssem, self.rsem, self.peer = ssem, rsem, peer
+        self.begun = []
 
     def copy(self, q):
-        index = (q,) + (slice(None),) * self.depth + (1 - self.core,)
         return remote(
-            self.grads.at[index], self.recv.at[q], self.ssem.at[q], self.rsem.at[q], self.peer
+            self.grads.at[q, :, 1 - self.core], self.recv.at[q], self.ssem.at[q], self.rsem.at[q], self.peer
         )
 
     def start(self, q):
         self.copy(q).start()
 
-    def add(self, q):
+    def add(self, q, put):
         self.copy(q).wait_recv()
 
         def body(i, carry):
-            index = (q, lax.div(i, 4), lax.rem(i, 4)) if self.depth == 2 else (q, i)
-            mine = self.grads[index + (self.core,)].astype(F32)
-            self.dst[index] = (mine + self.recv[index].astype(F32)).astype(BF16)
+            mine = self.grads[q, i, self.core].astype(F32)
+            put(q, i, (mine + self.recv[q, i].astype(F32)).astype(BF16))
             return carry
 
-        lax.fori_loop(0, 4**self.depth, body, 0)
+        lax.fori_loop(0, 4, body, 0)
 
     def wait_send(self):
         for q in range(4):
             self.copy(q).wait_send()
+
+
+class Whole(Pair):
+    def copy(self, q=0):
+        return remote(self.grads.at[:, :, 1 - self.core], self.recv, self.ssem, self.rsem, self.peer)
+
+    def add(self, put):
+        self.copy().wait_recv()
+
+        def body(i, carry):
+            q, j = lax.div(i, 4), lax.rem(i, 4)
+            mine = self.grads[q, j, self.core].astype(F32)
+            put(q, j, (mine + self.recv[q, j].astype(F32)).astype(BF16))
+            return carry
+
+        lax.fori_loop(0, 16, body, 0)
+
+    def wait_send(self):
+        self.copy().wait_send()
 
 
 class Halve:
@@ -383,18 +432,17 @@
     block_o, input_o, hidden_o, depth_o, gain_o, proj_o, qkv_o, out_o,
     block, hidden, cot, proj_w, qkv_w, out_w, loads,
     halo, taps, own_n, own_c, win_n, win_c, mid, act, slope,
-    norm_p, cot_p, qkv, gatt, att_p, gqkv, turned, gn_p, wide,
+    norm_p, cot_p, qkv, gatt, att_p, gqkv, turned, turned2, gn_p, probs,
     att_w, gn_w, att, gn, ig, gc, edges, depth,
-    agrads, ar0, as0, ary, as1, arx, as2, arz, alast, alrecv,
-    pgrads, pr0, ps0, prx, ps1, prz, ptile, precv,
+    agrads, ar0, as0, arx, as1, arz, atot, arow, atile, arecv,
+    pgrads, pr0, ps0, prx, ps1, prz, qs0, qrz, qs1, qrx, ptot, ptile, precv,
     small, srecv, ssum, sall, sfinal,
     hs, hr, ns, nr, cs, cr, ts, tr, us, ur, es, er,
-    a0s, a0r, ays, ayr, axs, axr, azs, azr, als, alr,
-    p0s, p0r, pxs, pxr, pzs, pzr, pls, plr,
+    a0s, a0r, axs, axr, azs, azr, als, alr,
+    p0s, p0r, pxs, pxr, pzs, pzr, qzs, qzr, qxs, qxr, pls, plr,
     d0s, d0r, d1s, d1r, d2s, d2r,
 ):
     dp, sp, x, zh, core = place()
-    y, zl = lax.div(sp, 2), lax.rem(sp, 2)
     pulls = {}
     pairs = ((hidden_h, hidden), (cot_h, cot), (proj_h, proj_w), (block_h, block), (out_h, out_w), (qkv_h, qkv_w))
     for n, (src, dst) in enumerate(pairs):
@@ -407,7 +455,6 @@
     greet(plane16 + others)
     xp = {m: (dp_of(flip(x, m), zh, core), sp) for m in (1, 3)}
     zp = {m: (dp_of(x, flip(zh, m), core), sp) for m in (1, 3)}
-    yp = {m: (dp, flip(y, m) * 2 + zl) for m in (1, 3)}
 
     edge = Halo(hidden_h.at[0], hidden_h.at[ROWS - 1], halo, hs, hr, dp, sp)
     edge.start()
@@ -471,72 +518,116 @@
         return carry
 
     lax.fori_loop(0, 9, qkv_step, 0)
-    attention(qkv, gatt, att_p, gqkv)
+    turned[...] = norm_p[...].T
+    attend(qkv, probs, att_p)
+
+    ring = lambda q, h: (q, pl.ds(2 * h, 2))
+    ring_piece = lambda q, h, i: (q, 2 * h + i)
+    line = lambda q, h: (q, slice(None), slice(256 * h, 256 + 128 * h))
+    line_piece = lambda q, h, i: line(q, h)
+
+    class Chunk:
+        def __init__(self, c):
+            self.c = c
+            self.pair = Whole(agrads.at[c], ar0.at[c], a0s.at[c], a0r.at[c], core, pair)
+            six = pl.ds(6 * c, 6)
+            self.first = Halve(
+                as0.at[c], arx.at[c], axs.at[six], axr.at[six], x, xp, ring, ring_piece, 2
+            )
+            self.second = Halve(
+                as1.at[c], arz.at[c], azs.at[six], azr.at[six], zh, zp, line, line_piece, 1
+            )
+
+        def put0(self, q, i, value):
+            as0[self.c, q, i] = value
+
+        def put1(self, h, i, value):
+            as1[self.c, 2 * h + i] = value.astype(BF16)
+
+        def put2(self, h, i, value):
+            atot[self.c, :, 256 * h : 256 + 128 * h] = value
+
+        def step(self, n):
+            if n == 0:
+                self.pair.start(0)
+            elif n == 1:
+                self.pair.add(self.put0)
+                self.first.start()
+            elif n == 2:
+                self.first.forward()
+            elif n == 3:
+                self.first.finish(self.put1)
+                self.second.start()
+            elif n == 4:
+                self.second.forward()
+            elif n == 5:
+                self.second.finish(self.put2)
+
+        def wait_send(self):
+            for one in (self.pair, self.first, self.second):
+                one.wait_send()
+
+    chunks = [Chunk(c) for c in range(4)]
+
+    def advance(slot):
+        for c in range(4):
+            if 0 <= slot - c <= 5:
+                chunks[c].step(slot - c)
+
+    turned2[...] = att_p[...].T
+
+    def out_grad_step(n, carry):
+        right = jnp.concatenate([cot_p[:, tile(n, 128)], cot_p[:, tile(n + 3, 128)]], axis=1)
+        agrads[0, :, :, :, :, tile(n, 128)] = half_rows(
+            jnp.dot(turned2[...], right, preferred_element_type=F32)
+        )
+        return carry
+
+    lax.fori_loop(0, 3, out_grad_step, 0)
+    advance(0)
     index = window_place(lax.broadcasted_iota(jnp.int32, (1, WIN), 1))
     tokens = lax.broadcasted_iota(jnp.int32, (TOK, WIN), 0)
     back = (index == tokens).astype(F32).astype(BF16)
-
-    def gn_step(n, carry):
-        gn_p[:, tile(n)] = lax.dot_general(
-            gqkv[...], qkv_w[tile(n), :], NT, preferred_element_type=F32
-        ).astype(BF16)
-        return carry
-
-    lax.fori_loop(0, 3, gn_step, 0)
     gns = Rows(gn_w, gn, us, ur, dp, sp, False)
     atts = Rows(att_w, att, ts, tr, dp, sp, False)
-    gn_w[...] = jnp.dot(back, gn_p[...], preferred_element_type=F32).astype(BF16)
-    for g in range(ROWS):
-        gns.start(g)
     att_w[...] = jnp.dot(back, att_p[...], preferred_element_type=F32).astype(BF16)
     for g in range(ROWS):
         atts.start(g)
-
-    apair = Pair(agrads, ar0, as0, a0s, a0r, core, pair, 2)
-    ahalf = [
-        Halve(as0, ary, ays, ayr, y, yp, lambda q, h: (q, slice(None), pl.ds(2 * h, 2)),
-              lambda q, h, i: (q, i, pl.ds(2 * h, 2)), 4),
-        Halve(as1, arx, axs, axr, x, xp, lambda q, h: (q, pl.ds(2 * h, 2)),
-              lambda q, h, i: (q, 2 * h + i), 2),
-        Halve(as2, arz, azs, azr, zh, zp, lambda q, h: (q, slice(None), slice(256 * h, 256 + 128 * h)),
-              lambda q, h, i: (q, slice(None), slice(256 * h, 256 + 128 * h)), 1),
-    ]
-    for half in range(2):
-        turned[...] = norm_p[...].T
-
-        def grad_step(n, carry, half=half):
-            right = gqkv[:, pl.ds(pl.multiple_of(1152 * half + 384 * n, 128), 384)]
-            wide[:, tile(n, 384)] = jnp.dot(turned[...], right, preferred_element_type=F32)
-            return carry
-
-        lax.fori_loop(0, 3, grad_step, 0)
-        turned[...] = att_p[...].T
-
-        def out_grad_step(n, carry, half=half):
-            right = cot_p[:, pl.ds(pl.multiple_of(384 * half + 128 * n, 128), 128)]
-            wide[:, pl.ds(pl.multiple_of(1152 + 128 * n, 128), 128)] = jnp.dot(
-                turned[...], right, preferred_element_type=F32
+    for c in range(1, 4):
+        attend_back(qkv, gatt, probs, gqkv, (2 * c - 2, 2 * c - 1))
+        if c == 3:
+
+            def gn_step(n, carry):
+                gn_p[:, tile(n)] = lax.dot_general(
+                    gqkv[...], qkv_w[tile(n), :], NT, preferred_element_type=F32
+                ).astype(BF16)
+                return carry
+
+            lax.fori_loop(0, 3, gn_step, 0)
+            gn_w[...] = jnp.dot(back, gn_p[...], preferred_element_type=F32).astype(BF16)
+            for g in range(ROWS):
+                gns.start(g)
+
+        def grad_step(n, carry, c=c):
+            right = gqkv[:, pl.ds(pl.multiple_of(768 * n + 256 * (c - 1), 256), 256)]
+            agrads[c, :, :, :, :, tile(n, 128)] = half_rows(
+                jnp.dot(turned[...], right, preferred_element_type=F32)
             )
             return carry
 
-        lax.fori_loop(0, 3, out_grad_step, 0)
-
-        def pack(xx, carry, half=half):
-            rows = pl.ds(pl.multiple_of(192 * xx, 8), 192)
-            for yy in range(2):
-                both = []
-                for low in range(2):
-                    i = 2 * yy + low
-                    left = wide[rows, 288 * i : 288 * (i + 1)]
-                    right = wide[rows, 1152 + 96 * i : 1152 + 96 * (i + 1)]
-                    both.append(jnp.concatenate([left, right], axis=1).reshape(8, 24, 384))
-                value = jnp.concatenate(both, axis=1).astype(BF16)
-                agrads[2 * half + yy, xx] = value.reshape(4, 2, 48, 384)
-            return carry
-
-        lax.fori_loop(0, 4, pack, 0)
-        apair.start(2 * half)
-        apair.start(2 * half + 1)
+        lax.fori_loop(0, 3, grad_step, 0)
+        advance(c)
+    for r in range(ROWS):
+        atts.wait_recv(r)
+
+    def out_step(n, carry):
+        part = jnp.dot(att[...], out_w[:, tile(n)], preferred_element_type=F32)
+        part = (part + mid[:, tile(n)]).astype(BF16)
+        for r in range(ROWS):
+            block_o[r, :, tile(n)] = part[PLANE * r : PLANE * r + COLS]
+        return carry
+
+    lax.fori_loop(0, C // 256, out_step, 0)
 
     for r in range(ROWS):
         gns.wait_recv(r)
@@ -557,28 +648,47 @@
 
     gain_part = lax.fori_loop(0, ROWS, norm_step, jnp.zeros((8, C), F32))
     gain_part = jnp.sum(gain_part, axis=0, keepdims=True)
-    for m in XORS:
-        apair.add(flip(y, m))
-    ahalf[0].start()
-
-    ppair = Pair(pgrads, pr0, ps0, p0s, p0r, core, pair, 1)
-    phalf = [
-        Halve(ps0, prx, pxs, pxr, x, xp, lambda q, h: (q, pl.ds(2 * h, 2)),
-              lambda q, h, i: (q, 2 * h + i), 2),
-        Halve(ps1, prz, pzs, pzr, zh, zp, lambda q, h: (q, slice(None), slice(384 * h, 384 * (h + 1))),
-              lambda q, h, i: (q, slice(None), slice(384 * h, 384 * (h + 1))), 1),
-    ]
+    advance(4)
+
+    ppair = Pair(pgrads, pr0, p0s, p0r, core, pair)
+    ends = lambda width: (
+        lambda q, h: (q, slice(None), slice(width * h, width * (h + 1))),
+        lambda q, h, i: (q, slice(None), slice(width * h, width * (h + 1))),
+    )
+    px = Halve(ps0, prx, pxs, pxr, x, xp, ring, ring_piece, 2)
+    pz = Halve(ps1, prz, pzs, pzr, zh, zp, *ends(256), 1)
+    qz = Halve(qs0, qrz, qzs, qzr, zh, zp, ring, ring_piece, 2)
+    qx = Halve(qs1, qrx, qxs, qxr, x, xp, *ends(128), 1)
+
+    def put_p0(q, i, value):
+        ps0[q, i] = value[:, 0:512]
+        qs0[i, q] = value[:, 512:768]
+
+    def put_ps1(h, i, value):
+        ps1[2 * h + i] = value.astype(BF16)
+
+    def put_qs1(h, i, value):
+        qs1[2 * h + i] = value.astype(BF16)
+
+    def put_p2(h, i, value):
+        ptot[:, 256 * h : 256 * (h + 1)] = value
+
+    def put_q2(h, i, value):
+        ptot[:, 512 + 128 * h : 512 + 128 * (h + 1)] = value
+
     for m in XORS:
         xx = flip(x, m)
-        turned[0:384, 0:TOK] = act[:, pl.ds(pl.multiple_of(xx * 384, 128), 384)].T
+        turned2[0:384, 0:TOK] = act[:, pl.ds(pl.multiple_of(xx * 384, 128), 384)].T
 
         def proj_step(n, carry, xx=xx):
-            part = jnp.dot(turned[0:384, 0:TOK], ig[:, tile(n)], preferred_element_type=F32)
+            part = jnp.dot(turned2[0:384, 0:TOK], ig[:, tile(n)], preferred_element_type=F32)
             pgrads[xx, :, :, :, tile(n)] = part.reshape(4, 2, 48, 256).astype(BF16)
             return carry
 
         lax.fori_loop(0, 3, proj_step, 0)
         ppair.start(xx)
+
+    advance(5)
 
     def act_step(n, carry):
         part = lax.dot_general(ig[...], proj_w[tile(n), :], NT, preferred_element_type=F32)
@@ -589,29 +699,15 @@
     edge2 = Halo(gc.at[0:PLANE], gc.at[TOK - PLANE : TOK], edges, es, er, dp, sp)
     edge2.start()
     for m in XORS:
-        ppair.add(flip(x, m))
-    phalf[0].start()
-    ahalf[0].forward()
-    for r in range(ROWS):
-        atts.wait_recv(r)
-
-    def out_step(n, carry):
-        part = jnp.dot(att[...], out_w[:, tile(n)], preferred_element_type=F32)
-        part = (part + mid[:, tile(n)]).astype(BF16)
-        for r in range(ROWS):
-            block_o[r, :, tile(n)] = part[PLANE * r : PLANE * r + COLS]
-        return carry
-
-    lax.fori_loop(0, C // 256, out_step, 0)
+        ppair.add(flip(x, m), put_p0)
+    px.start()
+    qz.start()
+    advance(6)
     edge2.wait_recv()
     conv_backward(gc, edges, hidden, taps, hidden_o, depth, 0, 6)
-    phalf[0].forward()
-
-    def put_as1(h, i, value):
-        as1[i, pl.ds(2 * h, 2)] = value.astype(BF16)
-
-    ahalf[0].finish(put_as1)
-    ahalf[1].start()
+    px.forward()
+    qz.forward()
+    advance(7)
     conv_backward(gc, edges, hidden, taps, hidden_o, depth, 6, 12)
 
     for n in range(12):
@@ -631,68 +727,67 @@
     spread = Fan(lambda n: ssum, lambda n: sall.at[n], d1s, d1r, others)
     collect = Fan(lambda n: sfinal.at[mine], lambda n: sfinal.at[mine], d2s, d2r, plane16)
     scatter.start()
-
-    def put_ps1(h, i, value):
-        ps1[2 * h + i] = value.astype(BF16)
-
-    phalf[0].finish(put_ps1)
-    phalf[1].start()
-    ahalf[1].forward()
+    px.finish(put_ps1)
+    pz.start()
+    qz.finish(put_qs1)
+    qx.start()
+    advance(8)
+    for hh in range(2):
+        rows = slice(24 * hh, 24 * (hh + 1))
+        arow[:, 2304 + 384 * hh : 2304 + 384 * (hh + 1)] = atot[0, rows, :]
+        for c in range(1, 4):
+            for part in range(3):
+                begin = C * part + 256 * (c - 1) + 128 * hh
+                arow[:, begin : begin + 128] = atot[c, rows, 128 * part : 128 * (part + 1)]
+    blank = jnp.zeros((8, 384), F32)
+    for j in range(8):
+        left = arow[:, 288 * j : 288 * (j + 1)]
+        right = arow[:, 2304 + 96 * j : 2304 + 96 * (j + 1)]
+        value = jnp.concatenate([jnp.concatenate([left, right], axis=1), blank], axis=0)
+        atile[j] = value.astype(BF16)
+    alast = Fan(lambda n: atile.at[lax.rem(sp + n + 1, 8)], lambda n: arecv.at[n], als, alr, sps)
+    alast.start()
     scatter.wait_recv()
     total = small[mine]
     for n in range(15):
         total = total + srecv[n]
     ssum[...] = total
     spread.start()
-    phalf[1].forward()
-
-    def put_as2(h, i, value):
-        as2[2 * h + i] = value.astype(BF16)
-
-    ahalf[1].finish(put_as2)
-    ahalf[2].start()
+    pz.forward()
+    qx.forward()
     spread.wait_recv()
     total = ssum[...]
     for n in range(15):
         total = total + sall[n]
     sfinal[mine] = total
     collect.start()
-
-    def put_tiles(h, i, value):
-        for j in range(4):
-            ptile[4 * h + j, :, 0:96] = value[:, 96 * j : 96 * (j + 1)].astype(BF16)
-
-    phalf[1].finish(put_tiles)
+    qx.finish(put_q2)
+    pz.finish(put_p2)
+    for j in range(8):
+        ptile[j, :, 0:96] = ptot[:, 96 * j : 96 * (j + 1)].astype(BF16)
     plast = Fan(lambda n: ptile.at[lax.rem(sp + n + 1, 8)], lambda n: precv.at[n], pls, plr, sps)
     plast.start()
-    ahalf[2].forward()
-
-    def put_last(h, i, value):
-        for low in range(2):
-            alast[low, :, 256 * h : 256 + 128 * h] = value[24 * low : 24 * (low + 1)]
-
-    ahalf[2].finish(put_last)
-    final = Fan(lambda n: alast.at[1 - zl], lambda n: alrecv, als, alr, [(dp, 2 * y + 1 - zl)])
-    final.start()
-    plast.wait_recv()
-    total = ptile[sp].astype(F32)
+    alast.wait_recv()
+    total = atile[sp].astype(F32)
     for n in range(7):
-        total = total + precv[n].astype(F32)
-    proj_o[...] = total[:, 0:96]
-    final.wait_recv()
-    total = alast[zl] + alrecv[...]
-    qkv_o[...] = total[:, 0:288]
-    out_o[...] = total[:, 288:384]
+        total = total + arecv[n].astype(F32)
+    qkv_o[...] = total[0:24, 0:288]
+    out_o[...] = total[0:24, 288:384]
     collect.wait_recv()
     for n in range(12):
         depth_o[0:8, 128 * n : 128 * (n + 1)] = sfinal[n]
         depth_o[8:9, 128 * n : 128 * (n + 1)] = sfinal[12 + n // 8, n % 8 : n % 8 + 1, :]
     gains = [sfinal[13 + (4 + n) // 8, (4 + n) % 8 : (4 + n) % 8 + 1, :] for n in range(6)]
     gain_o[...] = jnp.concatenate(gains, axis=1).reshape(C)
+    plast.wait_recv()
+    total = ptile[sp].astype(F32)
+    for n in range(7):
+        total = total + precv[n].astype(F32)
+    proj_o[...] = total[:, 0:96]
     for g in range(ROWS):
         for rows in (cots, norms, gns, atts):
             rows.wait_send(g)
-    for one in [edge, edge2, apair, ppair, scatter, spread, collect, plast, final] + ahalf + phalf:
+    for one in [edge, edge2, ppair, px, pz, qx, qz, scatter, spread, collect, plast, alast] + chunks:
         one.wait_send()
 
 
@@ -717,21 +812,22 @@
 def local(block, hidden, cot, depth_w, proj_w, gain, qkv_w, out_w):
     scratch = [low(ROWS, COLS, C), low(ROWS, COLS, E), low(ROWS, COLS, C), low(E, C), low(C, 3 * C), low(C, C), DMA((6,))]
     scratch += [low(2, COLS, E), full(16, E)] + [low(TOK, C)] * 4 + [full(TOK, C), low(TOK, E), full(TOK, E)]
-    scratch += [low(WIN, C), low(WIN, C), low(WIN, 3 * C), low(WIN, C), low(WIN, C), low(WIN, 3 * C), low(C, WIN), low(WIN, C)]
-    scratch += [full(C, E)]
+    scratch += [low(WIN, C), low(WIN, C), low(WIN, 3 * C), low(WIN, C), low(WIN, C), low(WIN, 3 * C), low(C, WIN), low(C, WIN), low(WIN, C)]
+    scratch += [full(6, WIN, 256)]
     scratch += [low(TOK, C)] * 5 + [low(TOK, E), low(2, PLANE, E), full(16, E)]
     scratch += [
-        low(4, 4, 4, 2, 48, 384), low(4, 4, 4, 48, 384), low(4, 4, 4, 48, 384), low(3, 4, 4, 48, 384),
-        low(4, 4, 48, 384), low(3, 4, 48, 384), low(4, 48, 384), low(3, 48, 384), full(2, 24, 384), full(24, 384),
+        low(4, 4, 4, 2, 48, 384), low(4, 4, 4, 48, 384), low(4, 4, 4, 48, 384), low(4, 3, 4, 48, 384),
+        low(4, 4, 48, 384), low(4, 3, 48, 384), full(4, 48, 384), full(24, 4 * C), low(8, 32, 384), low(7, 32, 384),
     ]
     scratch += [
-        low(4, 4, 2, 48, C), low(4, 4, 48, C), low(4, 4, 48, C), low(3, 4, 48, C),
-        low(4, 48, C), low(3, 48, C), low(8, 48, 128), low(7, 48, 128),
+        low(4, 4, 2, 48, C), low(4, 4, 48, C), low(4, 4, 48, 512), low(3, 4, 48, 512), low(4, 48, 512), low(3, 48, 512),
+        low(4, 4, 48, 256), low(3, 4, 48, 256), low(4, 48, 256), low(3, 48, 256),
+        full(48, C), low(8, 48, 128), low(7, 48, 128),
     ]
     scratch += [full(16, 8, 128), full(15, 8, 128), full(8, 128), full(15, 8, 128), full(16, 8, 128)]
     counts = [2, 2, 7, 7, 7, 7, 7, 7, 7, 7, 2, 2]
-    counts += [4, 4, 6, 6, 6, 6, 6, 6, 1, 1]
-    counts += [4, 4, 6, 6, 6, 6, 7, 7]
+    counts += [4, 4, 24, 24, 24, 24, 7, 7]
+    counts += [4, 4, 6, 6, 6, 6, 6, 6, 6, 6, 7, 7]
     counts += [15] * 6
     scratch += [DMA((n,)) for n in counts]
     block_o, input_o, hidden_o, depth_o, gain_o, proj_o, qkv_o, out_o = pl.pallas_call(

time: 134 us -> 137 us (1.022)
  Pallas kernels: 124 us -> 128 us
    pallas_call x1, Pallas kernels: 124 us -> 128 us  [local(): pl.pallas_call(section_kernel, out_shape=(shape((ROWS, COLS, C)), shape((...]
where the time goes in v4:
time: 137 us; the launch traced here: 136 us
  Pallas kernels  128 us (93%)
  local copies, waits for them, and re-layouts  6.98 us (5%)
    pallas_call x1, Pallas kernels, local(): pl.pallas_call(section_kernel, out_shape=(shape((ROWS, COLS, C)), shape((...  128 us
    unnamed x22, local copies, waits for them, and re-layouts  6.98 us

profile of v4, /device:TPU:2, one launch (start us, length us, event | category | flops | bytes accessed | tf_op | source)
XLA Modules:
  0.0 136.1 jit_solution(237894466997940060)
XLA Ops:
  0.6 128.5 %section.1 = (bf16[7,56,768]{2,1,0:T(8,128)(2,1)}, bf16[7,56,768]{2,1,0:T(8,128)(2,1)}, bf16[7,56,1536]{2,1,0:T(8,128)(2,1)}, f32[9,1536]{1,0:T(8,128)}, f32[768...) custom-call(bf16[7,56,768]{2,1,0:T(8,128)(2,1)} %bitcast.10, bf16[7,56,1536]{2,1,0:T(8,128)(2,1)} %bitcast.7, ...), custom_call_target="tpu_custom_call" | custom-call | tf_op jit(solution)/shard_map/section/pallas_call | solution.py:833
  129.1 0.0 copy-start.1
  129.1 0.0 copy-start
  129.1 2.1 %copy.24 = bf16[1,7,56,768]{3,2,1,0:T(8,128)(2,1)} copy(bf16[1,7,56,768]{3,2,1,0:T(8,128)(2,1)} %bitcast.9) | data formatting | bytes 1204224
  131.2 0.0 copy-done.1
  131.2 0.8 copy.25
  132.0 0.0 copy-done
  132.0 0.0 copy-start.2
  132.0 0.0 copy-start.6
  132.0 0.0 copy-start.4
  132.0 0.0 copy-start.3
  132.0 0.0 copy-start.5
  132.0 1.0 copy.26
  133.1 0.0 copy-done.2
  133.1 0.6 copy.27
  133.7 0.0 copy-done.6
  133.7 0.6 copy.28
  134.3 0.0 copy-done.4
  134.3 0.6 copy.29
  134.9 0.0 copy-done.3
  134.9 0.6 copy.30
  135.5 0.0 copy-done.5
  135.5 0.6 copy.31
Async XLA Ops:
  129.1 2.1 %copy-start.1 = (bf16[7,56,768]{2,1,0:T(8,128)(2,1)S(1)}, bf16[7,56,768]{2,1,0:T(8,128)(2,1)}, u32[]{:S(2)}) copy-start(bf16[7,56,768]{2,1,0:T(8,128)(2,1)} %get-tuple-element.17) | copy-start | bytes 1806340
  129.1 2.9 %copy-start = (bf16[7,56,1536]{2,1,0:T(8,128)(2,1)S(1)}, bf16[7,56,1536]{2,1,0:T(8,128)(2,1)}, u32[]{:S(2)}) copy-start(bf16[7,56,1536]{2,1,0:T(8,128)(2,1)} %get-tuple-element.18) | copy-start | bytes 3612676
  132.0 1.1 copy-start.2
  132.0 1.7 %copy-start.6 = (f32[768]{0:T(1024)S(1)}, f32[768]{0:T(1024)}, u32[]{:S(2)}) copy-start(f32[768]{0:T(1024)} %get-tuple-element.36) | copy-start | bytes 9220
  132.0 2.3 %copy-start.4 = (f32[48,96]{1,0:T(8,128)S(1)}, f32[48,96]{1,0:T(8,128)}, u32[]{:S(2)}) copy-start(f32[48,96]{1,0:T(8,128)} %get-tuple-element.37) | copy-start | bytes 55300
  132.0 2.9 %copy-start.3 = (f32[24,288]{1,0:T(8,128)S(1)}, f32[24,288]{1,0:T(8,128)}, u32[]{:S(2)}) copy-start(f32[24,288]{1,0:T(8,128)} %get-tuple-element.38) | copy-start | bytes 82948
  132.0 3.5 %copy-start.5 = (f32[24,96]{1,0:T(8,128)S(1)}, f32[24,96]{1,0:T(8,128)}, u32[]{:S(2)}) copy-start(f32[24,96]{1,0:T(8,128)} %get-tuple-element.39) | copy-start | bytes 27652

commit v5 on v4

--- a/solution.py
+++ b/solution.py
@@ -395,7 +395,34 @@
             cp.wait_send()
 
 
-def conv_backward(grad, halo, hidden, taps, hidden_grad, depth, begin, end):
+def depth_sums(grad, halo, hidden, depth):
+    def chunk(n, carry):
+        lanes = pl.ds(pl.multiple_of(n * 128, 128), 128)
+        first, last = col_masks(128)
+        rows = [grad[PLANE * r : PLANE * r + COLS, lanes].astype(F32) for r in range(ROWS)]
+        sums = [jnp.zeros((8, 128), F32) for _ in range(9)]
+        for r in range(-1, ROWS + 1):
+            if r < 0:
+                own = halo[0, :, lanes].astype(F32)
+            elif r == ROWS:
+                own = halo[1, :, lanes].astype(F32)
+            else:
+                own = hidden[r, :, lanes].astype(F32)
+            moved = [later(own, first), own, earlier(own, last)]
+            for a in range(3):
+                if 0 <= r + 1 - a < ROWS:
+                    for b in range(3):
+                        product = moved[b] * rows[r + 1 - a]
+                        for i in range(7):
+                            sums[3 * a + b] = sums[3 * a + b] + product[8 * i : 8 * i + 8]
+        for t in range(9):
+            depth[t : t + 1, lanes] = jnp.sum(sums[t], axis=0, keepdims=True)
+        return carry
+
+    lax.fori_loop(0, E // 128, chunk, 0)
+
+
+def conv_backward(grad, halo, taps, hidden_grad, begin, end):
     def chunk(n, carry):
         lanes = pl.ds(pl.multiple_of(n * 128, 128), 128)
         first, last = col_masks(128)
@@ -403,24 +430,24 @@
         rows += [grad[PLANE * r : PLANE * r + COLS, lanes].astype(F32) for r in range(ROWS)]
         rows += [halo[1, 0:COLS, lanes].astype(F32)]
         tap = [taps[t : t + 1, lanes] for t in range(9)]
-        sums = [jnp.zeros((8, 128), F32) for _ in range(9)]
         for r in range(ROWS):
-            near = [rows[r + 2 - a] for a in range(3)]
-            part = [sum(tap[3 * a + b] * near[a] for a in range(3)) for b in range(3)]
+            part = [sum(tap[3 * a + b] * rows[r + 2 - a] for a in range(3)) for b in range(3)]
             total = earlier(part[0], last) + part[1] + later(part[2], first)
             hidden_grad[r, :, lanes] = total.astype(BF16)
-            own = hidden[r, :, lanes].astype(F32)
-            moved = [later(own, first), own, earlier(own, last)]
-            for a in range(3):
-                for b in range(3):
-                    product = moved[b] * near[a]
-                    for i in range(7):
-                        sums[3 * a + b] = sums[3 * a + b] + product[8 * i : 8 * i + 8]
-        for t in range(9):
-            depth[t : t + 1, lanes] = jnp.sum(sums[t], axis=0, keepdims=True)
         return carry
 
     lax.fori_loop(begin, end, chunk, 0)
+
+
+def settle_kernel(*refs):
+    count = len(refs) // 2
+    copies = [
+        pltpu.make_async_copy(refs[n], refs[count + n], refs[2 * count].at[n]) for n in range(count)
+    ]
+    for cp in copies:
+        cp.start()
+    for cp in copies:
+        cp.wait()
 
 
 def tile(n, width=256):
@@ -444,7 +471,7 @@
 ):
     dp, sp, x, zh, core = place()
     pulls = {}
-    pairs = ((hidden_h, hidden), (cot_h, cot), (proj_h, proj_w), (block_h, block), (out_h, out_w), (qkv_h, qkv_w))
+    pairs = ((hidden_h, hidden), (proj_h, proj_w), (block_h, block), (cot_h, cot), (qkv_h, qkv_w), (out_h, out_w))
     for n, (src, dst) in enumerate(pairs):
         pulls[n] = pltpu.make_async_copy(src, dst, loads.at[n])
         pulls[n].start()
@@ -460,44 +487,72 @@
     edge.start()
     cots = Rows(own_c, win_c, cs, cr, dp, sp, True)
     norms = Rows(own_n, win_n, ns, nr, dp, sp, True)
+    taps[0:9] = depth_w[...].astype(F32)
+    scale = gain[...].reshape(1, C)
+
+    def norm(r):
+        here = tile(r, PLANE)
+        total = mid[here, :] + padded(block[r].astype(F32))
+        mid[here, :] = total
+        own_n[here, :] = (normal(total)[0] * scale).astype(BF16)
+        norms.start(r)
+
+    def norm_inner(r, carry):
+        norm(r)
+        return carry
+
+    def norm_outer(i, carry):
+        norm(lax.rem(i + 5, 7))
+        return carry
+
+    def proj_inner(n, carry):
+        mid[64:320, tile(n)] = jnp.dot(act[64:320, :], proj_w[:, tile(n)], preferred_element_type=F32)
+        return carry
+
+    def proj_outer(n, carry):
+        left = jnp.concatenate([act[0:64, :], act[320:448, :]], axis=0)
+        part = jnp.dot(left, proj_w[:, tile(n)], preferred_element_type=F32)
+        mid[0:64, tile(n)] = part[0:64]
+        mid[320:448, tile(n)] = part[64:192]
+        return carry
+
+    pulls[0].wait()
+    conv_forward(hidden, halo, taps, act, slope, 1, 5)
     pulls[1].wait()
+    lax.fori_loop(0, C // 256, proj_inner, 0)
+    pulls[2].wait()
+    lax.fori_loop(1, 5, norm_inner, 0)
+    edge.wait_recv()
+    conv_forward(hidden, halo, taps, act, slope, 5, 7)
+    conv_forward(hidden, halo, taps, act, slope, 0, 1)
+    lax.fori_loop(0, C // 256, proj_outer, 0)
+    lax.fori_loop(0, 3, norm_outer, 0)
+    pulls[3].wait()
     for r in range(ROWS):
         own_c[PLANE * r : PLANE * (r + 1)] = padded(cot[r].astype(F32)).astype(BF16)
         cots.start(r)
-    taps[0:9] = depth_w[...].astype(F32)
-    scale = gain[...].reshape(1, C)
-    pulls[0].wait()
-    edge.wait_recv()
-    for begin, end in ((0, 4), (4, 7)):
-        conv_forward(hidden, halo, taps, act, slope, begin, end)
-        if begin == 0:
-            pulls[2].wait()
-            pulls[3].wait()
-        span = slice(PLANE * begin, PLANE * end)
-
-        def proj(n, carry, span=span):
-            mid[span, tile(n)] = jnp.dot(act[span, :], proj_w[:, tile(n)], preferred_element_type=F32)
-            return carry
-
-        lax.fori_loop(0, C // 256, proj, 0)
-
-        def norm(r, carry):
-            here = tile(r, PLANE)
-            total = mid[here, :] + padded(block[r].astype(F32))
-            mid[here, :] = total
-            own_n[here, :] = (normal(total)[0] * scale).astype(BF16)
-            norms.start(r)
-            return carry
-
-        lax.fori_loop(begin, end, norm, 0)
 
     index = window_place(lax.broadcasted_iota(jnp.int32, (WIN, 1), 0))
     tokens = lax.broadcasted_iota(jnp.int32, (WIN, TOK), 1)
     perm = (index == tokens).astype(F32).astype(BF16)
     for r in range(ROWS):
+        norms.wait_recv(r)
+    norm_p[...] = jnp.dot(perm, win_n[...], preferred_element_type=F32).astype(BF16)
+    pulls[4].wait()
+
+    def qkv_step(n, carry):
+        qkv[:, tile(n)] = jnp.dot(
+            norm_p[...], qkv_w[:, tile(n)], preferred_element_type=F32
+        ).astype(BF16)
+        return carry
+
+    lax.fori_loop(0, 9, qkv_step, 0)
+    turned[...] = norm_p[...].T
+    attend(qkv, probs, att_p)
+    for r in range(ROWS):
         cots.wait_recv(r)
     cot_p[...] = jnp.dot(perm, win_c[...], preferred_element_type=F32).astype(BF16)
-    pulls[4].wait()
+    pulls[5].wait()
 
     def gatt_step(n, carry):
         gatt[:, tile(n)] = lax.dot_general(
@@ -506,20 +561,6 @@
         return carry
 
     lax.fori_loop(0, 3, gatt_step, 0)
-    for r in range(ROWS):
-        norms.wait_recv(r)
-    norm_p[...] = jnp.dot(perm, win_n[...], preferred_element_type=F32).astype(BF16)
-    pulls[5].wait()
-
-    def qkv_step(n, carry):
-        qkv[:, tile(n)] = jnp.dot(
-            norm_p[...], qkv_w[:, tile(n)], preferred_element_type=F32
-        ).astype(BF16)
-        return carry
-
-    lax.fori_loop(0, 9, qkv_step, 0)
-    turned[...] = norm_p[...].T
-    attend(qkv, probs, att_p)
 
     ring = lambda q, h: (q, pl.ds(2 * h, 2))
     ring_piece = lambda q, h, i: (q, 2 * h + i)
@@ -593,22 +634,9 @@
     att_w[...] = jnp.dot(back, att_p[...], preferred_element_type=F32).astype(BF16)
     for g in range(ROWS):
         atts.start(g)
-    for c in range(1, 4):
-        attend_back(qkv, gatt, probs, gqkv, (2 * c - 2, 2 * c - 1))
-        if c == 3:
-
-            def gn_step(n, carry):
-                gn_p[:, tile(n)] = lax.dot_general(
-                    gqkv[...], qkv_w[tile(n), :], NT, preferred_element_type=F32
-                ).astype(BF16)
-                return carry
-
-            lax.fori_loop(0, 3, gn_step, 0)
-            gn_w[...] = jnp.dot(back, gn_p[...], preferred_element_type=F32).astype(BF16)
-            for g in range(ROWS):
-                gns.start(g)
-
-        def grad_step(n, carry, c=c):
+
+    def qkv_grad(c):
+        def grad_step(n, carry):
             right = gqkv[:, pl.ds(pl.multiple_of(768 * n + 256 * (c - 1), 256), 256)]
             agrads[c, :, :, :, :, tile(n, 128)] = half_rows(
                 jnp.dot(turned[...], right, preferred_element_type=F32)
@@ -617,6 +645,24 @@
 
         lax.fori_loop(0, 3, grad_step, 0)
         advance(c)
+
+    attend_back(qkv, gatt, probs, gqkv, (0, 1))
+    qkv_grad(1)
+    attend_back(qkv, gatt, probs, gqkv, (2, 3))
+    attend_back(qkv, gatt, probs, gqkv, (4, 5))
+
+    def gn_step(n, carry):
+        gn_p[:, tile(n)] = lax.dot_general(
+            gqkv[...], qkv_w[tile(n), :], NT, preferred_element_type=F32
+        ).astype(BF16)
+        return carry
+
+    lax.fori_loop(0, 3, gn_step, 0)
+    gn_w[...] = jnp.dot(back, gn_p[...], preferred_element_type=F32).astype(BF16)
+    for g in range(ROWS):
+        gns.start(g)
+    qkv_grad(2)
+    qkv_grad(3)
     for r in range(ROWS):
         atts.wait_recv(r)
 
@@ -688,27 +734,21 @@
         lax.fori_loop(0, 3, proj_step, 0)
         ppair.start(xx)
 
-    advance(5)
-
-    def act_step(n, carry):
-        part = lax.dot_general(ig[...], proj_w[tile(n), :], NT, preferred_element_type=F32)
-        gc[:, tile(n)] = (part * slope[:, tile(n)]).astype(BF16)
-        return carry
-
-    lax.fori_loop(0, E // 256, act_step, 0)
-    edge2 = Halo(gc.at[0:PLANE], gc.at[TOK - PLANE : TOK], edges, es, er, dp, sp)
-    edge2.start()
     for m in XORS:
         ppair.add(flip(x, m), put_p0)
     px.start()
     qz.start()
-    advance(6)
-    edge2.wait_recv()
-    conv_backward(gc, edges, hidden, taps, hidden_o, depth, 0, 6)
-    px.forward()
-    qz.forward()
-    advance(7)
-    conv_backward(gc, edges, hidden, taps, hidden_o, depth, 6, 12)
+    advance(5)
+
+    def act_step(n, carry):
+        part = lax.dot_general(ig[...], proj_w[tile(n), :], NT, preferred_element_type=F32)
+        gc[:, tile(n)] = (part * slope[:, tile(n)]).astype(BF16)
+        return carry
+
+    lax.fori_loop(0, E // 256, act_step, 0)
+    edge2 = Halo(gc.at[0:PLANE], gc.at[TOK - PLANE : TOK], edges, es, er, dp, sp)
+    edge2.start()
+    depth_sums(gc, halo, hidden, depth)
 
     for n in range(12):
         small[n] = depth[0:8, 128 * n : 128 * (n + 1)]
@@ -727,10 +767,31 @@
     spread = Fan(lambda n: ssum, lambda n: sall.at[n], d1s, d1r, others)
     collect = Fan(lambda n: sfinal.at[mine], lambda n: sfinal.at[mine], d2s, d2r, plane16)
     scatter.start()
+    px.forward()
+    qz.forward()
+    advance(6)
+    edge2.wait_recv()
+    conv_backward(gc, edges, taps, hidden_o, 0, 6)
+    scatter.wait_recv()
+    total = small[mine]
+    for n in range(15):
+        total = total + srecv[n]
+    ssum[...] = total
+    spread.start()
     px.finish(put_ps1)
     pz.start()
     qz.finish(put_qs1)
     qx.start()
+    advance(7)
+    conv_backward(gc, edges, taps, hidden_o, 6, 12)
+    spread.wait_recv()
+    total = ssum[...]
+    for n in range(15):
+        total = total + sall[n]
+    sfinal[mine] = total
+    collect.start()
+    pz.forward()
+    qx.forward()
     advance(8)
     for hh in range(2):
         rows = slice(24 * hh, 24 * (hh + 1))
@@ -747,20 +808,6 @@
         atile[j] = value.astype(BF16)
     alast = Fan(lambda n: atile.at[lax.rem(sp + n + 1, 8)], lambda n: arecv.at[n], als, alr, sps)
     alast.start()
-    scatter.wait_recv()
-    total = small[mine]
-    for n in range(15):
-        total = total + srecv[n]
-    ssum[...] = total
-    spread.start()
-    pz.forward()
-    qx.forward()
-    spread.wait_recv()
-    total = ssum[...]
-    for n in range(15):
-        total = total + sall[n]
-    sfinal[mine] = total
-    collect.start()
     qx.finish(put_q2)
     pz.finish(put_p2)
     for j in range(8):
@@ -830,13 +877,14 @@
     counts += [4, 4, 6, 6, 6, 6, 6, 6, 6, 6, 7, 7]
     counts += [15] * 6
     scratch += [DMA((n,)) for n in counts]
-    block_o, input_o, hidden_o, depth_o, gain_o, proj_o, qkv_o, out_o = pl.pallas_call(
+    shapes = (
+        shape((ROWS, COLS, C)), shape((ROWS, COLS, C)), shape((ROWS, COLS, E)),
+        shape((9, E), F32), shape((C,), F32),
+        shape((48, 96), F32), shape((24, 288), F32), shape((24, 96), F32),
+    )
+    outs = pl.pallas_call(
         section_kernel,
-        out_shape=(
-            shape((ROWS, COLS, C)), shape((ROWS, COLS, C)), shape((ROWS, COLS, E)),
-            shape((9, E), F32), shape((C,), F32),
-            shape((48, 96), F32), shape((24, 288), F32), shape((24, 96), F32),
-        ),
+        out_shape=shapes,
         in_specs=[ANY] * 6 + [VM] * 2,
         out_specs=(VM,) * 8,
         scratch_shapes=scratch,
@@ -845,7 +893,15 @@
         ),
         name="section",
     )(block[0], hidden[0], cot[0], proj_w, qkv_w, out_w, depth_w, gain)
-    return (block_o[None], input_o[None], hidden_o[None], depth_o, gain_o, proj_o, qkv_o, out_o)
+    outs = pl.pallas_call(
+        settle_kernel,
+        out_shape=shapes,
+        in_specs=[ANY] * 8,
+        out_specs=(ANY,) * 8,
+        scratch_shapes=[DMA((8,))],
+        name="settle",
+    )(*outs)
+    return tuple(one[None] for one in outs[:3]) + tuple(outs[3:])
 
 
 def solution(mesh):

time: 137 us -> 204 us (1.49)
  Pallas kernels: 128 us -> 202 us
  local copies, waits for them, and re-layouts: 6.98 us -> 0 us
    pallas_call x1 -> x2, Pallas kernels: 128 us -> 202 us  [the longest x1 122 us: local(): pl.pallas_call(section_kernel, out_shape=shapes, in_specs=[ANY] * 6 + [VM...]
    unnamed x22 -> x0, local copies, waits for them, and re-layouts: 6.98 us -> none
where the time goes in v5:
time: 204 us; the launch traced here: 202 us
  Pallas kernels  202 us (99%)
    pallas_call x1, Pallas kernels, local(): pl.pallas_call(section_kernel, out_shape=shapes, in_specs=[ANY] * 6 + [VM...  122 us
    pallas_call x1, Pallas kernels, local(): pl.pallas_call(settle_kernel, out_shape=shapes, in_specs=[ANY] * 8, out_s...  79.4 us

profile of v5, /device:TPU:2, one launch (start us, length us, event | category | flops | bytes accessed | tf_op | source)
XLA Modules:
  0.0 202.3 jit_solution(15610943317246486980)
XLA Ops:
  0.6 122.1 %section.1 = (bf16[7,56,768]{2,1,0:T(8,128)(2,1)}, bf16[7,56,768]{2,1,0:T(8,128)(2,1)}, bf16[7,56,1536]{2,1,0:T(8,128)(2,1)}, f32[9,1536]{1,0:T(8,128)}, f32[768...) custom-call(bf16[7,56,768]{2,1,0:T(8,128)(2,1)} %bitcast.7, bf16[7,56,1536]{2,1,0:T(8,128)(2,1)} %bitcast.6, ...), custom_call_target="tpu_custom_call" | custom-call | tf_op jit(solution)/shard_map/section/pallas_call | solution.py:885
  122.7 79.4 %settle.1 = (bf16[7,56,768]{2,1,0:T(8,128)(2,1)}, bf16[7,56,768]{2,1,0:T(8,128)(2,1)}, bf16[7,56,1536]{2,1,0:T(8,128)(2,1)}, f32[9,1536]{1,0:T(8,128)}, f32[768]...) custom-call(bf16[7,56,768]{2,1,0:T(8,128)(2,1)} %get-tuple-element.24.refs_0_, ...), custom_call_target="tpu_custom_call" | custom-call | tf_op jit(solution)/shard_map/settle/pallas_call | solution.py:896

commit v6 on v5

--- a/solution.py
+++ b/solution.py
@@ -441,13 +441,8 @@
 
 def settle_kernel(*refs):
     count = len(refs) // 2
-    copies = [
-        pltpu.make_async_copy(refs[n], refs[count + n], refs[2 * count].at[n]) for n in range(count)
-    ]
-    for cp in copies:
-        cp.start()
-    for cp in copies:
-        cp.wait()
+    for n in range(count):
+        refs[count + n][...] = refs[n][...]
 
 
 def tile(n, width=256):
@@ -896,9 +891,8 @@
     outs = pl.pallas_call(
         settle_kernel,
         out_shape=shapes,
-        in_specs=[ANY] * 8,
-        out_specs=(ANY,) * 8,
-        scratch_shapes=[DMA((8,))],
+        in_specs=[VM] * 8,
+        out_specs=(VM,) * 8,
         name="settle",
     )(*outs)
     return tuple(one[None] for one in outs[:3]) + tuple(outs[3:])

time: 204 us -> 127 us (0.62)
  Pallas kernels: 202 us -> 125 us
    pallas_call x1, Pallas kernels: 79.4 us -> 3.21 us  [local(): pl.pallas_call(settle_kernel, out_shape=shapes, in_specs=[VM] * 8, out_sp...]
where the time goes in v6:
time: 127 us; the launch traced here: 126 us
  Pallas kernels  125 us (98%)
    pallas_call x1, Pallas kernels, local(): pl.pallas_call(section_kernel, out_shape=shapes, in_specs=[ANY] * 6 + [VM...  122 us
    pallas_call x1, Pallas kernels, local(): pl.pallas_call(settle_kernel, out_shape=shapes, in_specs=[VM] * 8, out_sp...  3.21 us

profile of v6, /device:TPU:2, one launch (start us, length us, event | category | flops | bytes accessed | tf_op | source)
XLA Modules:
  0.0 126.0 jit_solution(14154749925960103871)
XLA Ops:
  0.6 122.1 %section.1 = (bf16[7,56,768]{2,1,0:T(8,128)(2,1)}, bf16[7,56,768]{2,1,0:T(8,128)(2,1)}, bf16[7,56,1536]{2,1,0:T(8,128)(2,1)}, f32[9,1536]{1,0:T(8,128)}, f32[768...) custom-call(bf16[7,56,768]{2,1,0:T(8,128)(2,1)} %bitcast.7, bf16[7,56,1536]{2,1,0:T(8,128)(2,1)} %bitcast.6, ...), custom_call_target="tpu_custom_call" | custom-call | tf_op jit(solution)/shard_map/section/pallas_call | solution.py:880
  122.7 3.2 %settle.1 = (bf16[7,56,768]{2,1,0:T(8,128)(2,1)}, bf16[7,56,768]{2,1,0:T(8,128)(2,1)}, bf16[7,56,1536]{2,1,0:T(8,128)(2,1)}, f32[9,1536]{1,0:T(8,128)}, f32[768]...) custom-call(bf16[7,56,768]{2,1,0:T(8,128)(2,1)} %get-tuple-element.24.refs_0_, ...), custom_call_target="tpu_custom_call" | custom-call | tf_op jit(solution)/shard_map/settle/pallas_call | solution.py:891

commit v7 on v6

--- a/solution.py
+++ b/solution.py
@@ -241,8 +241,8 @@
     spread, gather = head_tools()
 
     def window(pair, carry):
-        for w in range(2):
-            rows = pl.ds(pl.multiple_of(pair * 128 + 64 * w, 64), 64)
+        for w in range(4):
+            rows = pl.ds(pl.multiple_of(pair * 256 + 64 * w, 64), 64)
             for g in groups:
                 query, key, value = (qkv[rows, heads(part, g)] for part in range(3))
                 query = spread(query)
@@ -261,7 +261,7 @@
                 gqkv[rows, heads(2, g)] = jnp.dot(low, grad, preferred_element_type=F32).astype(BF16)
         return carry
 
-    lax.fori_loop(0, 4, window, 0)
+    lax.fori_loop(0, 2, window, 0)
 
 
 def half_rows(value):

time: 127 us -> 127 us (level)
  no operation moved by 1% of the time
where the time goes in v7:
time: 127 us; the launch traced here: 125 us
  Pallas kernels  124 us (98%)
    pallas_call x1, Pallas kernels, local(): pl.pallas_call(section_kernel, out_shape=shapes, in_specs=[ANY] * 6 + [VM...  121 us
    pallas_call x1, Pallas kernels, local(): pl.pallas_call(settle_kernel, out_shape=shapes, in_specs=[VM] * 8, out_sp...  3.21 us

profile of v7, /device:TPU:2, one launch (start us, length us, event | category | flops | bytes accessed | tf_op | source)
XLA Modules:
  0.0 124.7 jit_solution(16468687563808845729)
XLA Ops:
  0.6 120.8 %section.1 = (bf16[7,56,768]{2,1,0:T(8,128)(2,1)}, bf16[7,56,768]{2,1,0:T(8,128)(2,1)}, bf16[7,56,1536]{2,1,0:T(8,128)(2,1)}, f32[9,1536]{1,0:T(8,128)}, f32[768...) custom-call(bf16[7,56,768]{2,1,0:T(8,128)(2,1)} %bitcast.7, bf16[7,56,1536]{2,1,0:T(8,128)(2,1)} %bitcast.6, ...), custom_call_target="tpu_custom_call" | custom-call | tf_op jit(solution)/shard_map/section/pallas_call | solution.py:880
  121.5 3.2 %settle.1 = (bf16[7,56,768]{2,1,0:T(8,128)(2,1)}, bf16[7,56,768]{2,1,0:T(8,128)(2,1)}, bf16[7,56,1536]{2,1,0:T(8,128)(2,1)}, f32[9,1536]{1,0:T(8,128)}, f32[768]...) custom-call(bf16[7,56,768]{2,1,0:T(8,128)(2,1)} %get-tuple-element.24.refs_0_, ...), custom_call_target="tpu_custom_call" | custom-call | tf_op jit(solution)/shard_map/settle/pallas_call | solution.py:891
